TPU v7x, 32 devices: a whole 2x2x4 slice. The times are simulated.
32 devices in a mesh: replica: 8 (over y, x, core), group: 4 (over z).
Axes of the slice: x: 2, y: 2, z: 4, core: 2. Of those that a mesh axis runs over, the one named last changes fastest.
Arguments:
- images: bfloat16 [160, 197, 512], P(('replica', 'group')), may hold values from -6 to 6
- attn_norm_gain: bfloat16 [512], P('group'), may hold values from 0.5 to 1.5
- attn_norm_bias: bfloat16 [512], P('group'), may hold values from -1.1953125 to 1.1953125
- qkv_weight: bfloat16 [512, 1536], P('group'), may hold values from -0.25 to 0.25
- query_value_bias: bfloat16 [1024], P('group'), may hold values from -1.1953125 to 1.1953125
- proj_weight: bfloat16 [512, 512], P('group'), may hold values from -2 to 2
- proj_bias: bfloat16 [512], P('group'), may hold values from -1.1953125 to 1.1953125
- moe_norm_gain: bfloat16 [512], P('group'), may hold values from 0.5 to 1.5
- moe_norm_bias: bfloat16 [512], P('group'), may hold values from -1.1953125 to 1.1953125
- router_weight: bfloat16 [512, 4], P('group'), may hold values from -0.1875 to 0.1875
- expert_inner: bfloat16 [4, 512, 2048], P('group'), may hold values from -0.25 to 0.25
- expert_inner_bias: bfloat16 [4, 2048], P('group'), may hold values from -0.8984375 to 0.8984375
- expert_outer: bfloat16 [4, 2048, 512], P('group'), may hold values from -0.5 to 0.5
- expert_outer_bias: bfloat16 [4, 512], P('group'), may hold values from -1.796875 to 1.796875
- live_count: int32 [32], P(('replica', 'group')), may hold values from 3 to 5, as said below
- routes: int32 [160, 197, 2], P(('replica', 'group')), may hold values from 0 to 3, as said below
- slot_ids: int32 [160, 197, 2], P(('replica', 'group')), may hold values from -1 to 639, as said below
- cotangent: bfloat16 [160, 197, 512], P(('replica', 'group')), may hold values from -6 to 6
Outputs:
- block_out: bfloat16 [160, 197, 512], P(('replica', 'group'))
- input_grad: float32 [160, 197, 512], P(('replica', 'group'))
- grad_attn_norm_gain: float32 [512], P('group')
- grad_attn_norm_bias: float32 [512], P('group')
- grad_qkv_weight: float32 [512, 1536], P('group')
- grad_query_value_bias: float32 [1024], P('group')
- grad_proj_weight: float32 [512, 512], P('group')
- grad_proj_bias: float32 [512], P('group')
- grad_moe_norm_gain: float32 [512], P('group')
- grad_moe_norm_bias: float32 [512], P('group')
- grad_router_weight: float32 [512, 4], P('group')
- grad_expert_inner: float32 [4, 512, 2048], P('group')
- grad_expert_inner_bias: float32 [4, 2048], P('group')
- grad_expert_outer: float32 [4, 2048, 512], P('group')
- grad_expert_outer_bias: float32 [4, 512], P('group')
Inputs may be any that keep to these rules, and one draw needn't show every extreme that they name: Each device holds 5 image slots; the first live_count of them are images, the others padding whose outputs are zero; some device is full in every draw. `routes`: every token names two different experts. `slot_ids`: on each device and for each expert, the routes of live tokens to that expert take the slots 0, 1, 2, ... in order of token and then of choice; -1 marks a route of a padding image or one after the expert's 640 slots on that device are full.
All inputs are finite; a program needn't handle non-finite values.
Results may differ from a plain program's by a relative error of at most 0.017.
Values may be sent and summed in bfloat16 or wider, within the bound.
No kernel may reach another device: no remote copies, remote signals or barrier semaphores. Data moves between devices by JAX's collectives and lax.ppermute only.
A program may use at most 256 MiB of HBM per device.

v0:
```python
import math

import jax
import jax.numpy as jnp
from jax import lax
from jax.sharding import PartitionSpec as P

HEADS = 8
CAP = 640


NORM_EPS = 1e-06


def layer_norm(values, gain_vector, shift_vector):
    center = values - jnp.mean(values, axis=-1, keepdims=True)
    spread = jnp.mean(center * center, axis=-1, keepdims=True)
    return center * lax.rsqrt(spread + NORM_EPS) * gain_vector + shift_vector


def gelu_exact(values):
    return jax.nn.gelu(values, approximate=False)


def expert_forward(expert_input, inner, inner_shift, outer, outer_shift):
    hidden = jnp.einsum("ecd,edf->ecf", expert_input, inner, preferred_element_type=jnp.float32)
    hidden = hidden + inner_shift.astype(jnp.float32)[:, None, :]
    active = gelu_exact(hidden).astype(jnp.bfloat16)
    result = jnp.einsum("ecf,efd->ecd", active, outer, preferred_element_type=jnp.float32)
    return (result + outer_shift.astype(jnp.float32)[:, None, :], hidden)


def expert_backward(expert_input, hidden, grad_result, inner, outer):
    active, gelu_pull = jax.vjp(gelu_exact, hidden)
    active_low = active.astype(jnp.bfloat16)
    grad_outer = jnp.einsum(
        "ecf,ecd->efd", active_low, grad_result, preferred_element_type=jnp.float32
    )
    grad_outer_shift = jnp.sum(grad_result.astype(jnp.float32), axis=1)
    grad_active = jnp.einsum("ecd,efd->ecf", grad_result, outer, preferred_element_type=jnp.float32)
    grad_hidden = gelu_pull(grad_active)[0].astype(jnp.bfloat16)
    grad_inner_shift = jnp.sum(grad_hidden.astype(jnp.float32), axis=1)
    grad_inner = jnp.einsum(
        "ecd,ecf->edf", expert_input, grad_hidden, preferred_element_type=jnp.float32
    )
    grad_input = jnp.einsum("ecf,edf->ecd", grad_hidden, inner, preferred_element_type=jnp.float32)
    return (grad_input, grad_inner, grad_inner_shift, grad_outer, grad_outer_shift)


def group_sum(grad_tuple):
    return (
        lax.psum_scatter(
            grad_tuple[0].astype(jnp.bfloat16), "group", scatter_dimension=0, tiled=True
        ).astype(jnp.float32),
        lax.psum_scatter(
            grad_tuple[1].astype(jnp.bfloat16), "group", scatter_dimension=0, tiled=True
        ).astype(jnp.float32),
        lax.psum_scatter(
            grad_tuple[2].astype(jnp.bfloat16), "group", scatter_dimension=0, tiled=True
        ).astype(jnp.float32),
        lax.psum_scatter(
            grad_tuple[3].astype(jnp.bfloat16), "group", scatter_dimension=0, tiled=True
        ).astype(jnp.float32),
    )


def local(
    images,
    attn_norm_gain,
    attn_norm_bias,
    qkv_weight,
    query_value_bias,
    proj_weight,
    proj_bias,
    moe_norm_gain,
    moe_norm_bias,
    router_weight,
    expert_inner,
    expert_inner_bias,
    expert_outer,
    expert_outer_bias,
    live_count,
    routes,
    slot_ids,
    cotangent,
):
    image_count, length, model_width = images.shape
    row_count = image_count * length
    expert_count = router_weight.shape[1]
    slot_total = expert_count * CAP
    head_size = model_width // HEADS
    score_scale = 1.0 / math.sqrt(head_size)
    dense = (
        lax.all_gather(attn_norm_gain, "group", axis=0, tiled=True),
        lax.all_gather(attn_norm_bias, "group", axis=0, tiled=True),
        lax.all_gather(qkv_weight, "group", axis=0, tiled=True),
        lax.all_gather(query_value_bias, "group", axis=0, tiled=True),
        lax.all_gather(proj_weight, "group", axis=0, tiled=True),
        lax.all_gather(proj_bias, "group", axis=0, tiled=True),
        lax.all_gather(moe_norm_gain, "group", axis=0, tiled=True),
        lax.all_gather(moe_norm_bias, "group", axis=0, tiled=True),
        lax.all_gather(router_weight, "group", axis=0, tiled=True),
    )
    qkv_full = dense[2]
    proj_full = dense[4]
    router_full = dense[8]
    pair_shift = dense[3].astype(jnp.float32)
    token_rows = images.reshape(row_count, model_width).astype(jnp.float32)
    live_rows = (jnp.arange(row_count) // length < live_count[0]).astype(jnp.float32)[:, None]
    normed, norm1_pull = jax.vjp(
        layer_norm, token_rows, dense[0].astype(jnp.float32), dense[1].astype(jnp.float32)
    )
    normed_low = normed.astype(jnp.bfloat16)
    projected = jnp.dot(normed_low, qkv_full, preferred_element_type=jnp.float32)
    queries = (projected[:, :model_width] + pair_shift[:model_width]).astype(jnp.bfloat16)
    keys_all = projected[:, model_width : 2 * model_width].astype(jnp.bfloat16)
    values_all = (projected[:, 2 * model_width :] + pair_shift[model_width:]).astype(jnp.bfloat16)

    def by_head(matrix):
        return matrix.reshape(image_count, length, HEADS, head_size)

    query_heads = by_head(queries)
    key_heads = by_head(keys_all)
    value_heads = by_head(values_all)
    scores = (
        jnp.einsum("bqhc,bkhc->bhqk", query_heads, key_heads, preferred_element_type=jnp.float32)
        * score_scale
    )
    score_peak = jnp.max(scores, axis=-1, keepdims=True)
    score_exp = jnp.exp(scores - score_peak)
    score_total = jnp.sum(score_exp, axis=-1, keepdims=True)
    log_total = score_peak + jnp.log(score_total)
    attn_low = (score_exp / score_total).astype(jnp.bfloat16)
    attended = jnp.einsum(
        "bhqk,bkhc->bqhc", attn_low, value_heads, preferred_element_type=jnp.float32
    )
    attended = attended.reshape(row_count, model_width).astype(jnp.bfloat16)
    branch = jnp.dot(attended, proj_full, preferred_element_type=jnp.float32) + dense[5].astype(
        jnp.float32
    )
    residual = token_rows + branch
    normed2, norm2_pull = jax.vjp(
        layer_norm, residual, dense[6].astype(jnp.float32), dense[7].astype(jnp.float32)
    )
    normed2_low = normed2.astype(jnp.bfloat16)
    logits = jnp.dot(normed2_low, router_full, preferred_element_type=jnp.float32)
    router_probs = jax.nn.softmax(logits, axis=-1)
    route_flat = routes.reshape(row_count, 2)
    slot_flat = slot_ids.reshape(row_count, 2)
    routed = slot_flat >= 0
    chosen = (
        (route_flat[:, :, None] == jnp.arange(expert_count)[None, None, :]) & routed[:, :, None]
    ).astype(jnp.float32)
    gate_values = jnp.sum(router_probs[:, None, :] * chosen, axis=-1)
    target = jnp.where(routed, route_flat * CAP + slot_flat, slot_total).reshape(-1)
    fetch_index = jnp.minimum(target, slot_total - 1)
    buffer = (
        jnp.zeros((slot_total, model_width), jnp.bfloat16)
        .at[target]
        .set(jnp.repeat(normed2_low, 2, axis=0), mode="drop")
    )
    buffer = buffer.reshape(expert_count, CAP, model_width)
    pieces = (
        lax.all_gather(expert_inner, "group", axis=0, tiled=True),
        lax.all_gather(expert_inner_bias, "group", axis=0, tiled=True),
        lax.all_gather(expert_outer, "group", axis=0, tiled=True),
        lax.all_gather(expert_outer_bias, "group", axis=0, tiled=True),
    )
    piece_rows = buffer
    result, hidden = expert_forward(piece_rows, pieces[0], pieces[1], pieces[2], pieces[3])
    picked = jnp.take(result.reshape(slot_total, model_width), fetch_index, axis=0).reshape(
        row_count, 2, model_width
    )
    mixture = jnp.sum(gate_values[:, :, None] * picked, axis=1)
    block_out = ((residual + mixture) * live_rows).astype(jnp.bfloat16).reshape(images.shape)
    grad_out = cotangent.reshape(row_count, model_width).astype(jnp.float32) * live_rows
    slot_grads = (
        (gate_values[:, :, None] * grad_out[:, None, :])
        .reshape(row_count * 2, model_width)
        .astype(jnp.bfloat16)
    )
    grad_slots = (
        jnp.zeros((slot_total, model_width), jnp.bfloat16).at[target].set(slot_grads, mode="drop")
    )
    grad_slots = grad_slots.reshape(expert_count, CAP, model_width)
    grad_gates = jnp.sum(grad_out[:, None, :] * picked, axis=-1)
    grad_probs = jnp.sum(grad_gates[:, :, None] * chosen, axis=1)
    grad_logits = (
        router_probs * (grad_probs - jnp.sum(router_probs * grad_probs, axis=-1, keepdims=True))
    ).astype(jnp.bfloat16)
    pieces = (
        lax.all_gather(expert_inner, "group", axis=0, tiled=True),
        lax.all_gather(expert_outer, "group", axis=0, tiled=True),
    )
    piece_rows = buffer
    results = expert_backward(piece_rows, hidden, grad_slots, pieces[0], pieces[1])
    full_back = tuple((update for update in results))
    grad_buffer = full_back[0]
    expert_shards = group_sum((full_back[1], full_back[2], full_back[3], full_back[4]))
    returned = jnp.take(grad_buffer.reshape(slot_total, model_width), fetch_index, axis=0).reshape(
        row_count, 2, model_width
    )
    grad_normed2 = jnp.sum(returned * routed[:, :, None].astype(jnp.float32), axis=1)
    grad_normed2 = grad_normed2 + jnp.dot(
        grad_logits, router_full.T, preferred_element_type=jnp.float32
    )
    grad_router = jnp.dot(normed2_low.T, grad_logits, preferred_element_type=jnp.float32)
    grad_resid_part, grad_gain2, grad_shift2 = norm2_pull(grad_normed2)
    grad_residual = grad_out + grad_resid_part
    grad_branch = grad_residual.astype(jnp.bfloat16)
    grad_proj_shift = jnp.sum(grad_branch.astype(jnp.float32), axis=0)
    grad_proj = jnp.dot(attended.T, grad_branch, preferred_element_type=jnp.float32)
    grad_attended = jnp.dot(grad_branch, proj_full.T, preferred_element_type=jnp.float32).astype(
        jnp.bfloat16
    )
    grad_att_heads = by_head(grad_attended)
    again_scores = (
        jnp.einsum("bqhc,bkhc->bhqk", query_heads, key_heads, preferred_element_type=jnp.float32)
        * score_scale
    )
    again_probs = jnp.exp(again_scores - log_total)
    grad_weights = jnp.einsum(
        "bqhc,bkhc->bhqk", grad_att_heads, value_heads, preferred_element_type=jnp.float32
    )
    grad_values = jnp.einsum(
        "bhqk,bqhc->bkhc",
        again_probs.astype(jnp.bfloat16),
        grad_att_heads,
        preferred_element_type=jnp.float32,
    )
    grad_values = grad_values.reshape(row_count, model_width).astype(jnp.bfloat16)
    grad_scores = again_probs * (
        grad_weights - jnp.sum(grad_weights * again_probs, axis=-1, keepdims=True)
    )
    grad_scores = grad_scores.astype(jnp.bfloat16)
    grad_queries = (
        jnp.einsum("bhqk,bkhc->bqhc", grad_scores, key_heads, preferred_element_type=jnp.float32)
        * score_scale
    )
    grad_queries = grad_queries.reshape(row_count, model_width).astype(jnp.bfloat16)
    grad_keys = (
        jnp.einsum("bhqk,bqhc->bkhc", grad_scores, query_heads, preferred_element_type=jnp.float32)
        * score_scale
    )
    grad_keys = grad_keys.reshape(row_count, model_width).astype(jnp.bfloat16)
    grad_projected = jnp.concatenate([grad_queries, grad_keys, grad_values], axis=1)
    grad_pairs = jnp.concatenate(
        [
            jnp.sum(grad_queries.astype(jnp.float32), axis=0),
            jnp.sum(grad_values.astype(jnp.float32), axis=0),
        ]
    )
    grad_qkv = jnp.dot(normed_low.T, grad_projected, preferred_element_type=jnp.float32)
    grad_normed = jnp.dot(grad_projected, qkv_full.T, preferred_element_type=jnp.float32)
    grad_input_part, grad_gain1, grad_shift1 = norm1_pull(grad_normed)
    input_grad = (grad_residual + grad_input_part).reshape(images.shape)
    dense_shards = (
        lax.psum_scatter(
            grad_gain1.astype(jnp.bfloat16), "group", scatter_dimension=0, tiled=True
        ).astype(jnp.float32),
        lax.psum_scatter(
            grad_shift1.astype(jnp.bfloat16), "group", scatter_dimension=0, tiled=True
        ).astype(jnp.float32),
        lax.psum_scatter(
            grad_qkv.astype(jnp.bfloat16), "group", scatter_dimension=0, tiled=True
        ).astype(jnp.float32),
        lax.psum_scatter(
            grad_pairs.astype(jnp.bfloat16), "group", scatter_dimension=0, tiled=True
        ).astype(jnp.float32),
        lax.psum_scatter(
            grad_proj.astype(jnp.bfloat16), "group", scatter_dimension=0, tiled=True
        ).astype(jnp.float32),
        lax.psum_scatter(
            grad_proj_shift.astype(jnp.bfloat16), "group", scatter_dimension=0, tiled=True
        ).astype(jnp.float32),
        lax.psum_scatter(
            grad_gain2.astype(jnp.bfloat16), "group", scatter_dimension=0, tiled=True
        ).astype(jnp.float32),
        lax.psum_scatter(
            grad_shift2.astype(jnp.bfloat16), "group", scatter_dimension=0, tiled=True
        ).astype(jnp.float32),
        lax.psum_scatter(
            grad_router.astype(jnp.bfloat16), "group", scatter_dimension=0, tiled=True
        ).astype(jnp.float32),
    )
    every_grad = lax.psum(
        (
            dense_shards[0],
            dense_shards[1],
            dense_shards[2],
            dense_shards[3],
            dense_shards[4],
            dense_shards[5],
            dense_shards[6],
            dense_shards[7],
            dense_shards[8],
            expert_shards[0],
            expert_shards[1],
            expert_shards[2],
            expert_shards[3],
        ),
        "replica",
    )
    return (
        block_out,
        input_grad,
        every_grad[0],
        every_grad[1],
        every_grad[2],
        every_grad[3],
        every_grad[4],
        every_grad[5],
        every_grad[6],
        every_grad[7],
        every_grad[8],
        every_grad[9],
        every_grad[10],
        every_grad[11],
        every_grad[12],
    )


def solution(mesh):
    in_specs = (
        P(("replica", "group"), None, None),
        P("group"),
        P("group"),
        P("group", None),
        P("group"),
        P("group", None),
        P("group"),
        P("group"),
        P("group"),
        P("group", None),
        P("group", None, None),
        P("group", None),
        P("group", None, None),
        P("group", None),
        P(("replica", "group")),
        P(("replica", "group"), None, None),
        P(("replica", "group"), None, None),
        P(("replica", "group"), None, None),
    )
    out_specs = (
        P(("replica", "group"), None, None),
        P(("replica", "group"), None, None),
        P("group"),
        P("group"),
        P("group", None),
        P("group"),
        P("group", None),
        P("group"),
        P("group"),
        P("group"),
        P("group", None),
        P("group", None, None),
        P("group", None),
        P("group", None, None),
        P("group", None),
    )
    return jax.shard_map(local, mesh=mesh, in_specs=in_specs, out_specs=out_specs, check_vma=False)
```

profile of v0, /device:TPU:0, one launch (start us, length us, event | category | flops | bytes accessed | tf_op | source)
XLA Modules:
  0.0 1100.8 jit_solution(393625634451455167)
XLA Ops:
  11.5 12.7 %all-gather = bf16[4,1,128]{2,1,0:T(2,128)(2,1)S(1)} all-gather(bf16[1,1,128]{2,1,0:T(2,128)(2,1)S(1)} %bitcast.117), channel_id=1, replica_groups=mesh['replica'=8,'group'=4] {'group'}, dimensions={0}, use_global_device_ids=true | all-gather | bytes 1280 | tf_op jit(solution)/shard_map/all_gather | solution.py:94
  41.5 19.0 %all_gather.45 = bf16[512,512]{1,0:T(8,128)(2,1)} all-gather(bf16[128,512]{1,0:T(8,128)(2,1)S(1)} %copy-done.35), channel_id=1, replica_groups=mesh['replica'=8,'group'=4] {'group'}, dimensions={0}, use_global_device_ids=true | all-gather | bytes 655360 | tf_op jit(solution)/shard_map/all_gather | solution.py:98
  60.5 9.8 all-gather.3
  78.0 11.9 %all-gather.5 = bf16[4,1,128]{2,1,0:T(2,128)(2,1)S(1)} all-gather(bf16[1,1,128]{2,1,0:T(2,128)(2,1)S(1)} %bitcast.121), channel_id=1, replica_groups=mesh['replica'=8,'group'=4] {'group'}, dimensions={0}, use_global_device_ids=true | all-gather | bytes 1280 | tf_op jit(solution)/shard_map/all_gather | solution.py:101
  89.9 9.8 all_gather.49
  100.3 18.2 %all-gather.6 = bf16[4,1,2048]{2,1,0:T(2,128)(2,1)S(1)} all-gather(bf16[1,1,2048]{2,1,0:T(2,128)(2,1)S(1)} %bitcast.112), channel_id=1, replica_groups=mesh['replica'=8,'group'=4] {'group'}, dimensions={0}, use_global_device_ids=true | all-gather | bytes 20480 | tf_op jit(solution)/shard_map/all_gather | solution.py:165
  118.4 13.9 %all-gather.7 = bf16[4,1,512]{2,1,0:T(2,128)(2,1)S(1)} all-gather(bf16[1,1,512]{2,1,0:T(2,128)(2,1)S(1)} %bitcast.116), channel_id=1, replica_groups=mesh['replica'=8,'group'=4] {'group'}, dimensions={0}, use_global_device_ids=true | all-gather | bytes 5120 | tf_op jit(solution)/shard_map/all_gather | solution.py:167
  199.0 12.7 %scatter_custom_fusion = bf16[2560,512]{1,0:T(8,128)(2,1)} fusion(s32[1970]{0:T(1024)S(1)} %bitcast.113, bf16[1970,512]{1,0:T(8,128)(2,1)} %reshape.345, bf16[]{:T(256)} %constant.18.clone.1), kind=kCustom, calls=%fused_computation.79 | custom fusion | bytes 2621952 | tf_op jit(solution)/shard_map/scatter | solution.py:160
  211.7 21.8 %fusion.9 = (u8[640,2048]{1,0:T(8,128)(4,1)S(1)}, u8[640,2048]{1,0:T(8,128)(4,1)}, f32[4,640,2048]{2,1,0:T(8,128)}) fusion(f32[4,2048]{1,0:T(4,128)S(1)} %bitcast.96, bf16[4,640,512]{2,1,0:T(8,128)(2,1)} %bitcast.94, bf16[4,512,2048]{2,1,0:T(8,128)(2,1)} %all-gather.14.cloned.1.call-done), kind=kOutput, calls=%fused_computation.36 | convolution fusion | flops 5439488000 | bytes 34635776 | tf_op jit(solution)/shard_map/ecd,edf->ecf/dot_general | solution.py:26
  233.5 51.4 %multiply_convert_fusion = (bf16[4,640,2048]{2,1,0:T(8,128)(2,1)}, f32[4,640,2048]{2,1,0:T(8,128)}) fusion(f32[4,640,2048]{2,1,0:T(8,128)} %get-tuple-element.70, f32[4,2048]{1,0:T(4,128)S(1)} %bitcast.97, u8[640,2048]{1,0:T(8,128)(4,1)} %get-tuple-element.17, u8[640,2048]{1,0:T(8,128)(4,1)S(1)} %get-tuple-element.16), kind=kLoop, calls=%fused_computation.12 | loop fusion | flops 372244480 | bytes 55083008 | tf_op jit(solution)/shard_map/convert_element_type | solution.py:28
  284.9 71.5 %all-gather.16.cloned.1.call-done = bf16[4,2048,512]{2,1,0:T(8,128)(2,1)} async-done(((bf16[1,2048,512]{2,1,0:T(8,128)(2,1)}), bf16[4,2048,512]{2,1,0:T(8,128)(2,1)}) %all-gather.16.cloned.1.call-update) | async-done | bytes 8388624 | tf_op jit(solution)/shard_map/all_gather | solution.py:166
  356.5 12.2 %broadcast_add_fusion = f32[4,640,512]{2,1,0:T(8,128)} fusion(f32[4,512]{1,0:T(4,128)S(1)} %bitcast.115, bf16[4,640,2048]{2,1,0:T(8,128)(2,1)} %get-tuple-element.59, bf16[4,2048,512]{2,1,0:T(8,128)(2,1)} %all-gather.16.cloned.1.call-done), kind=kOutput, calls=%fused_computation.50 | convolution fusion | flops 5370019840 | bytes 24125440 | tf_op jit(solution)/shard_map/ecf,efd->ecd/dot_general | solution.py:29
  368.7 11.9 %gather_fusion = f32[1970,512]{1,0:T(8,128)} fusion(f32[2560,512]{1,0:T(8,128)} %bitcast.88, s32[2048]{0:T(1024)S(1)} %pad_clamp_fusion), kind=kCustom, calls=%fused_computation.clone | custom fusion | bytes 8077000 | tf_op jit(solution)/shard_map/jit(_take)/gather | solution.py:171
  391.9 14.2 %scatter_custom_fusion.1 = bf16[2560,512]{1,0:T(8,128)(2,1)} fusion(s32[1970]{0:T(1024)} %bitcast.114, f32[1970,512]{1,0:T(8,128)} %mul.283, f32[1970]{0:T(1024)} %mul.280, bf16[]{:T(256)} %constant.18.clone.1), kind=kCustom, calls=%fused_computation.68 | custom fusion | flops 2017280 | bytes 6676992 | tf_op jit(solution)/shard_map/scatter | solution.py:183
  421.4 25.9 %fusion.41 = (bf16[4,2048]{1,0:T(4,128)(2,1)}, bf16[4,640,2048]{2,1,0:T(8,128)(2,1)}) fusion(f32[4,640,2048]{2,1,0:T(8,128)} %get-tuple-element.60, f32[4,640,2048]{2,1,0:T(8,128)} %get-tuple-element.70, f32[4,2048]{1,0:T(4,128)S(1)} %bitcast.98, bf16[4,640,512]{2,1,0:T(8,128)(2,1)S(1)} %bitcast.91, bf16[4,2048,512]{2,1,0:T(8,128)(2,1)} %all-gather.16.cloned.1.call-done), kind=kOutput, calls=%fused_computation.138 | convolution fusion | flops 5452587008 | bytes 63488000 | tf_op jit(solution)/shard_map/ecd,efd->ecf/dot_general | solution.py:40
  447.3 12.4 %fusion.52 = f32[4,640,512]{2,1,0:T(8,128)} fusion(bf16[4,640,2048]{2,1,0:T(8,128)(2,1)} %get-tuple-element.48, bf16[4,512,2048]{2,1,0:T(8,128)(2,1)} %all-gather.14.cloned.1.call-done), kind=kOutput, calls=%fused_computation.147 | convolution fusion | flops 5368709120 | bytes 24117248 | tf_op jit(solution)/shard_map/ecf,edf->ecd/dot_general | solution.py:46
  459.7 11.9 %gather_fusion.1 = f32[1970,512]{1,0:T(8,128)} fusion(f32[2560,512]{1,0:T(8,128)} %bitcast.87, s32[2048]{0:T(1024)S(1)} %copy-done.47), kind=kCustom, calls=%fused_computation.1.clone | custom fusion | bytes 8077000 | tf_op jit(solution)/shard_map/jit(_take)/gather | solution.py:200
  481.5 22.5 %multiply_reduce_fusion.3 = f32[985,512]{1,0:T(8,128)S(1)} fusion(f32[985,2,512]{2,1,0:T(2,128)} %reshape.320, f32[985,2]{1,0:T(8,128)S(1)} %copy-done.23), kind=kLoop, calls=%fused_computation.43 | loop fusion | flops 1512960 | bytes 6059720 | tf_op jit(solution)/shard_map/reduce_sum | solution.py:203
  570.0 12.6 %convolution_convert_fusion = bf16[4,2048,512]{2,1,0:T(8,128)(2,1)} fusion(bf16[4,640,2048]{2,1,0:T(8,128)(2,1)} %get-tuple-element.59, bf16[4,640,512]{2,1,0:T(8,128)(2,1)} %bitcast.89), kind=kOutput, calls=%fused_computation.32 | convolution fusion | flops 5372903424 | bytes 21495808 | tf_op jit(solution)/shard_map/ecf,ecd->efd/dot_general | solution.py:36
  582.7 13.3 %convolution_convert_fusion.1 = bf16[4,512,2048]{2,1,0:T(8,128)(2,1)} fusion(bf16[4,640,512]{2,1,0:T(8,128)(2,1)} %bitcast.95, bf16[4,640,2048]{2,1,0:T(8,128)(2,1)} %get-tuple-element.48), kind=kOutput, calls=%fused_computation.33 | convolution fusion | flops 5372903424 | bytes 21495808 | tf_op jit(solution)/shard_map/ecd,ecf->edf/dot_general | solution.py:43
  610.9 17.0 %all-reduce.9 = (bf16[512]{0:T(512)(128)(2,1)S(1)}, bf16[512]{0:T(512)(128)(2,1)S(1)}, bf16[1024]{0:T(1024)(128)(2,1)S(1)}, bf16[512]{0:T(512)(128)(2,1)S(1)}, b...) all-reduce(bf16[512]{0:T(512)(128)(2,1)S(1)} %get-tuple-element.20,, ...), channel_id=2, replica_groups=mesh['replica'=8,'group'=4] {'group'}, use_global_device_ids=true, to_apply=%region_22.24.clone | all-reduce | flops 13824 | bytes 55296
  630.4 125.5 %reduce-scatter.14.cloned.1.call-done = bf16[1,2048,512]{2,1,0:T(8,128)(2,1)} async-done(((bf16[4,2048,512]{2,1,0:T(8,128)(2,1)}), bf16[1,2048,512]{2,1,0:T(8,128)(2,1)}) %reduce-scatter.14.cloned.1.call-update) | async-done | bytes 2097168 | tf_op jit(solution)/shard_map/reduce_scatter | solution.py:58
  755.8 147.8 %reduce-scatter.12.cloned.1.call-done = bf16[1,512,2048]{2,1,0:T(8,128)(2,1)} async-done(((bf16[4,512,2048]{2,1,0:T(8,128)(2,1)}), bf16[1,512,2048]{2,1,0:T(8,128)(2,1)}) %reduce-scatter.12.cloned.1.call-update) | async-done | bytes 2097168 | tf_op jit(solution)/shard_map/reduce_scatter | solution.py:52
  903.6 189.9 %all-reduce.11 = (f32[128]{0:T(128)}, f32[128]{0:T(128)}, f32[128,1536]{1,0:T(8,128)}, f32[256]{0:T(256)}, f32[128,512]{1,0:T(8,128)}, /*index=5*/f32[128]{0:T(1...) all-reduce(f32[128]{0:T(128)S(1)} %dynamic-slice_convert_fusion.7, ...), channel_id=1, replica_groups=mesh['replica'=8,'group'=4] {'replica'}, use_global_device_ids=true, to_apply=%region_23.25 | all-reduce | flops 2363264 | bytes 14186496 | tf_op jit(solution)/shard_map/psum | solution.py:286
  (307 shorter events, 213.4 us)
Async XLA Ops:
  7.2 141.4 %all-gather.12.cloned.1.call-start = ((), (), s32[]{:S(2)}) async-start(), calls=%async_computation.5 | async-start | bytes 1966080 | tf_op jit(solution)/shard_map/all_gather | solution.py:96
  7.9 203.7 %all-gather.14.cloned.1.call-start = ((), (), s32[]{:S(2)}) async-start(), calls=%async_computation.6 | async-start | bytes 10485760 | tf_op jit(solution)/shard_map/all_gather | solution.py:164
  8.7 347.7 %all-gather.16.cloned.1.call-start = ((), (), s32[]{:S(2)}) async-start(), calls=%async_computation.7 | async-start | bytes 10485760 | tf_op jit(solution)/shard_map/all_gather | solution.py:166
  9.5 68.5 %copy-start.76 = (bf16[128]{0:T(256)(128)(2,1)S(1)}, bf16[128]{0:T(256)(128)(2,1)}, u32[]{:S(2)}) copy-start(bf16[128]{0:T(256)(128)(2,1)} %param.28) | copy-start | bytes 772
  9.5 80.4 %copy-start.71 = (bf16[128,4]{0,1:T(4,128)(2,1)S(1)}, bf16[128,4]{0,1:T(4,128)(2,1)}, u32[]{:S(2)}) copy-start(bf16[128,4]{0,1:T(4,128)(2,1)} %param.29) | copy-start | bytes 3076
  9.5 90.7 %copy-start.68 = (bf16[1,2048]{1,0:T(2,128)(2,1)S(1)}, bf16[1,2048]{1,0:T(2,128)(2,1)}, u32[]{:S(2)}) copy-start(bf16[1,2048]{1,0:T(2,128)(2,1)} %param.31) | copy-start | bytes 12292
  9.5 108.9 %copy-start.70 = (bf16[1,512]{1,0:T(2,128)(2,1)S(1)}, bf16[1,512]{1,0:T(2,128)(2,1)}, u32[]{:S(2)}) copy-start(bf16[1,512]{1,0:T(2,128)(2,1)} %param.33) | copy-start | bytes 3076
  9.5 620.0 %reduce-scatter.16.cloned.1.call-start = ((), (), s32[]{:S(2)}) async-start(), calls=%async_computation.12 | async-start | bytes 163840
  10.1 138.5 %copy-start.2 = (f32[985,512]{1,0:T(8,128)}, f32[985,512]{1,0:T(8,128)S(1)}, u32[]{:S(2)}) copy-start(f32[985,512]{1,0:T(8,128)S(1)} %reshape.323) | copy-start | bytes 6051844
  10.8 137.8 %copy-start.29 = (f32[985]{0:T(1024)}, f32[985]{0:T(1024)S(1)}, u32[]{:S(2)}) copy-start(f32[985]{0:T(1024)S(1)} %div.65) | copy-start | bytes 11824
  11.3 369.3 %copy-start.65 = (pred[1970]{0:T(1024)(128)(4,1)}, pred[1970]{0:T(1024)(128)(4,1)S(1)}, u32[]{:S(2)}) copy-start(pred[1970]{0:T(1024)(128)(4,1)S(1)} %compare_and_fusion) | copy-start | bytes 5914
  11.4 126.1 %copy-start.58 = (f32[985]{0:T(1024)}, f32[985]{0:T(1024)S(1)}, u32[]{:S(2)}) copy-start(f32[985]{0:T(1024)S(1)} %add.190) | copy-start | bytes 11824
  11.5 137.2 %copy-start.31 = (f32[985]{0:T(1024)}, f32[985]{0:T(1024)S(1)}, u32[]{:S(2)}) copy-start(f32[985]{0:T(1024)S(1)} %rsqrt.20) | copy-start | bytes 11824
  24.1 124.5 %copy-start.42 = (f32[4,1,128]{2,1,0:T(1,128)}, f32[4,1,128]{2,1,0:T(1,128)S(1)}, u32[]{:S(2)}) copy-start(f32[4,1,128]{2,1,0:T(1,128)S(1)} %convert_element_type.294) | copy-start | bytes 6148
  31.8 116.8 %copy-start.52 = (f32[4,1,128]{2,1,0:T(1,128)}, f32[4,1,128]{2,1,0:T(1,128)S(1)}, u32[]{:S(2)}) copy-start(f32[4,1,128]{2,1,0:T(1,128)S(1)} %convert_element_type.295) | copy-start | bytes 6148
  78.0 111.2 %copy-start.63 = (f32[4,1,128]{2,1,0:T(1,128)}, f32[4,1,128]{2,1,0:T(1,128)S(1)}, u32[]{:S(2)}) copy-start(f32[4,1,128]{2,1,0:T(1,128)S(1)} %convert_element_type.298) | copy-start | bytes 6148
  99.7 89.9 %copy-start.61 = (bf16[512,4]{0,1:T(4,128)(2,1)}, bf16[512,4]{0,1:T(4,128)(2,1)S(1)}, u32[]{:S(2)}) copy-start(bf16[512,4]{0,1:T(4,128)(2,1)S(1)} %all_gather.49) | copy-start | bytes 12292
  100.2 98.7 %copy-start.69 = (s32[1970,1]{0,1:T(1,128)}, s32[1970,1]{0,1:T(1,128)S(1)}, u32[]{:S(2)}) copy-start(s32[1970,1]{0,1:T(1,128)S(1)} %compare_select_fusion) | copy-start | bytes 23644
  118.4 115.1 %copy-start.33 = (f32[4,1,2048]{2,0,1:T(4,128)}, f32[4,1,2048]{2,0,1:T(4,128)S(1)}, u32[]{:S(2)}) copy-start(f32[4,1,2048]{2,0,1:T(4,128)S(1)} %copy.138) | copy-start | bytes 98308
  132.3 236.3 %copy-start.46 = (s32[2048]{0:T(1024)}, s32[2048]{0:T(1024)S(1)}, u32[]{:S(2)}) copy-start(s32[2048]{0:T(1024)S(1)} %pad_clamp_fusion) | copy-start | bytes 24580
  533.2 97.1 %reduce-scatter.10.cloned.1.call-start = ((), (), s32[]{:S(2)}) async-start(), calls=%async_computation.9 | async-start | bytes 655360 | tf_op jit(solution)/shard_map/reduce_scatter | solution.py:270
  536.4 94.0 %reduce-scatter.8.cloned.1.call-start = ((), (), s32[]{:S(2)}) async-start(), calls=%async_computation.8 | async-start | bytes 1966080 | tf_op jit(solution)/shard_map/reduce_scatter | solution.py:264
  570.0 185.9 %reduce-scatter.14.cloned.1.call-start = ((), (), s32[]{:S(2)}) async-start(), calls=%async_computation.11 | async-start | bytes 10485760 | tf_op jit(solution)/shard_map/reduce_scatter | solution.py:58
  582.7 320.9 %reduce-scatter.12.cloned.1.call-start = ((), (), s32[]{:S(2)}) async-start(), calls=%async_computation.10 | async-start | bytes 10485760 | tf_op jit(solution)/shard_map/reduce_scatter | solution.py:52
  (65 other events, 621.0 us)
Sparse Core Ops, SparseCore 0:
  9.6 46.5 all-gather.11
  57.8 149.1 all-gather.13
  208.6 147.8 all-gather.15
  533.4 17.3 reduce-scatter.15
  553.6 19.8 reduce-scatter.9
  575.8 33.5 reduce-scatter.7
  611.8 143.9 reduce-scatter.13
  758.3 145.2 reduce-scatter.11
where the time goes:
time: 1110 us; the launch traced here: 1100 us
  waiting for transfers between devices  347 us (31%)
  blocking collectives  327 us (29%)
  local copies, waits for them, and re-layouts  143 us (13%)
  matrix products  138 us (12%)
  other arithmetic  128 us (12%)
  between operations  17.7 us (2%)
    psum x1, blocking collectives, local(): lax.psum((dense_shards[0], dense_shards[1], dense_shards[2], dense_shards...  190 us
    reduce_scatter x1, waiting for transfers between devices, group_sum(): lax.psum_scatter(grad_tuple[0].astype(jnp.bfloat16), 'group', scatter_dim...  148 us
    reduce_scatter x1, waiting for transfers between devices, group_sum(): lax.psum_scatter(grad_tuple[2].astype(jnp.bfloat16), 'group', scatter_dim...  125 us
    all_gather x1, waiting for transfers between devices, local(): lax.all_gather(expert_outer, 'group', axis=0, tiled=True)  71.5 us
    convert_element_type x1, other arithmetic, expert_forward(): active = gelu_exact(hidden).astype(jnp.bfloat16)  51.4 us
    reshape x8, local copies, waits for them, and re-layouts, by_head(): return matrix.reshape(image_count, length, HEADS, head_size)  26.6 us
    dot_general x1, matrix products, expert_backward(): jnp.einsum('ecd,efd->ecf', grad_result, outer, preferred_element_type=jnp...  25.9 us
    reduce_sum x1, other arithmetic, local(): jnp.sum(returned * routed[:, :, None].astype(jnp.float32), axis=1)  22.5 us
  transfers between devices with their start and end apart: 8, of which 3 were waited for; matrix products, arithmetic and copies ran while one was open for 21% of the time, Pallas kernels for 0%

commit v1 on v0

v1 whole, which is shorter than its diff:
```python
import functools
import math

import jax
import jax.numpy as jnp
from jax import lax
from jax.experimental import pallas as pl
from jax.experimental.pallas import tpu as pltpu
from jax.sharding import PartitionSpec as P

HEADS = 8
CAP = 640
NORM_EPS = 1e-06
F32 = jnp.float32
BF16 = jnp.bfloat16
PAD = 256
PIECES = 8
SPLIT_A = (2, 4, 1)
SPLIT_B = (4, 2, 1)
SMALL = 128
MIB = 1 << 20


def offset_of(position, order):
    total = 0
    for k, bit in enumerate(order):
        total = total + ((position >> k) & 1) * bit
    return total


def dot_nn(a, b):
    return lax.dot_general(a, b, (((1,), (0,)), ((), ())), preferred_element_type=F32)


def dot_nt(a, b):
    return lax.dot_general(a, b, (((1,), (1,)), ((), ())), preferred_element_type=F32)


def dot_tn(a, b):
    return lax.dot_general(a, b, (((0,), (0,)), ((), ())), preferred_element_type=F32)


def norm_parts(values):
    center = values - jnp.mean(values, axis=-1, keepdims=True)
    spread = jnp.mean(center * center, axis=-1, keepdims=True)
    rstd = lax.rsqrt(spread + NORM_EPS)
    return center * rstd, rstd


def gelu_parts(v):
    size = jnp.abs(v)
    density = jnp.exp(v * v * (-0.5)) * 0.3989422804014327
    t = 1.0 / (1.0 + 0.2316418882 * size)
    series = t * (
        0.319381530 + t * (-0.356563782 + t * (1.781477937 + t * (-1.821255978 + t * 1.330274429)))
    )
    tail = density * series
    phi = jnp.where(v < 0, tail, 1.0 - tail)
    return v * phi, phi + v * density


def forward_kernel(
    place, images, cot, a_lo, a_hi, b_lo, b_hi,
    qkv_out, att_out, res_out, tok_out, gates_out, full_out, small_out,
):
    model = images.shape[2]
    length = images.shape[1]
    depth = a_lo.shape[2]
    parts = a_lo.shape[1]
    split = a_lo.shape[3]

    @pl.when(pl.program_id(0) == 0)
    def _():
        z, r = place[0], place[1]
        for pos in range(PIECES):
            for d in range(parts):
                owner = lax.rem(z + parts - d, parts) * PIECES
                for lo, hi, order, start in ((a_lo, a_hi, SPLIT_A, 0), (b_lo, b_hi, SPLIT_B, split)):
                    block = (lo if pos < PIECES // 2 else hi)[pos % (PIECES // 2), d]
                    row = pl.multiple_of((owner + jnp.bitwise_xor(r, offset_of(pos, order))) * depth, depth)
                    full_out[pl.ds(row, depth), start : start + block.shape[1]] = block
        small_out[...] = full_out[:, 4 * model :].astype(F32).T

    def vector(row):
        return small_out[row : row + 1, :]

    x = images[0].astype(F32)
    xhat, _ = norm_parts(x)
    normed = (xhat * vector(4) + vector(5)).astype(BF16)
    projected = dot_nn(normed, full_out[:, : 3 * model])
    bias_parts = []
    for part in range(parts):
        lanes = slice(part * 128, part * 128 + 128)
        bias_parts += [small_out[9:10, lanes], small_out[10:11, lanes]]
    pair = jnp.concatenate(bias_parts, axis=1)
    q = (projected[:, :model] + pair[:, :model]).astype(BF16)
    k = projected[:, model : 2 * model].astype(BF16)
    v = (projected[:, 2 * model :] + pair[:, model:]).astype(BF16)
    qkv_out[0, :, :model] = q
    qkv_out[0, :, model : 2 * model] = k
    qkv_out[0, :, 2 * model :] = v
    head = model // HEADS
    first = lax.broadcasted_iota(jnp.int32, (1, 2 * head), 1) < head
    scale = 1.0 / math.sqrt(head)
    attended = []
    for two in range(HEADS // 2):
        lanes = slice(two * 2 * head, (two + 1) * 2 * head)
        q2, k2, v2 = q[:, lanes], k[:, lanes], v[:, lanes]
        total = None
        for mask in (first, jnp.logical_not(first)):
            scores = dot_nt(jnp.where(mask, q2, jnp.zeros_like(q2)), k2) * scale
            e = jnp.exp(scores - jnp.max(scores, axis=-1, keepdims=True))
            probs = (e * (1.0 / jnp.sum(e, axis=-1, keepdims=True))).astype(BF16)
            part = dot_nn(probs, jnp.where(mask, v2, jnp.zeros_like(v2)))
            total = part if total is None else total + part
        attended.append(total.astype(BF16))
    attended = jnp.concatenate(attended, axis=1)
    att_out[0] = attended
    residual = x + (dot_nn(attended, full_out[:, 3 * model : 4 * model]) + vector(6))
    res_out[0] = residual
    xhat2, _ = norm_parts(residual)
    normed2 = (xhat2 * vector(7) + vector(8)).astype(BF16)
    tail = length // 64 * 64
    tok_out[tail:, :] = jnp.zeros((PAD - tail, 2 * model), BF16)
    tok_out[:length, :model] = normed2
    tok_out[:length, model:] = cot[0]
    logits = dot_nt(small_out[0:8, :].astype(BF16), tok_out[:, :model])
    experts = lax.broadcasted_iota(jnp.int32, logits.shape, 0) < parts
    logits = jnp.where(experts, logits, -jnp.inf)
    e = jnp.exp(logits - jnp.max(logits, axis=0, keepdims=True))
    gates_out[0] = e / jnp.sum(e, axis=0, keepdims=True)


def forward_call(place, images, cot, a_lo, a_hi, b_lo, b_hi):
    count, length, model = images.shape
    whole = lambda a: pl.BlockSpec(a.shape, lambda i, *_: (0,) * a.ndim)
    image = lambda *dims: pl.BlockSpec((1,) + dims, lambda i, *_: (i, 0, 0))
    outs = (
        jax.ShapeDtypeStruct((count, length, 3 * model), BF16),
        jax.ShapeDtypeStruct((count, length, model), BF16),
        jax.ShapeDtypeStruct((count, length, model), F32),
        jax.ShapeDtypeStruct((count * PAD, 2 * model), BF16),
        jax.ShapeDtypeStruct((count, 8, PAD), F32),
        jax.ShapeDtypeStruct((model, 4 * model + SMALL), BF16),
        jax.ShapeDtypeStruct((SMALL, model), F32),
    )
    return pl.pallas_call(
        forward_kernel,
        out_shape=outs,
        grid_spec=pltpu.PrefetchScalarGridSpec(
            num_scalar_prefetch=1,
            grid=(count,),
            in_specs=[image(length, model), image(length, model)] + [whole(a) for a in (a_lo, a_hi, b_lo, b_hi)],
            out_specs=[
                image(length, 3 * model), image(length, model), image(length, model),
                pl.BlockSpec((PAD, 2 * model), lambda i, *_: (i, 0)),
                image(8, PAD), whole(outs[5]), whole(outs[6]),
            ],
        ),
        compiler_params=pltpu.CompilerParams(vmem_limit_bytes=40 * MIB),
        cost_estimate=pl.CostEstimate(flops=14 * 10**9, bytes_accessed=12 * MIB, transcendentals=0),
        name="attention_forward",
    )(place, images, cot, a_lo, a_hi, b_lo, b_hi)


def expert_kernel(
    place, tok, slots, gates, small, ia_lo, ia_hi, ib_lo, ib_hi,
    a_keep, a_send, b_keep, b_send, rows_out, back_out, bias_out,
    onehot, buffer, grad_slots, rows, back, *, turn,
):
    i = pl.program_id(0)
    count = slots.shape[0]
    model = tok.shape[1] // 2
    half = PIECES // 2
    piece = place[4 + 4 * PIECES + i]

    @pl.when(i == 0)
    def _():
        e = place[2]
        where = lax.broadcasted_iota(jnp.int32, (CAP, PAD), 0)
        gate = jnp.zeros((CAP, 128), F32)
        for b in range(count):
            mask = where == slots[b, turn : turn + 1, :]
            onehot[:, b * PAD : (b + 1) * PAD] = mask.astype(F32).astype(BF16)
            weighted = jnp.where(mask, gates[b, pl.ds(e, 1), :], 0.0)
            gate = gate + weighted[:, :128] + weighted[:, 128:]
        gate = jnp.sum(gate, axis=1, keepdims=True)
        buffer[...] = dot_nn(onehot[...], tok[:, :model]).astype(BF16)
        grads = (dot_nn(onehot[...], tok[:, model:]) * gate).astype(BF16)
        grad_slots[...] = grads
        sums = jnp.sum(grads.astype(F32), axis=0, keepdims=True)
        for c in range(4):
            bias_out[16 + c : 17 + c, :] = sums[:, c * 128 : (c + 1) * 128]
        bias_out[20:32, :] = jnp.zeros((12, 128), F32)
        outer_bias = jnp.concatenate([small[28 + c : 29 + c, :] for c in range(4)], axis=1)
        rows[...] = jnp.broadcast_to(outer_bias, rows.shape)
        back[...] = jnp.zeros_like(back)

    early = i < half
    wa = jnp.where(early, ia_lo[...], ia_hi[...])
    wb = jnp.where(early, ib_lo[...], ib_hi[...])
    buf = buffer[...]
    gs = grad_slots[...]
    bias = jnp.concatenate([small[pl.ds(12 + 2 * piece, 1), :], small[pl.ds(13 + 2 * piece, 1), :]], axis=1)
    hidden = dot_nt(buf, wa) + bias
    active, slope = gelu_parts(hidden)
    active = active.astype(BF16)
    rows[...] += dot_nn(active, wb)
    grad_hidden = dot_nt(gs, wb) * slope
    grad_low = grad_hidden.astype(BF16)
    sums = jnp.sum(grad_low.astype(F32), axis=0, keepdims=True)
    bias_out[pl.ds(2 * piece, 1), :] = sums[:, :128]
    bias_out[pl.ds(2 * piece + 1, 1), :] = sums[:, 128:]
    grad_a = dot_tn(grad_low, buf).astype(BF16)
    grad_b = dot_tn(active, gs).astype(BF16)
    back[...] += dot_nn(grad_low, wa)

    @pl.when(early)
    def _():
        a_keep[...] = grad_a
        b_keep[...] = grad_b

    @pl.when(jnp.logical_not(early))
    def _():
        a_send[...] = grad_a
        b_send[...] = grad_b

    @pl.when(i == PIECES - 1)
    def _():
        rows_out[...] = rows[...].astype(BF16)
        back_out[...] = back[...].astype(BF16)


def expert_call(turn, place, tok, slots, gates, small, weights):
    model = tok.shape[1] // 2
    count = slots.shape[0]
    depth = PIECES * 256
    half = depth // 2
    whole = lambda a: pl.BlockSpec(a.shape, lambda i, *_: (0,) * a.ndim)
    table = lambda k: pl.BlockSpec((256, model), lambda i, s: (s[4 + k * PIECES + i], 0))
    out_half = lambda f: pl.BlockSpec((256, model), lambda i, s: (f(i), 0))
    swap = lambda i: ((i & 1) << 1) | ((i >> 1) & 1)
    outs = tuple(jax.ShapeDtypeStruct((half, model), BF16) for _ in range(4)) + (
        jax.ShapeDtypeStruct((CAP, model), BF16),
        jax.ShapeDtypeStruct((CAP, model), BF16),
        jax.ShapeDtypeStruct((32, 128), F32),
    )
    keep_a = lambda i: jnp.minimum(i, 3)
    send_a = lambda i: jnp.maximum(i - 4, 0)
    keep_b = lambda i: jnp.where(i < 4, swap(i), 3)
    send_b = lambda i: jnp.where(i < 4, 0, swap(i - 4))
    return pl.pallas_call(
        functools.partial(expert_kernel, turn=turn),
        out_shape=outs,
        grid_spec=pltpu.PrefetchScalarGridSpec(
            num_scalar_prefetch=1,
            grid=(PIECES,),
            in_specs=[
                whole(tok), whole(slots), whole(gates),
                pl.BlockSpec((SMALL, 128), lambda i, s: (0, s[2])),
                table(0), table(1), table(2), table(3),
            ],
            out_specs=[
                out_half(keep_a), out_half(send_a), out_half(keep_b), out_half(send_b),
                whole(outs[4]), whole(outs[5]), whole(outs[6]),
            ],
            scratch_shapes=[
                pltpu.VMEM((CAP, count * PAD), BF16),
                pltpu.VMEM((CAP, model), BF16),
                pltpu.VMEM((CAP, model), BF16),
                pltpu.VMEM((CAP, model), F32),
                pltpu.VMEM((CAP, model), F32),
            ],
        ),
        compiler_params=pltpu.CompilerParams(vmem_limit_bytes=40 * MIB),
        cost_estimate=pl.CostEstimate(flops=14 * 10**9, bytes_accessed=14 * MIB, transcendentals=0),
        name="expert",
    )(place, tok, slots, gates, small, *weights)


def backward_kernel(place, *refs, turns):
    images, cot, qkv, att, res, tok, slots, full, small = refs[:9]
    rows = refs[9 : 9 + turns]
    back = refs[9 + turns : 9 + 2 * turns]
    biases = refs[9 + 2 * turns : 9 + 3 * turns]
    block_out, input_grad, a_keep, a_send, b_keep, b_send = refs[9 + 3 * turns : 15 + 3 * turns]
    acc_qkv, acc_proj, acc_router, acc_small = refs[15 + 3 * turns :]
    b = pl.program_id(0)
    model = images.shape[2]
    length = images.shape[1]
    parts = turns

    @pl.when(b == 0)
    def _():
        acc_qkv[...] = jnp.zeros_like(acc_qkv)
        acc_proj[...] = jnp.zeros_like(acc_proj)
        acc_router[...] = jnp.zeros_like(acc_router)
        acc_small[...] = jnp.zeros_like(acc_small)

    def vector(row):
        return small[row : row + 1, :]

    def add_row(row, values):
        acc_small[row : row + 1, :] += jnp.sum(values, axis=0, keepdims=True)

    live = (b < place[3]).astype(F32)
    x = images[0].astype(F32)
    xhat1, rstd1 = norm_parts(x)
    residual = res[0]
    xhat2, rstd2 = norm_parts(residual)
    normed2 = tok[:length, :model]
    grad_out = cot[0].astype(F32) * live

    logits = dot_nn(normed2, full[:, 4 * model :])
    lane = lax.broadcasted_iota(jnp.int32, logits.shape, 1)
    logits = jnp.where(lane < parts, logits, -jnp.inf)
    e = jnp.exp(logits - jnp.max(logits, axis=-1, keepdims=True))
    probs = e / jnp.sum(e, axis=-1, keepdims=True)

    seat = lax.broadcasted_iota(jnp.int32, (length, CAP), 1)
    mixture = jnp.zeros((length, model), F32)
    grad_n2 = jnp.zeros((length, model), F32)
    grad_probs = jnp.zeros_like(probs)
    for j in range(turns):
        expert = lax.rem(place[0] + parts - j, parts)
        mask = (slots[0][:, j : j + 1] == seat).astype(F32).astype(BF16)
        picked = dot_nn(mask, rows[j][...])
        gate = jnp.sum(jnp.where(lane == expert, probs, 0.0), axis=-1, keepdims=True)
        mixture = mixture + gate * picked
        grad_gate = jnp.sum(grad_out * picked, axis=-1, keepdims=True)
        grad_probs = jnp.where(lane == expert, grad_gate, grad_probs)
        grad_n2 = grad_n2 + dot_nn(mask, back[j][...])
    block_out[0] = ((residual + mixture) * live).astype(BF16)
    grad_logits = probs * (grad_probs - jnp.sum(probs * grad_probs, axis=-1, keepdims=True))
    grad_logits = grad_logits.astype(BF16)
    grad_n2 = grad_n2 + dot_nt(grad_logits, full[:, 4 * model :])
    acc_router[...] += dot_tn(normed2, grad_logits)

    add_row(7, grad_n2 * xhat2)
    add_row(8, grad_n2)
    inner = grad_n2 * vector(7)
    grad_res = grad_out + rstd2 * (
        inner
        - jnp.mean(inner, axis=-1, keepdims=True)
        - xhat2 * jnp.mean(inner * xhat2, axis=-1, keepdims=True)
    )
    branch = grad_res.astype(BF16)
    add_row(6, branch.astype(F32))
    attended = att[0]
    acc_proj[...] += dot_tn(attended, branch)
    grad_att = dot_nt(branch, full[:, 3 * model : 4 * model]).astype(BF16)

    head = model // HEADS
    first = lax.broadcasted_iota(jnp.int32, (1, 2 * head), 1) < head
    scale = 1.0 / math.sqrt(head)
    grads = [[], [], []]
    for two in range(HEADS // 2):
        lanes = slice(two * 2 * head, (two + 1) * 2 * head)
        q2 = qkv[0, :, two * 2 * head : (two + 1) * 2 * head]
        k2 = qkv[0, :, model + two * 2 * head : model + (two + 1) * 2 * head]
        v2 = qkv[0, :, 2 * model + two * 2 * head : 2 * model + (two + 1) * 2 * head]
        g2 = grad_att[:, lanes]
        totals = [None, None, None]
        for mask in (first, jnp.logical_not(first)):
            only = lambda t: jnp.where(mask, t, jnp.zeros_like(t))
            q1, g1 = only(q2), only(g2)
            scores = dot_nt(q1, k2) * scale
            e = jnp.exp(scores - jnp.max(scores, axis=-1, keepdims=True))
            weights = e * (1.0 / jnp.sum(e, axis=-1, keepdims=True))
            grad_weights = dot_nt(g1, v2)
            grad_scores = weights * (
                grad_weights - jnp.sum(grad_weights * weights, axis=-1, keepdims=True)
            )
            grad_scores = grad_scores.astype(BF16)
            new = (
                dot_nn(grad_scores, only(k2)),
                dot_tn(grad_scores, q1),
                dot_tn(weights.astype(BF16), g1),
            )
            totals = [n if t is None else t + n for t, n in zip(totals, new)]
        grads[0].append((totals[0] * scale).astype(BF16))
        grads[1].append((totals[1] * scale).astype(BF16))
        grads[2].append(totals[2].astype(BF16))
    grad_projected = jnp.concatenate(grads[0] + grads[1] + grads[2], axis=1)
    normed = (xhat1 * vector(4) + vector(5)).astype(BF16)
    acc_qkv[...] += dot_tn(normed, grad_projected)
    grad_normed = dot_nt(grad_projected, full[:, : 3 * model])
    for row, start in ((9, 0), (10, 2 * model)):
        sums = jnp.sum(grad_projected[:, start : start + model].astype(F32), axis=0, keepdims=True)
        acc_small[row + 23 : row + 24, :] += sums
    add_row(4, grad_normed * xhat1)
    add_row(5, grad_normed)
    inner = grad_normed * vector(4)
    input_grad[0] = grad_res + rstd1 * (
        inner
        - jnp.mean(inner, axis=-1, keepdims=True)
        - xhat1 * jnp.mean(inner * xhat1, axis=-1, keepdims=True)
    )

    @pl.when(b == pl.num_programs(0) - 1)
    def _():
        for part in range(parts):
            for k in range(2):
                start = (part * 2 + k) * 128
                source = 32 + start // model
                acc_small[9 + k : 10 + k, part * 128 : part * 128 + 128] = acc_small[
                    source : source + 1, start % model : start % model + 128
                ]
        acc_small[32:34, :] = jnp.zeros((2, model), F32)
        for j in range(turns):
            expert = lax.rem(place[0] + parts - j, parts)
            acc_small[12:32, pl.ds(pl.multiple_of(expert * 128, 128), 128)] = biases[j][0:20, :]
        acc_router[...] = acc_router[...] + acc_small[...].T
        depth = a_keep.shape[2]
        split = a_keep.shape[3]
        for pos in range(PIECES):
            for d in range(parts):
                owner = lax.rem(place[0] + parts - d, parts) * PIECES
                where = pos % (PIECES // 2)
                row = pl.multiple_of((owner + jnp.bitwise_xor(place[1], offset_of(pos, SPLIT_A))) * depth, depth)
                out = a_keep if pos < PIECES // 2 else a_send
                out[where, d] = acc_qkv[pl.ds(row, depth), :split].astype(BF16)
                row = pl.multiple_of((owner + jnp.bitwise_xor(place[1], offset_of(pos, SPLIT_B))) * depth, depth)
                out = b_keep if pos < PIECES // 2 else b_send
                rest = 3 * model - split
                out[where, d, :, :rest] = acc_qkv[pl.ds(row, depth), split:].astype(BF16)
                out[where, d, :, rest : rest + model] = acc_proj[pl.ds(row, depth), :].astype(BF16)
                out[where, d, :, rest + model :] = acc_router[pl.ds(row, depth), :].astype(BF16)


def backward_call(place, images, cot, qkv, att, res, tok, slots, full, small, rows, back, biases):
    count, length, model = images.shape
    turns = len(rows)
    depth = model // (turns * PIECES)
    whole = lambda a: pl.BlockSpec(a.shape, lambda i, *_: (0,) * a.ndim)
    image = lambda *dims: pl.BlockSpec((1,) + dims, lambda i, *_: (i, 0, 0))
    outs = (
        jax.ShapeDtypeStruct((count, length, model), BF16),
        jax.ShapeDtypeStruct((count, length, model), F32),
    ) + tuple(
        jax.ShapeDtypeStruct((PIECES // 2, turns, depth, w), BF16)
        for w in (2 * model, 2 * model, 2 * model + SMALL, 2 * model + SMALL)
    )
    return pl.pallas_call(
        functools.partial(backward_kernel, turns=turns),
        out_shape=outs,
        grid_spec=pltpu.PrefetchScalarGridSpec(
            num_scalar_prefetch=1,
            grid=(count,),
            in_specs=[
                image(length, model), image(length, model), image(length, 3 * model),
                image(length, model), image(length, model),
                pl.BlockSpec((PAD, 2 * model), lambda i, *_: (i, 0)),
                image(length, slots.shape[2]), whole(full), whole(small),
            ] + [whole(a) for a in (*rows, *back, *biases)],
            out_specs=[image(length, model), image(length, model)] + [whole(o) for o in outs[2:]],
            scratch_shapes=[
                pltpu.VMEM((model, 3 * model), F32),
                pltpu.VMEM((model, model), F32),
                pltpu.VMEM((model, SMALL), F32),
                pltpu.VMEM((SMALL, model), F32),
            ],
        ),
        compiler_params=pltpu.CompilerParams(vmem_limit_bytes=48 * MIB),
        cost_estimate=pl.CostEstimate(flops=35 * 10**9, bytes_accessed=16 * MIB, transcendentals=0),
        name="attention_backward",
    )(place, images, cot, qkv, att, res, tok, slots, full, small, *rows, *back, *biases)


def finish_kernel(place, a_lo, a_hi, b_lo, b_hi, inner_out, outer_out):
    early = pl.program_id(0) < PIECES // 2
    inner_out[0] = jnp.where(early, a_lo[...], a_hi[...]).astype(F32).T
    outer_out[0] = jnp.where(early, b_lo[...], b_hi[...]).astype(F32)


def finish_call(place, a_lo, a_hi, b_lo, b_hi):
    model = a_lo.shape[1]
    depth = PIECES * 256
    swap = lambda i: ((i & 1) << 1) | ((i >> 1) & 1)
    block = lambda f: pl.BlockSpec((256, model), lambda i, s: (f(i), 0))
    piece = lambda i, s: s[4 + 4 * PIECES + i]
    return pl.pallas_call(
        finish_kernel,
        out_shape=(
            jax.ShapeDtypeStruct((1, model, depth), F32),
            jax.ShapeDtypeStruct((1, depth, model), F32),
        ),
        grid_spec=pltpu.PrefetchScalarGridSpec(
            num_scalar_prefetch=1,
            grid=(PIECES,),
            in_specs=[
                block(lambda i: jnp.minimum(i, 3)),
                block(lambda i: jnp.maximum(i - 4, 0)),
                block(lambda i: jnp.where(i < 4, swap(i), 3)),
                block(lambda i: jnp.where(i < 4, 0, swap(i - 4))),
            ],
            out_specs=[
                pl.BlockSpec((1, model, 256), lambda i, s: (0, 0, piece(i, s))),
                pl.BlockSpec((1, 256, model), lambda i, s: (0, piece(i, s), 0)),
            ],
        ),
        cost_estimate=pl.CostEstimate(flops=6 * 10**9, bytes_accessed=12 * MIB, transcendentals=0),
        name="finish_experts",
    )(place, a_lo, a_hi, b_lo, b_hi)


def finish_dense_kernel(place, a_lo, a_hi, b_lo, b_hi, qkv_out, proj_out, small_out, turned_out):
    model = proj_out.shape[1]
    depth = a_lo.shape[1]
    split = a_lo.shape[2]
    for pos in range(PIECES):
        where = pos % (PIECES // 2)
        row = pl.multiple_of(jnp.bitwise_xor(place[1], offset_of(pos, SPLIT_A)) * depth, depth)
        block = (a_lo if pos < PIECES // 2 else a_hi)[where].astype(F32)
        qkv_out[pl.ds(row, depth), :split] = block
        row = pl.multiple_of(jnp.bitwise_xor(place[1], offset_of(pos, SPLIT_B)) * depth, depth)
        block = (b_lo if pos < PIECES // 2 else b_hi)[where].astype(F32)
        rest = 3 * model - split
        qkv_out[pl.ds(row, depth), split:] = block[:, :rest]
        proj_out[pl.ds(row, depth), :] = block[:, rest : rest + model]
        small_out[pl.ds(row, depth), :] = block[:, rest + model :]
    turned_out[...] = small_out[...].T


def finish_dense_call(place, a_lo, a_hi, b_lo, b_hi, model):
    rows = a_lo.shape[1] * PIECES
    return pl.pallas_call(
        finish_dense_kernel,
        out_shape=(
            jax.ShapeDtypeStruct((rows, 3 * model), F32),
            jax.ShapeDtypeStruct((rows, model), F32),
            jax.ShapeDtypeStruct((rows, SMALL), F32),
            jax.ShapeDtypeStruct((SMALL, rows), F32),
        ),
        in_specs=[pl.BlockSpec(memory_space=pltpu.SMEM)] + [pl.BlockSpec(memory_space=pltpu.VMEM)] * 4,
        cost_estimate=pl.CostEstimate(flops=2 * 10**9, bytes_accessed=2 * MIB, transcendentals=0),
        name="finish_dense",
    )(place, a_lo, a_hi, b_lo, b_hi)


def local(
    images, attn_norm_gain, attn_norm_bias, qkv_weight, query_value_bias, proj_weight, proj_bias,
    moe_norm_gain, moe_norm_bias, router_weight, expert_inner, expert_inner_bias, expert_outer,
    expert_outer_bias, live_count, routes, slot_ids, cotangent, *, n_replica, n_group,
):
    count, length, model = images.shape
    shard = qkv_weight.shape[0]
    hidden = expert_inner.shape[2]
    depth = shard // PIECES
    block = hidden // PIECES
    z = lax.axis_index("group").astype(jnp.int32)
    replica = lax.axis_index("replica").astype(jnp.int32)
    r = replica & (PIECES - 1)

    def across(value, bit):
        return lax.ppermute(value, "replica", [(i, i ^ bit) for i in range(n_replica)])

    def along(value, shift):
        return lax.ppermute(value, "group", [(i, (i + shift) % n_group) for i in range(n_group)])

    def add(one, other):
        return (one.astype(F32) + other.astype(F32)).astype(BF16)

    def collect(value, order):
        for bit in order[:-1]:
            value = jnp.concatenate([value, across(value, bit)], axis=0)
        return value, across(value, order[-1])

    def reduce(keep, send, order):
        value = add(keep, across(send, order[-1]))
        for bit in order[-2::-1]:
            half = value.shape[0] // 2
            value = add(value[:half], across(value[half:], bit))
        bit = PIECES
        while bit < n_replica:
            value = add(value, across(value, bit))
            bit *= 2
        return value

    column = lambda vector: vector.reshape(-1, shard).T
    table = jnp.concatenate(
        [qkv_weight, proj_weight, router_weight]
        + [column(v) for v in (attn_norm_gain, attn_norm_bias, proj_bias, moe_norm_gain, moe_norm_bias, query_value_bias)]
        + [jnp.zeros((shard, 1), BF16), column(expert_inner_bias), column(expert_outer_bias)]
        + [jnp.zeros((shard, SMALL - 32), BF16)],
        axis=1,
    )
    mine = lax.dynamic_slice_in_dim(table, r * depth, depth, 0)
    split = 2 * model
    dense = []
    for part, order in ((mine[:, :split], SPLIT_A), (mine[:, split:], SPLIT_B)):
        stack = jnp.stack([part] + [along(part, d) for d in range(1, n_group)])
        dense += collect(stack[None], order)

    inner_turned = expert_inner[0].T
    outer_here = expert_outer[0]
    piece_a = lax.dynamic_slice_in_dim(inner_turned, r * block, block, 0)
    piece_b = lax.dynamic_slice_in_dim(outer_here, r * block, block, 0)
    weights = [(inner_turned, inner_turned, outer_here, outer_here)]
    for d in range(1, n_group):
        weights.append(collect(along(piece_a, d), SPLIT_A) + collect(along(piece_b, d), SPLIT_B))

    steps = jnp.arange(PIECES, dtype=jnp.int32)
    swap = ((steps & 1) << 1) | ((steps >> 1) & 1)
    pieces = r ^ offset_of(steps, SPLIT_A)
    halves = [
        jnp.minimum(steps, 3), jnp.maximum(steps - 4, 0),
        jnp.where(steps < 4, swap, 3), jnp.where(steps < 4, 0, swap),
    ]
    own = [
        pieces[jnp.minimum(steps, 3)], pieces[jnp.maximum(steps, 4)],
        pieces[jnp.minimum(steps, 3)], pieces[jnp.maximum(steps, 4)],
    ]

    def place_of(turn):
        expert = (z + n_group - turn) % n_group
        head = jnp.stack([z, r, expert, live_count[0].astype(jnp.int32)])
        return jnp.concatenate([head] + (own if turn == 0 else halves) + [pieces]).astype(jnp.int32)

    experts = (z + n_group - jnp.arange(n_group, dtype=jnp.int32)) % n_group
    chosen = routes[:, None] == experts[None, :, None, None]
    seats = jnp.max(jnp.where(chosen, slot_ids[:, None], -1), axis=-1)
    slots_lane = jnp.pad(seats, ((0, 0), (0, 8 - n_group), (0, PAD - length)), constant_values=-1)
    slots_row = jnp.pad(seats.transpose(0, 2, 1), ((0, 0), (0, 0), (0, 8 - n_group)), constant_values=-1)

    place = place_of(0)
    qkv, att, res, tok, gates, full, small = forward_call(place, images, cotangent, *dense)
    rows, back, biases, shards_a, shards_b = [], [], [], [], []
    for turn in range(n_group):
        out = expert_call(turn, place_of(turn), tok, slots_lane, gates, small, weights[turn])
        rows.append(out[4])
        back.append(out[5])
        biases.append(out[6])
        sum_a = reduce(out[0], out[1], SPLIT_A)
        sum_b = reduce(out[2], out[3], SPLIT_B)
        shards_a.append(along(sum_a, -turn) if turn else sum_a)
        shards_b.append(along(sum_b, -turn) if turn else sum_b)

    block_out, input_grad, *dense_grads = backward_call(
        place, images, cotangent, qkv, att, res, tok, slots_row, full, small, rows, back, biases
    )

    def total(values):
        return sum(v.astype(F32) for v in values).astype(BF16)

    halves_a = collect(total(shards_a), SPLIT_A)
    halves_b = collect(total(shards_b), SPLIT_B)
    dense_halves = []
    for keep, send, order in ((dense_grads[0], dense_grads[1], SPLIT_A), (dense_grads[2], dense_grads[3], SPLIT_B)):
        value = reduce(keep, send, order)[0]
        value = total([value[0]] + [along(value[d], -d) for d in range(1, n_group)])
        dense_halves += collect(value[None], order)
    grad_qkv, grad_proj, grad_small, turned = finish_dense_call(place, *dense_halves, model)
    grad_inner, grad_outer = finish_call(place, *halves_a, *halves_b)
    return (
        block_out,
        input_grad,
        turned[4],
        turned[5],
        grad_qkv,
        turned[9:11].reshape(-1),
        grad_proj,
        turned[6],
        turned[7],
        turned[8],
        grad_small[:, :n_group],
        grad_inner,
        turned[12:28].reshape(1, -1),
        grad_outer,
        turned[28:32].reshape(1, -1),
    )


def solution(mesh):
    both = ("replica", "group")
    in_specs = (
        P(both, None, None), P("group"), P("group"), P("group", None), P("group"), P("group", None),
        P("group"), P("group"), P("group"), P("group", None), P("group", None, None), P("group", None),
        P("group", None, None), P("group", None), P(both), P(both, None, None), P(both, None, None),
        P(both, None, None),
    )
    out_specs = (
        P(both, None, None), P(both, None, None), P("group"), P("group"), P("group", None), P("group"),
        P("group", None), P("group"), P("group"), P("group"), P("group", None), P("group", None, None),
        P("group", None), P("group", None, None), P("group", None),
    )
    body = functools.partial(local, n_replica=mesh.shape["replica"], n_group=mesh.shape["group"])
    return jax.shard_map(body, mesh=mesh, in_specs=in_specs, out_specs=out_specs, check_vma=False)
```

time: 1110 us -> 495 us (0.45)
  blocking collectives: 327 us -> 0 us
  waiting for transfers between devices: 347 us -> 153 us
  Pallas kernels: 0 us -> 158 us
  matrix products: 138 us -> 0 us
  other arithmetic: 128 us -> 15.3 us
  starting transfers between devices: 0.32 us -> 112 us
  local copies, waits for them, and re-layouts: 143 us -> 46.5 us
  between operations: 17.7 us -> 2.71 us
    reduce_scatter x4 -> x0, waiting for transfers between devices: 273 us -> none  [the longest x1 148 us: group_sum(): lax.psum_scatter(grad_tuple[0].astype(jnp.bfloat16), 'group', scatter_dim...]
    psum x1 -> x0, blocking collectives: 190 us -> none  [local(): lax.psum((dense_shards[0], dense_shards[1], dense_shards[2], dense_shards...]
    pallas_call x0 -> x8, Pallas kernels: none -> 158 us  [the longest x4 95.9 us: expert_call(): pl.pallas_call(functools.partial(expert_kernel, turn=turn), out_shape=out...]
    ppermute x0 -> x90, waiting for transfers between devices: none -> 153 us  [the longest x66 114 us: across(): lax.ppermute(value, 'replica', [(i, i ^ bit) for i in range(n_replica)])]
    dot_general x21 -> x0, matrix products: 138 us -> none  [the longest x1 25.9 us: expert_backward(): jnp.einsum('ecd,efd->ecf', grad_result, outer, preferred_element_type=jnp...]
    all_gather x10 -> x0, blocking collectives: 120 us -> none  [the longest x1 19 us: local(): lax.all_gather(proj_weight, 'group', axis=0, tiled=True)]
    ppermute x0 -> x90, starting transfers between devices: none -> 112 us  [the longest x24 60.9 us: along(): lax.ppermute(value, 'group', [(i, (i + shift) % n_group) for i in range(n...]
    all_gather x3 -> x0, waiting for transfers between devices: 71.5 us -> none  [the longest x1 71.5 us: local(): lax.all_gather(expert_outer, 'group', axis=0, tiled=True)]
  transfers between devices with their start and end apart: 8 -> 90, of which waited for: 3 -> 34; matrix products, arithmetic and copies ran while one was open for 21% -> 7% of each run, Pallas kernels for 0% -> 31%
where the time goes in v1:
time: 495 us; the launch traced here: 488 us
  Pallas kernels  158 us (32%)
  waiting for transfers between devices  153 us (31%)
  starting transfers between devices  112 us (23%)
  local copies, waits for them, and re-layouts  46.5 us (9%)
  other arithmetic  15.3 us (3%)
    ppermute x66, waiting for transfers between devices, across(): lax.ppermute(value, 'replica', [(i, i ^ bit) for i in range(n_replica)])  114 us
    pallas_call x4, Pallas kernels, expert_call(): pl.pallas_call(functools.partial(expert_kernel, turn=turn), out_shape=out...  95.9 us
    ppermute x24, starting transfers between devices, along(): lax.ppermute(value, 'group', [(i, (i + shift) % n_group) for i in range(n...  60.9 us
    ppermute x66, starting transfers between devices, across(): lax.ppermute(value, 'replica', [(i, i ^ bit) for i in range(n_replica)])  50.9 us
    ppermute x24, waiting for transfers between devices, along(): lax.ppermute(value, 'group', [(i, (i + shift) % n_group) for i in range(n...  39 us
    pallas_call x1, Pallas kernels, backward_call(): pl.pallas_call(functools.partial(backward_kernel, turns=turns), out_shape...  38.3 us
    unnamed x95, local copies, waits for them, and re-layouts  27.4 us
    pallas_call x1, Pallas kernels, forward_call(): pl.pallas_call(forward_kernel, out_shape=outs, grid_spec=pltpu.PrefetchSc...  13.6 us
  transfers between devices with their start and end apart: 90, of which 34 were waited for; matrix products, arithmetic and copies ran while one was open for 7% of the time, Pallas kernels for 31%

profile of v1, /device:TPU:0, one launch (start us, length us, event | category | flops | bytes accessed | tf_op | source)
XLA Modules:
  0.0 487.7 jit_solution(15340669204176031932)
XLA Ops:
  38.4 19.7 %collective-permute-start.28 = (bf16[256,512]{1,0:T(8,128)(2,1)}, bf16[256,512]{1,0:T(8,128)(2,1)S(1)}, u32[]{:S(2)}, u32[]{:S(2)}) collective-permute-start(bf16[256,512]{1,0:T(8,128)(2,1)} %bitcast.30), channel_id=1, source_target_pairs={{0,3},{1,0},{2,1},{3,2},{4,7},{5,4},{6,5},{7,6},{8,11},{9,8},{10,9... | collective-permute-start | bytes 786440 | tf_op jit(solution)/shard_map/ppermute | solution.py:559
  91.6 5.2 %collective-permute-done.14 = bf16[512,512]{1,0:T(8,128)(2,1)S(1)} collective-permute-done((bf16[512,512]{1,0:T(8,128)(2,1)S(1)}, bf16[512,512]{1,0:T(8,128)(2,1)S(1)}, u32[]{:S(2)}, u32[]{:S(2)}) %collective-permute-start.14) | collective-permute-done | bytes 524320 | tf_op jit(solution)/shard_map/ppermute | solution.py:556
  98.8 9.2 %collective-permute-done.22 = bf16[512,512]{1,0:T(8,128)(2,1)S(1)} collective-permute-done((bf16[512,512]{1,0:T(8,128)(2,1)S(1)}, bf16[512,512]{1,0:T(8,128)(2,1)S(1)}, u32[]{:S(2)}, u32[]{:S(2)}) %collective-permute-start.22) | collective-permute-done | bytes 524320 | tf_op jit(solution)/shard_map/ppermute | solution.py:556
  109.5 5.2 %collective-permute-done.30 = bf16[512,512]{1,0:T(8,128)(2,1)S(1)} collective-permute-done((bf16[512,512]{1,0:T(8,128)(2,1)S(1)}, bf16[512,512]{1,0:T(8,128)(2,1)S(1)}, u32[]{:S(2)}, u32[]{:S(2)}) %collective-permute-start.30) | collective-permute-done | bytes 524320 | tf_op jit(solution)/shard_map/ppermute | solution.py:556
  116.7 13.6 %attention_forward.1 = (bf16[5,197,1536]{2,1,0:T(8,128)(2,1)}, bf16[5,197,512]{2,1,0:T(8,128)(2,1)S(1)}, f32[5,197,512]{2,1,0:T(8,128)S(1)}, bf16[1280,1024]{1,0...) custom-call(s32[44]{0:T(128)S(1)} %concatenate.100.place, ...), custom_call_target="tpu_custom_call" | custom-call | flops 14000000000 | bytes 12582912 | tf_op jit(solution)/shard_map/attention_forward/pallas_call | solution.py:147
  138.2 23.5 %expert.4 = (bf16[1024,512]{1,0:T(8,128)(2,1)S(1)}, bf16[1024,512]{1,0:T(8,128)(2,1)}, bf16[1024,512]{1,0:T(8,128)(2,1)S(1)}, bf16[1024,512]{1,0:T(8,128)(2,1)},...) custom-call(s32[44]{0:T(128)S(1)} %concatenate.100.place, ...), custom_call_target="tpu_custom_call" | custom-call | flops 14000000000 | bytes 14680064 | tf_op jit(solution)/shard_map/expert/pallas_call | solution.py:252
  163.9 24.4 %expert.5 = (bf16[1024,512]{1,0:T(8,128)(2,1)S(1)}, bf16[1024,512]{1,0:T(8,128)(2,1)S(1)}, bf16[1024,512]{1,0:T(8,128)(2,1)S(1)}, bf16[1024,512]{1,0:T(8,128)(2,...) custom-call(s32[44]{0:T(128)S(1)} %concatenate.106.place, ...), custom_call_target="tpu_custom_call" | custom-call | flops 14000000000 | bytes 14680064 | tf_op jit(solution)/shard_map/expert/pallas_call | solution.py:252
  190.5 24.5 %expert.6 = (bf16[1024,512]{1,0:T(8,128)(2,1)S(1)}, bf16[1024,512]{1,0:T(8,128)(2,1)S(1)}, bf16[1024,512]{1,0:T(8,128)(2,1)S(1)}, bf16[1024,512]{1,0:T(8,128)(2,...) custom-call(s32[44]{0:T(128)S(1)} %concatenate.111.place, ...), custom_call_target="tpu_custom_call" | custom-call | flops 14000000000 | bytes 14680064 | tf_op jit(solution)/shard_map/expert/pallas_call | solution.py:252
  217.0 23.5 %expert.7 = (bf16[1024,512]{1,0:T(8,128)(2,1)S(1)}, bf16[1024,512]{1,0:T(8,128)(2,1)S(1)}, bf16[1024,512]{1,0:T(8,128)(2,1)S(1)}, bf16[1024,512]{1,0:T(8,128)(2,...) custom-call(s32[44]{0:T(128)S(1)} %concatenate.116.place, ...), custom_call_target="tpu_custom_call" | custom-call | flops 14000000000 | bytes 14680064 | tf_op jit(solution)/shard_map/expert/pallas_call | solution.py:252
  245.5 38.3 %attention_backward.1 = (bf16[5,197,512]{2,1,0:T(8,128)(2,1)}, f32[5,197,512]{2,1,0:T(8,128)}, bf16[4,4,16,1024]{3,2,1,0:T(8,128)(2,1)S(1)}, bf16[4,4,16,1024]{3...) custom-call(s32[44]{0:T(128)S(1)} %concatenate.100.place, ...), custom_call_target="tpu_custom_call" | custom-call | flops 35000000512 | bytes 16777216 | tf_op jit(solution)/shard_map/attention_backward/pallas_call | solution.py:444
  289.8 10.3 %collective-permute-done.73 = bf16[512,512]{1,0:T(8,128)(2,1)S(1)} collective-permute-done((bf16[512,512]{1,0:T(8,128)(2,1)S(1)}, bf16[512,512]{1,0:T(8,128)(2,1)S(1)}, u32[]{:S(2)}, u32[]{:S(2)}) %collective-permute-start.73) | collective-permute-done | bytes 524320 | tf_op jit(solution)/shard_map/ppermute | solution.py:556
  302.1 5.7 %collective-permute-done.37 = bf16[2,4,16,1024]{3,2,1,0:T(8,128)(2,1)S(1)} collective-permute-done((bf16[2,4,16,1024]{3,2,1,0:T(8,128)(2,1)S(1)}, bf16[2,4,16,1024]{3,2,1,0:T(8,128)(2,1)S(1)}, u32[]{:S(2)}, u32[]{:S(2)}) %collective-permute-start.37) | collective-permute-done | bytes 262176 | tf_op jit(solution)/shard_map/ppermute | solution.py:556
  310.2 4.1 collective-permute-done.38
  314.3 9.8 %collective-permute-start.39 = (bf16[16,1024]{1,0:T(8,128)(2,1)S(1)}, bf16[16,1024]{1,0:T(8,128)(2,1)S(1)}, u32[]{:S(2)}, u32[]{:S(2)}) collective-permute-start(bf16[16,1024]{1,0:T(8,128)(2,1)S(1)} %get-tuple-element.157), channel_id=1, source_target_pairs={{0,3},{1,0},{2,1},{3,2},{4,7},{5,4},{6,5},{7,6},{8,11},{9,8},{10,9... | collective-permute-start | bytes 98312 | tf_op jit(solution)/shard_map/ppermute | solution.py:559
  345.4 9.4 %collective-permute-done.76 = bf16[512,512]{1,0:T(8,128)(2,1)S(1)} collective-permute-done((bf16[512,512]{1,0:T(8,128)(2,1)S(1)}, bf16[512,512]{1,0:T(8,128)(2,1)S(1)}, u32[]{:S(2)}, u32[]{:S(2)}) %collective-permute-start.76) | collective-permute-done | bytes 524320 | tf_op jit(solution)/shard_map/ppermute | solution.py:556
  355.3 10.7 %collective-permute-done.80 = bf16[512,512]{1,0:T(8,128)(2,1)S(1)} collective-permute-done((bf16[512,512]{1,0:T(8,128)(2,1)S(1)}, bf16[512,512]{1,0:T(8,128)(2,1)S(1)}, u32[]{:S(2)}, u32[]{:S(2)}) %collective-permute-start.80) | collective-permute-done | bytes 524320 | tf_op jit(solution)/shard_map/ppermute | solution.py:556
  366.6 9.4 %collective-permute-done.84 = bf16[512,512]{1,0:T(8,128)(2,1)S(1)} collective-permute-done((bf16[512,512]{1,0:T(8,128)(2,1)S(1)}, bf16[512,512]{1,0:T(8,128)(2,1)S(1)}, u32[]{:S(2)}, u32[]{:S(2)}) %collective-permute-start.84) | collective-permute-done | bytes 524320 | tf_op jit(solution)/shard_map/ppermute | solution.py:556
  382.2 5.4 %collective-permute-done.77 = bf16[256,512]{1,0:T(8,128)(2,1)S(1)} collective-permute-done((bf16[256,512]{1,0:T(8,128)(2,1)S(1)}, bf16[256,512]{1,0:T(8,128)(2,1)S(1)}, u32[]{:S(2)}, u32[]{:S(2)}) %collective-permute-start.77) | collective-permute-done | bytes 262176 | tf_op jit(solution)/shard_map/ppermute | solution.py:556
  387.7 5.5 %collective-permute-done.81 = bf16[256,512]{1,0:T(8,128)(2,1)S(1)} collective-permute-done((bf16[256,512]{1,0:T(8,128)(2,1)S(1)}, bf16[256,512]{1,0:T(8,128)(2,1)S(1)}, u32[]{:S(2)}, u32[]{:S(2)}) %collective-permute-start.81) | collective-permute-done | bytes 262176 | tf_op jit(solution)/shard_map/ppermute | solution.py:556
  405.7 4.2 collective-permute-start.60
  409.9 17.6 %collective-permute-done.82 = bf16[256,512]{1,0:T(8,128)(2,1)S(1)} collective-permute-done((bf16[256,512]{1,0:T(8,128)(2,1)S(1)}, bf16[256,512]{1,0:T(8,128)(2,1)S(1)}, u32[]{:S(2)}, u32[]{:S(2)}) %collective-permute-start.82) | collective-permute-done | bytes 262176 | tf_op jit(solution)/shard_map/ppermute | solution.py:559
  429.9 11.9 %collective-permute-done.64 = bf16[256,512]{1,0:T(8,128)(2,1)S(1)} collective-permute-done((bf16[256,512]{1,0:T(8,128)(2,1)S(1)}, bf16[256,512]{1,0:T(8,128)(2,1)S(1)}, u32[]{:S(2)}, u32[]{:S(2)}) %collective-permute-start.64) | collective-permute-done | bytes 262176 | tf_op jit(solution)/shard_map/ppermute | solution.py:559
  454.0 8.4 %collective-permute-done.51 = bf16[1,16,1152]{2,1,0:T(8,128)(2,1)S(1)} collective-permute-done((bf16[1,16,1152]{2,1,0:T(8,128)(2,1)S(1)}, bf16[1,16,1152]{2,1,0:T(8,128)(2,1)S(1)}, u32[]{:S(2)}, u32[]{:S(2)}) %collective-permute-start.51) | collective-permute-done | bytes 36896 | tf_op jit(solution)/shard_map/ppermute | solution.py:556
  479.1 8.4 %finish_experts.1 = (f32[1,512,2048]{2,1,0:T(8,128)}, f32[1,2048,512]{2,1,0:T(8,128)}) custom-call(s32[44]{0:T(128)} %copy-done.8, bf16[1024,512]{1,0:T(8,128)(2,1)} %copy-done.33, bf16[1024,512]{1,0:T(8,128)(2,1)} %collective-permute-done.71.a_hi, bf16[1024,512]{1,0:T(8,128)(2,1)} %copy-done.32, bf16[1024,512]{1,0:T(8,128)(2,1)} %copy-done.38), custom_call_target="tpu_custom_call" | custom-call | flops 6000000000 | bytes 12582912 | tf_op jit(solution)/shard_map/finish_experts/pallas_call | solution.py:482
  (380 shorter events, 177.3 us)
Async XLA Ops:
  23.0 36.0 %collective-permute-start.12 = (bf16[256,512]{1,0:T(8,128)(2,1)}, bf16[256,512]{1,0:T(8,128)(2,1)S(1)}, u32[]{:S(2)}, u32[]{:S(2)}) collective-permute-start(bf16[256,512]{1,0:T(8,128)(2,1)} %bitcast.30), channel_id=1, source_target_pairs={{0,1},{1,2},{2,3},{3,0},{4,5},{5,6},{6,7},{7,4},{8,9},{9,10},{10,1... | collective-permute-start | bytes 786440 | tf_op jit(solution)/shard_map/ppermute | solution.py:559
  24.4 36.3 %collective-permute-start.20 = (bf16[256,512]{1,0:T(8,128)(2,1)}, bf16[256,512]{1,0:T(8,128)(2,1)S(1)}, u32[]{:S(2)}, u32[]{:S(2)}) collective-permute-start(bf16[256,512]{1,0:T(8,128)(2,1)} %bitcast.30), channel_id=1, source_target_pairs={{0,2},{1,3},{2,0},{3,1},{4,6},{5,7},{6,4},{7,5},{8,10},{9,11},{10,... | collective-permute-start | bytes 786440 | tf_op jit(solution)/shard_map/ppermute | solution.py:559
  26.5 32.7 %collective-permute-start.16 = (bf16[256,512]{1,0:T(8,128)(2,1)}, bf16[256,512]{1,0:T(8,128)(2,1)}, u32[]{:S(2)}, u32[]{:S(2)}) collective-permute-start(bf16[256,512]{1,0:T(8,128)(2,1)} %dynamic-slice_bitcast_fusion), channel_id=1, source_target_pairs={{0,1},{1,2},{2,3},{3,0},{4,5},{5,6},{6,7},{7,4},{8,9},{9,10},{10,1... | collective-permute-start | bytes 786440 | tf_op jit(solution)/shard_map/ppermute | solution.py:559
  37.0 25.3 %collective-permute-start.24 = (bf16[256,512]{1,0:T(8,128)(2,1)}, bf16[256,512]{1,0:T(8,128)(2,1)S(1)}, u32[]{:S(2)}, u32[]{:S(2)}) collective-permute-start(bf16[256,512]{1,0:T(8,128)(2,1)} %dynamic-slice_bitcast_fusion), channel_id=1, source_target_pairs={{0,2},{1,3},{2,0},{3,1},{4,6},{5,7},{6,4},{7,5},{8,10},{9,11},{10,... | collective-permute-start | bytes 786440 | tf_op jit(solution)/shard_map/ppermute | solution.py:559
  83.5 24.5 %collective-permute-start.22 = (bf16[512,512]{1,0:T(8,128)(2,1)S(1)}, bf16[512,512]{1,0:T(8,128)(2,1)S(1)}, u32[]{:S(2)}, u32[]{:S(2)}) collective-permute-start(bf16[512,512]{1,0:T(8,128)(2,1)S(1)} %pad_maximum_fusion.6), channel_id=1, source_target_pairs={{0,16},{4,20},{8,24},{12,28},{16,0},{20,4},{24,8},{28,12},{1,17},{... | collective-permute-start | bytes 1572872 | tf_op jit(solution)/shard_map/ppermute | solution.py:556
  89.2 25.5 %collective-permute-start.30 = (bf16[512,512]{1,0:T(8,128)(2,1)S(1)}, bf16[512,512]{1,0:T(8,128)(2,1)S(1)}, u32[]{:S(2)}, u32[]{:S(2)}) collective-permute-start(bf16[512,512]{1,0:T(8,128)(2,1)S(1)} %pad_maximum_fusion.8), channel_id=1, source_target_pairs={{0,16},{4,20},{8,24},{12,28},{16,0},{20,4},{24,8},{28,12},{1,17},{... | collective-permute-start | bytes 1572872 | tf_op jit(solution)/shard_map/ppermute | solution.py:556
  109.5 53.9 %collective-permute-start.15 = (bf16[1024,512]{1,0:T(8,128)(2,1)S(1)}, bf16[1024,512]{1,0:T(8,128)(2,1)}, u32[]{:S(2)}, u32[]{:S(2)}) collective-permute-start(bf16[1024,512]{1,0:T(8,128)(2,1)S(1)} %constant_dynamic-update-slice_fusion.ia_lo), channel_id=1, source_target_pairs={{0,4},{4,0},{8,12},{12,8},{16,20},{20,16},{24,28},{28,24},{1,5},{5... | collective-permute-start | bytes 3145736 | tf_op jit(solution)/shard_map/ppermute | solution.py:556
  114.7 48.9 %collective-permute-start.19 = (bf16[1024,512]{1,0:T(8,128)(2,1)S(1)}, bf16[1024,512]{1,0:T(8,128)(2,1)}, u32[]{:S(2)}, u32[]{:S(2)}) collective-permute-start(bf16[1024,512]{1,0:T(8,128)(2,1)S(1)} %constant_dynamic-update-slice_fusion.3.ib_lo), channel_id=1, source_target_pairs={{0,4},{4,0},{8,12},{12,8},{16,20},{20,16},{24,28},{28,24},{1,5},{5... | collective-permute-start | bytes 3145736 | tf_op jit(solution)/shard_map/ppermute | solution.py:556
  115.1 74.8 %collective-permute-start.23 = (bf16[1024,512]{1,0:T(8,128)(2,1)S(1)}, bf16[1024,512]{1,0:T(8,128)(2,1)}, u32[]{:S(2)}, u32[]{:S(2)}) collective-permute-start(bf16[1024,512]{1,0:T(8,128)(2,1)S(1)} %constant_dynamic-update-slice_fusion.6.ia_lo), channel_id=1, source_target_pairs={{0,4},{4,0},{8,12},{12,8},{16,20},{20,16},{24,28},{28,24},{1,5},{5... | collective-permute-start | bytes 3145736 | tf_op jit(solution)/shard_map/ppermute | solution.py:556
  116.2 74.0 %collective-permute-start.27 = (bf16[1024,512]{1,0:T(8,128)(2,1)S(1)}, bf16[1024,512]{1,0:T(8,128)(2,1)}, u32[]{:S(2)}, u32[]{:S(2)}) collective-permute-start(bf16[1024,512]{1,0:T(8,128)(2,1)S(1)} %constant_dynamic-update-slice_fusion.9.ib_lo), channel_id=1, source_target_pairs={{0,4},{4,0},{8,12},{12,8},{16,20},{20,16},{24,28},{28,24},{1,5},{5... | collective-permute-start | bytes 3145736 | tf_op jit(solution)/shard_map/ppermute | solution.py:556
  116.4 100.2 %collective-permute-start.31 = (bf16[1024,512]{1,0:T(8,128)(2,1)S(1)}, bf16[1024,512]{1,0:T(8,128)(2,1)}, u32[]{:S(2)}, u32[]{:S(2)}) collective-permute-start(bf16[1024,512]{1,0:T(8,128)(2,1)S(1)} %constant_dynamic-update-slice_fusion.12.ia_lo), channel_id=1, source_target_pairs={{0,4},{4,0},{8,12},{12,8},{16,20},{20,16},{24,28},{28,24},{1,5},{5... | collective-permute-start | bytes 3145736 | tf_op jit(solution)/shard_map/ppermute | solution.py:556
  163.4 53.6 %collective-permute-start.35 = (bf16[1024,512]{1,0:T(8,128)(2,1)}, bf16[1024,512]{1,0:T(8,128)(2,1)S(1)}, u32[]{:S(2)}, u32[]{:S(2)}) collective-permute-start(bf16[1024,512]{1,0:T(8,128)(2,1)} %constant_dynamic-update-slice_fusion.15.ib_lo), channel_id=1, source_target_pairs={{0,4},{4,0},{8,12},{12,8},{16,20},{20,16},{24,28},{28,24},{1,5},{5... | collective-permute-start | bytes 3145736 | tf_op jit(solution)/shard_map/ppermute | solution.py:556
  163.6 120.5 %collective-permute-start.72 = (bf16[1024,512]{1,0:T(8,128)(2,1)}, bf16[1024,512]{1,0:T(8,128)(2,1)}, u32[]{:S(2)}, u32[]{:S(2)}) collective-permute-start(bf16[1024,512]{1,0:T(8,128)(2,1)} %get-tuple-element.100), channel_id=1, source_target_pairs={{0,4},{4,0},{8,12},{12,8},{16,20},{20,16},{24,28},{28,24},{1,5},{5... | collective-permute-start | bytes 3145736 | tf_op jit(solution)/shard_map/ppermute | solution.py:556
  189.9 96.0 %collective-permute-start.54 = (bf16[1024,512]{1,0:T(8,128)(2,1)}, bf16[1024,512]{1,0:T(8,128)(2,1)}, u32[]{:S(2)}, u32[]{:S(2)}) collective-permute-start(bf16[1024,512]{1,0:T(8,128)(2,1)} %get-tuple-element.92), channel_id=1, source_target_pairs={{0,4},{4,0},{8,12},{12,8},{16,20},{20,16},{24,28},{28,24},{1,5},{5... | collective-permute-start | bytes 3145736 | tf_op jit(solution)/shard_map/ppermute | solution.py:556
  190.2 145.5 %collective-permute-start.75 = (bf16[1024,512]{1,0:T(8,128)(2,1)}, bf16[1024,512]{1,0:T(8,128)(2,1)S(1)}, u32[]{:S(2)}, u32[]{:S(2)}) collective-permute-start(bf16[1024,512]{1,0:T(8,128)(2,1)} %get-tuple-element.102), channel_id=1, source_target_pairs={{0,4},{4,0},{8,12},{12,8},{16,20},{20,16},{24,28},{28,24},{1,5},{5... | collective-permute-start | bytes 3145736 | tf_op jit(solution)/shard_map/ppermute | solution.py:556
  216.7 119.9 %collective-permute-start.79 = (bf16[1024,512]{1,0:T(8,128)(2,1)}, bf16[1024,512]{1,0:T(8,128)(2,1)}, u32[]{:S(2)}, u32[]{:S(2)}) collective-permute-start(bf16[1024,512]{1,0:T(8,128)(2,1)} %get-tuple-element.104), channel_id=1, source_target_pairs={{0,4},{4,0},{8,12},{12,8},{16,20},{20,16},{24,28},{28,24},{1,5},{5... | collective-permute-start | bytes 3145736 | tf_op jit(solution)/shard_map/ppermute | solution.py:556
  283.8 25.5 %collective-permute-start.45 = (bf16[4,4,16,1152]{3,2,1,0:T(8,128)(2,1)S(1)}, bf16[4,4,16,1152]{3,2,1,0:T(8,128)(2,1)S(1)}, u32[]{:S(2)}, u32[]{:S(2)}) collective-permute-start(bf16[4,4,16,1152]{3,2,1,0:T(8,128)(2,1)S(1)} %get-tuple-element.86), channel_id=1, source_target_pairs={{0,4},{4,0},{8,12},{12,8},{16,20},{20,16},{24,28},{28,24},{1,5},{5... | collective-permute-start | bytes 1769480 | tf_op jit(solution)/shard_map/ppermute | solution.py:556
  336.6 64.5 %collective-permute-start.74 = (bf16[256,512]{1,0:T(8,128)(2,1)S(1)}, bf16[256,512]{1,0:T(8,128)(2,1)S(1)}, u32[]{:S(2)}, u32[]{:S(2)}) collective-permute-start(bf16[256,512]{1,0:T(8,128)(2,1)S(1)} %slice.283), channel_id=1, source_target_pairs={{0,16},{4,20},{8,24},{12,28},{16,0},{20,4},{24,8},{28,12},{1,17},{... | collective-permute-start | bytes 786440 | tf_op jit(solution)/shard_map/ppermute | solution.py:556
  342.8 33.3 %collective-permute-start.84 = (bf16[512,512]{1,0:T(8,128)(2,1)S(1)}, bf16[512,512]{1,0:T(8,128)(2,1)S(1)}, u32[]{:S(2)}, u32[]{:S(2)}) collective-permute-start(bf16[512,512]{1,0:T(8,128)(2,1)S(1)} %slice.293), channel_id=1, source_target_pairs={{0,8},{4,12},{8,0},{12,4},{16,24},{20,28},{24,16},{28,20},{1,9},{5... | collective-permute-start | bytes 1572872 | tf_op jit(solution)/shard_map/ppermute | solution.py:556
  344.6 31.9 %collective-permute-start.58 = (bf16[512,512]{1,0:T(8,128)(2,1)S(1)}, bf16[512,512]{1,0:T(8,128)(2,1)S(1)}, u32[]{:S(2)}, u32[]{:S(2)}) collective-permute-start(bf16[512,512]{1,0:T(8,128)(2,1)S(1)} %slice.269), channel_id=1, source_target_pairs={{0,16},{4,20},{8,24},{12,28},{16,0},{20,4},{24,8},{28,12},{1,17},{... | collective-permute-start | bytes 1572872 | tf_op jit(solution)/shard_map/ppermute | solution.py:556
  398.8 28.7 %collective-permute-start.82 = (bf16[256,512]{1,0:T(8,128)(2,1)S(1)}, bf16[256,512]{1,0:T(8,128)(2,1)S(1)}, u32[]{:S(2)}, u32[]{:S(2)}) collective-permute-start(bf16[256,512]{1,0:T(8,128)(2,1)S(1)} %add_convert_fusion.21), channel_id=1, source_target_pairs={{0,2},{1,3},{2,0},{3,1},{4,6},{5,7},{6,4},{7,5},{8,10},{9,11},{10,... | collective-permute-start | bytes 786440 | tf_op jit(solution)/shard_map/ppermute | solution.py:559
  399.0 28.5 %collective-permute-start.86 = (bf16[256,512]{1,0:T(8,128)(2,1)S(1)}, bf16[256,512]{1,0:T(8,128)(2,1)S(1)}, u32[]{:S(2)}, u32[]{:S(2)}) collective-permute-start(bf16[256,512]{1,0:T(8,128)(2,1)S(1)} %add_convert_fusion.20), channel_id=1, source_target_pairs={{0,1},{1,2},{2,3},{3,0},{4,5},{5,6},{6,7},{7,4},{8,9},{9,10},{10,1... | collective-permute-start | bytes 786440 | tf_op jit(solution)/shard_map/ppermute | solution.py:559
  399.7 29.9 %collective-permute-start.56 = (bf16[256,512]{1,0:T(8,128)(2,1)S(1)}, bf16[256,512]{1,0:T(8,128)(2,1)S(1)}, u32[]{:S(2)}, u32[]{:S(2)}) collective-permute-start(bf16[256,512]{1,0:T(8,128)(2,1)S(1)} %slice.267), channel_id=1, source_target_pairs={{0,8},{4,12},{8,0},{12,4},{16,24},{20,28},{24,16},{28,20},{1,9},{5... | collective-permute-start | bytes 786440 | tf_op jit(solution)/shard_map/ppermute | solution.py:556
  401.0 52.3 %collective-permute-start.42 = (bf16[1,16,1024]{2,1,0:T(8,128)(2,1)S(1)}, bf16[1,16,1024]{2,1,0:T(8,128)(2,1)S(1)}, u32[]{:S(2)}, u32[]{:S(2)}) collective-permute-start(bf16[1,16,1024]{2,1,0:T(8,128)(2,1)S(1)} %fusion.7), channel_id=1, source_target_pairs={{0,8},{4,12},{8,0},{12,4},{16,24},{20,28},{24,16},{28,20},{1,9},{5... | collective-permute-start | bytes 98312 | tf_op jit(solution)/shard_map/ppermute | solution.py:556
  (106 other events, 1420.8 us)

commit v2 on v1

v2 whole, which is shorter than its diff:
```python
import functools
import math

import jax
import jax.numpy as jnp
from jax import lax
from jax.experimental import pallas as pl
from jax.experimental.pallas import tpu as pltpu
from jax.sharding import PartitionSpec as P

HEADS = 8
CAP = 640
NORM_EPS = 1e-06
F32 = jnp.float32
BF16 = jnp.bfloat16
PAD = 256
PIECES = 8
BITS = (2, 4, 1)
WIDE = 512
SMALL = 128
MIB = 1 << 20


def offset_of(position):
    total = 0
    for k, bit in enumerate(BITS):
        total = total + ((position >> k) & 1) * bit
    return total


def dot_nn(a, b):
    return lax.dot_general(a, b, (((1,), (0,)), ((), ())), preferred_element_type=F32)


def dot_nt(a, b):
    return lax.dot_general(a, b, (((1,), (1,)), ((), ())), preferred_element_type=F32)


def dot_tn(a, b):
    return lax.dot_general(a, b, (((0,), (0,)), ((), ())), preferred_element_type=F32)


def norm_parts(values):
    center = values - jnp.mean(values, axis=-1, keepdims=True)
    spread = jnp.mean(center * center, axis=-1, keepdims=True)
    rstd = lax.rsqrt(spread + NORM_EPS)
    return center * rstd, rstd


def gelu_parts(v):
    size = jnp.abs(v)
    density = jnp.exp(v * v * (-0.5)) * 0.3989422804014327
    t = 1.0 / (1.0 + 0.2316418882 * size)
    series = t * (
        0.319381530 + t * (-0.356563782 + t * (1.781477937 + t * (-1.821255978 + t * 1.330274429)))
    )
    tail = density * series
    phi = jnp.where(v < 0, tail, 1.0 - tail)
    return v * phi, phi + v * density


def params(megabytes=60):
    return pltpu.CompilerParams(vmem_limit_bytes=megabytes * MIB)


def cost(microseconds, megabytes):
    return pl.CostEstimate(flops=int(microseconds * 1.1e9), bytes_accessed=int(megabytes * MIB), transcendentals=0)


def padded(length):
    return -(-length // 16) * 16


def pack_kernel(place, qkv, proj, router, *refs):
    *vectors, out, lines, turned = refs
    depth = out.shape[0]
    row = pl.multiple_of(place[1] * depth, depth)
    width = qkv.shape[1] + proj.shape[1]
    lines[...] = jnp.zeros_like(lines)
    lines[: router.shape[0], :] = router[...].astype(F32)
    at = 4
    for vector in vectors:
        values = vector[...].astype(F32).reshape(1, -1)
        for c in range(values.shape[1] // 128):
            lines[at : at + 1, :] = values[:, c * 128 : (c + 1) * 128]
            at += 1
        if at == 11:
            at = 12
    turned[...] = lines[...].T
    out[:, : qkv.shape[1]] = qkv[pl.ds(row, depth), :]
    out[:, qkv.shape[1] : width] = proj[pl.ds(row, depth), :]
    out[:, width:] = turned[pl.ds(row, depth), :].astype(BF16)


def pack_call(place, qkv, proj, router, vectors):
    shard = qkv.shape[0]
    vmem = pl.BlockSpec(memory_space=pltpu.VMEM)
    return pl.pallas_call(
        pack_kernel,
        out_shape=jax.ShapeDtypeStruct((shard // PIECES, qkv.shape[1] + proj.shape[1] + SMALL), BF16),
        in_specs=[pl.BlockSpec(memory_space=pltpu.SMEM)] + [vmem] * (3 + len(vectors)),
        out_specs=vmem,
        scratch_shapes=[pltpu.VMEM((SMALL, shard), F32), pltpu.VMEM((shard, SMALL), F32)],
        cost_estimate=cost(2, 1),
        name="pack_dense",
    )(place, qkv, proj, router.T, *vectors)


def cut_kernel(place, inner, outer, out):
    out[0] = inner[0].T
    out[1] = outer[0]


def cut_call(place, inner, outer):
    _, model, hidden = inner.shape
    block = hidden // PIECES
    return pl.pallas_call(
        cut_kernel,
        out_shape=jax.ShapeDtypeStruct((2, block, model), BF16),
        grid_spec=pltpu.PrefetchScalarGridSpec(
            num_scalar_prefetch=1,
            grid=(1,),
            in_specs=[
                pl.BlockSpec((1, model, block), lambda i, s: (0, 0, s[1])),
                pl.BlockSpec((1, block, model), lambda i, s: (0, s[1], 0)),
            ],
            out_specs=pl.BlockSpec((2, block, model), lambda i, s: (0, 0, 0)),
        ),
        compiler_params=params(),
        cost_estimate=cost(2, 1),
        name="cut_own",
    )(place, inner, outer)


def forward_kernel(
    place, images, cot, *refs,
):
    dense = refs[:PIECES]
    qkv_out, att_out, res_out, lse_out, tok_out, gates_out, full_out, small_out, rows = refs[PIECES:]
    model = images.shape[2]
    length = images.shape[1]
    size = rows.shape[0]
    parts, depth = dense[0].shape[:2]

    @pl.when(pl.program_id(0) == 0)
    def _():
        z, r = place[0], place[1]
        for pos in range(PIECES):
            for d in range(parts):
                owner = lax.rem(z + parts - d, parts) * PIECES
                row = pl.multiple_of((owner + jnp.bitwise_xor(r, offset_of(pos))) * depth, depth)
                full_out[pl.ds(row, depth), :] = dense[pos][d]
        small_out[...] = full_out[:, 4 * model :].astype(F32).T
        rows[...] = jnp.zeros_like(rows)

    def vector(row):
        return small_out[row : row + 1, :]

    rows[:length, :] = images[0].astype(F32)
    x = rows[...]
    xhat, _ = norm_parts(x)
    normed = (xhat * vector(4) + vector(5)).astype(BF16)
    projected = dot_nn(normed, full_out[:, : 3 * model])
    bias_parts = []
    for part in range(parts):
        lanes = slice(part * 128, part * 128 + 128)
        bias_parts += [small_out[9:10, lanes], small_out[10:11, lanes]]
    pair = jnp.concatenate(bias_parts, axis=1)
    qkv_out[0, :, :model] = (projected[:, :model] + pair[:, :model]).astype(BF16)
    qkv_out[0, :, model : 2 * model] = projected[:, model : 2 * model].astype(BF16)
    qkv_out[0, :, 2 * model :] = (projected[:, 2 * model :] + pair[:, model:]).astype(BF16)
    qkv_out[0, length:, :] = jnp.zeros((size - length, 3 * model), BF16)

    head = model // HEADS
    first = lax.broadcasted_iota(jnp.int32, (1, 2 * head), 1) < head
    real = lax.broadcasted_iota(jnp.int32, (1, size), 1) < length
    column = lax.broadcasted_iota(jnp.int32, (size, 128), 1)
    scale = 1.0 / math.sqrt(head)
    lse = jnp.zeros((size, 128), F32)
    attended = []
    for two in range(HEADS // 2):
        lanes = lambda start: slice(start + two * 2 * head, start + (two + 1) * 2 * head)
        q2, k2, v2 = (qkv_out[0, :, lanes(s * model)] for s in range(3))
        zero = jnp.zeros_like(q2)
        stack = jnp.concatenate([jnp.where(first, q2, zero), jnp.where(first, zero, q2)], axis=0)
        scores = jnp.where(real, dot_nt(stack, k2) * scale, -1e30)
        peak = jnp.max(scores, axis=-1, keepdims=True)
        e = jnp.exp(scores - peak)
        total = jnp.sum(e, axis=-1, keepdims=True)
        probs = (e * (1.0 / total)).astype(BF16)
        both = dot_nn(probs, v2)
        attended.append(jnp.where(first, both[:size], both[size:]).astype(BF16))
        logs = peak + jnp.log(total)
        lse = jnp.where(column == 2 * two, logs[:size], lse)
        lse = jnp.where(column == 2 * two + 1, logs[size:], lse)
    lse_out[0] = lse
    attended = jnp.concatenate(attended, axis=1)
    att_out[0] = attended
    residual = x + (dot_nn(attended, full_out[:, 3 * model : 4 * model]) + vector(6))
    res_out[0] = residual
    xhat2, _ = norm_parts(residual)
    normed2 = (xhat2 * vector(7) + vector(8)).astype(BF16)
    tail = length // 16 * 16
    tok_out[tail:, :] = jnp.zeros((PAD - tail, 2 * model), BF16)
    tok_out[:size, :model] = normed2
    tok_out[:length, model:] = cot[0]
    logits = dot_nt(small_out[0:8, :].astype(BF16), tok_out[:, :model])
    experts = lax.broadcasted_iota(jnp.int32, logits.shape, 0) < parts
    logits = jnp.where(experts, logits, -jnp.inf)
    e = jnp.exp(logits - jnp.max(logits, axis=0, keepdims=True))
    gates_out[0] = e / jnp.sum(e, axis=0, keepdims=True)


def whole(a):
    return pl.BlockSpec(a.shape, lambda i, *_: (0,) * len(a.shape))


def image(*dims):
    return pl.BlockSpec((1,) + dims, lambda i, *_: (i, 0, 0))


def forward_call(place, images, cot, dense):
    count, length, model = images.shape
    size = padded(length)
    outs = (
        jax.ShapeDtypeStruct((count, size, 3 * model), BF16),
        jax.ShapeDtypeStruct((count, size, model), BF16),
        jax.ShapeDtypeStruct((count, size, model), F32),
        jax.ShapeDtypeStruct((count, size, 128), F32),
        jax.ShapeDtypeStruct((count * PAD, 2 * model), BF16),
        jax.ShapeDtypeStruct((count, 8, PAD), F32),
        jax.ShapeDtypeStruct((model, 4 * model + SMALL), BF16),
        jax.ShapeDtypeStruct((SMALL, model), F32),
    )
    return pl.pallas_call(
        forward_kernel,
        out_shape=outs,
        grid_spec=pltpu.PrefetchScalarGridSpec(
            num_scalar_prefetch=1,
            grid=(count,),
            in_specs=[image(length, model), image(length, model)] + [whole(d) for d in dense],
            out_specs=[
                image(size, 3 * model), image(size, model), image(size, model), image(size, 128),
                pl.BlockSpec((PAD, 2 * model), lambda i, *_: (i, 0)),
                image(8, PAD), whole(outs[6]), whole(outs[7]),
            ],
            scratch_shapes=[pltpu.VMEM((size, model), F32)],
        ),
        compiler_params=params(),
        cost_estimate=cost(12, 12),
        name="attention_forward",
    )(place, images, cot, *dense)


def expert_kernel(place, slots, gates, small, tok, *refs, turn, sources, count_in):
    arrays = refs[:count_in]
    keep, send, pair_out, bias_out = refs[count_in : count_in + 4]
    tokens, onehot, buffer, grad_slots, rows, back, mine, inners, outers, staged, token_sem, in_sems, out_sems = (
        refs[count_in + 4 :]
    )
    local = sources is None
    count = slots.shape[0]
    model = buffer.shape[1]
    block = outers.shape[1]
    per = staged.shape[1]
    steps = staged.shape[0]

    token_copy = pltpu.make_async_copy(tok, tokens, token_sem)
    token_copy.start()
    loads = []
    for pos in range(PIECES):
        for side, matrices in enumerate((inners, outers)):
            if local:
                start = pl.multiple_of(jnp.bitwise_xor(place[1], offset_of(pos)) * block, block)
                source = arrays[1].at[0, pl.ds(start, block)] if side else arrays[0].at[0, :, pl.ds(start, block)]
            else:
                which, at = sources(pos, side)
                source = arrays[which].at[at]
            loads.append(pltpu.make_async_copy(source, matrices.at[pos], in_sems.at[pos, side]))

    expert = lax.rem(place[0] + place[3] - turn, place[3])
    lanes = pl.ds(pl.multiple_of(expert * 128, 128), 128)
    mine[...] = small[:, lanes]
    where = lax.broadcasted_iota(jnp.int32, (CAP, PAD), 0)
    gate = jnp.zeros((CAP, 128), F32)
    for b in range(count):
        mask = where == slots[b, turn : turn + 1, :]
        onehot[:, b * PAD : (b + 1) * PAD] = mask.astype(F32).astype(BF16)
        weighted = jnp.where(mask, gates[b, pl.ds(expert, 1), :], 0.0)
        gate = gate + weighted[:, :128] + weighted[:, 128:]
    gate = jnp.sum(gate, axis=1, keepdims=True)
    outer_bias = jnp.concatenate([mine[28 + c : 29 + c, :] for c in range(model // 128)], axis=1)
    token_copy.wait()
    for copy in loads:
        copy.start()
    buffer[...] = dot_nn(onehot[...], tokens[:, :model]).astype(BF16)
    grads = (dot_nn(onehot[...], tokens[:, model:]) * gate).astype(BF16)
    grad_slots[...] = grads
    sums = jnp.sum(grads.astype(F32), axis=0, keepdims=True)
    for c in range(model // 128):
        bias_out[16 + c : 17 + c, :] = sums[:, c * 128 : (c + 1) * 128]
    bias_out[20:32, :] = jnp.zeros((12, 128), F32)

    def first_products(i):
        for copy in loads[2 * i * per : 2 * (i + 1) * per]:
            copy.wait()
        buf, gs = buffer[...], grad_slots[...]
        here = slice(i * per, (i + 1) * per)
        lines = [
            jnp.bitwise_xor(place[1], offset_of(pos)) * (block // 128) + c
            for pos in range(here.start, here.stop)
            for c in range(block // 128)
        ]
        bias = jnp.concatenate([mine[pl.ds(12 + line, 1), :] for line in lines], axis=1)
        if local:
            hidden = jnp.concatenate([dot_nn(buf, inners[pos]) for pos in range(here.start, here.stop)], axis=1)
        else:
            hidden = dot_nt(buf, inners[here].reshape(per * block, model))
        return hidden + bias, dot_nt(gs, outers[here].reshape(per * block, model)), lines

    stores = []
    for i in range(steps):
        hidden, grad_active, lines = first_products(i)
        here = slice(i * per, (i + 1) * per)
        active, slope = gelu_parts(hidden)
        active = active.astype(BF16)
        grad_low = (grad_active * slope).astype(BF16)
        sums = jnp.sum(grad_low.astype(F32), axis=0, keepdims=True)
        for k, line in enumerate(lines):
            bias_out[pl.ds(line, 1), :] = sums[:, k * 128 : (k + 1) * 128]
        staged[i, :, 0] = dot_tn(grad_low, buffer[...]).astype(BF16).reshape(per, block, model)
        staged[i, :, 1] = dot_tn(active, grad_slots[...]).astype(BF16).reshape(per, block, model)
        out = keep if i < steps // 2 else send
        stores.append(pltpu.make_async_copy(staged.at[i], out.at[:, i % (steps // 2)], out_sems.at[i]))
        stores[-1].start()
        new_rows = dot_nn(active, outers[here].reshape(per * block, model))
        if local:
            new_back = sum(
                dot_nt(grad_low[:, j * block : (j + 1) * block], inners[i * per + j]) for j in range(per)
            )
        else:
            new_back = dot_nn(grad_low, inners[here].reshape(per * block, model))
        rows[...] = new_rows + (outer_bias if i == 0 else rows[...])
        back[...] = new_back if i == 0 else new_back + back[...]
    pair_out[:, :model] = rows[...].astype(BF16)
    pair_out[:, model:] = back[...].astype(BF16)
    for copy in stores:
        copy.wait()


def expert_call(turn, place, tok, slots, gates, small, weights):
    arrays, sources = weights
    model = tok.shape[1] // 2
    count = slots.shape[0]
    block = arrays[1].shape[1] // PIECES if sources is None else arrays[0].shape[-2]
    per = WIDE // block
    steps = PIECES // per
    vmem = pl.BlockSpec(memory_space=pltpu.VMEM)
    anywhere = pl.BlockSpec(memory_space=pl.ANY)
    half = jax.ShapeDtypeStruct((2, 2, 2, block, model), BF16)
    return pl.pallas_call(
        functools.partial(expert_kernel, turn=turn, sources=sources, count_in=len(arrays)),
        out_shape=(
            half,
            half,
            jax.ShapeDtypeStruct((CAP, 2 * model), BF16),
            jax.ShapeDtypeStruct((32, 128), F32),
        ),
        in_specs=[pl.BlockSpec(memory_space=pltpu.SMEM), vmem, vmem, vmem, anywhere] + [anywhere] * len(arrays),
        out_specs=[anywhere, anywhere, vmem, vmem],
        scratch_shapes=[
            pltpu.VMEM(tok.shape, BF16),
            pltpu.VMEM((CAP, count * PAD), BF16),
            pltpu.VMEM((CAP, model), BF16),
            pltpu.VMEM((CAP, model), BF16),
            pltpu.VMEM((CAP, model), F32),
            pltpu.VMEM((CAP, model), F32),
            pltpu.VMEM((SMALL, 128), F32),
            pltpu.VMEM((PIECES, model, block) if sources is None else (PIECES, block, model), BF16),
            pltpu.VMEM((PIECES, block, model), BF16),
            pltpu.VMEM((steps, per, 2, block, model), BF16),
            pltpu.SemaphoreType.DMA(()),
            pltpu.SemaphoreType.DMA((PIECES, 2)),
            pltpu.SemaphoreType.DMA((steps,)),
        ],
        compiler_params=params(),
        cost_estimate=cost(18, 14),
        name="expert",
    )(place, slots, gates, small, tok, *arrays)


def norm_back(inner, xhat, rstd):
    return rstd * (
        inner - jnp.mean(inner, axis=-1, keepdims=True) - xhat * jnp.mean(inner * xhat, axis=-1, keepdims=True)
    )


def combine_kernel(place, *refs, turns, lo, carried, last):
    cot, att, res, tok, slots, full, small = refs[:7]
    pairs = refs[7 : 7 + turns]
    biases = refs[7 + turns : 7 + 2 * turns]
    before = refs[7 + 2 * turns : 7 + 2 * turns + 6 * carried]
    *outs, cots = refs[7 + 2 * turns + 6 * carried :]
    block_out, gres_out, gatt_out, acc_proj, acc_router, acc_small = outs[:6]
    b = pl.program_id(0)
    length, model = cot.shape[1:]
    size = cots.shape[0]
    parts = turns

    @pl.when(b == 0)
    def _():
        cots[...] = jnp.zeros_like(cots)
        for k, acc in enumerate((acc_proj, acc_router, acc_small)):
            acc[...] = before[3 + k][...] if carried else jnp.zeros_like(acc)

    def vector(row):
        return small[row : row + 1, :]

    def add_row(row, values):
        acc_small[row : row + 1, :] += jnp.sum(values, axis=0, keepdims=True)

    live = (lo + b < place[2]).astype(F32)
    cots[:length, :] = cot[0].astype(F32) * live
    grad_out = cots[...]
    residual = res[0]
    xhat2, rstd2 = norm_parts(residual)
    normed2 = tok[:size, :model]
    router = full[:, 4 * model :]

    logits = dot_nn(normed2, router)
    lane = lax.broadcasted_iota(jnp.int32, logits.shape, 1)
    logits = jnp.where(lane < parts, logits, -jnp.inf)
    e = jnp.exp(logits - jnp.max(logits, axis=-1, keepdims=True))
    probs = e / jnp.sum(e, axis=-1, keepdims=True)

    seat = lax.broadcasted_iota(jnp.int32, (size, CAP), 1)
    mixture = None
    grad_n2 = None
    grad_probs = jnp.zeros_like(probs)
    for j in range(turns):
        expert = lax.rem(place[0] + parts - j, parts)
        mask = (slots[0][:, j : j + 1] == seat).astype(F32).astype(BF16)
        both = dot_nn(mask, pairs[j][...])
        picked = both[:, :model]
        gate = jnp.sum(jnp.where(lane == expert, probs, 0.0), axis=-1, keepdims=True)
        mixture = gate * picked if mixture is None else mixture + gate * picked
        grad_gate = jnp.sum(grad_out * picked, axis=-1, keepdims=True)
        grad_probs = jnp.where(lane == expert, grad_gate, grad_probs)
        grad_n2 = both[:, model:] if grad_n2 is None else grad_n2 + both[:, model:]
    block_out[0] = ((residual + mixture) * live).astype(BF16)[:length]
    grad_logits = probs * (grad_probs - jnp.sum(probs * grad_probs, axis=-1, keepdims=True))
    grad_logits = grad_logits.astype(BF16)
    grad_n2 = grad_n2 + dot_nt(grad_logits, router)
    acc_router[...] += dot_tn(normed2, grad_logits)

    add_row(7, grad_n2 * xhat2)
    add_row(8, grad_n2)
    grad_res = grad_out + norm_back(grad_n2 * vector(7), xhat2, rstd2)
    gres_out[0] = grad_res
    branch = grad_res.astype(BF16)
    add_row(6, branch.astype(F32))
    acc_proj[...] += dot_tn(att[0], branch)
    gatt_out[0] = dot_nt(branch, full[:, 3 * model : 4 * model]).astype(BF16)

    if not last:
        return

    @pl.when(b == pl.num_programs(0) - 1)
    def _():
        late_out = outs[-1]
        for j in range(turns):
            expert = lax.rem(place[0] + parts - j, parts)
            acc_small[12:32, pl.ds(pl.multiple_of(expert * 128, 128), 128)] = biases[j][0:20, :]
        late_out[:, :model] = acc_proj[...].astype(BF16)
        late_out[:, model:] = (acc_router[...] + acc_small[...].T).astype(BF16)


def part_of(lo, *dims):
    return pl.BlockSpec((1,) + dims, lambda i, *_: (lo + i, 0, 0))


def combine_call(lo, hi, before, place, cot, att, res, tok, slots, full, small, pairs, biases):
    count, length, model = cot.shape
    size = att.shape[1]
    turns = len(pairs)
    last = hi == count
    outs = (
        jax.ShapeDtypeStruct((count, length, model), BF16),
        jax.ShapeDtypeStruct((count, size, model), F32),
        jax.ShapeDtypeStruct((count, size, model), BF16),
        jax.ShapeDtypeStruct((model, model), F32),
        jax.ShapeDtypeStruct((model, SMALL), F32),
        jax.ShapeDtypeStruct((SMALL, model), F32),
    ) + ((jax.ShapeDtypeStruct((model, model + SMALL), BF16),) if last else ())
    image = functools.partial(part_of, lo)
    inputs = (cot, att, res, tok, slots, full, small, *pairs, *biases)
    return pl.pallas_call(
        functools.partial(combine_kernel, turns=turns, lo=lo, carried=len(before) > 0, last=last),
        out_shape=outs,
        grid_spec=pltpu.PrefetchScalarGridSpec(
            num_scalar_prefetch=1,
            grid=(hi - lo,),
            in_specs=[
                image(length, model), image(size, model), image(size, model),
                pl.BlockSpec((PAD, 2 * model), lambda i, *_: (lo + i, 0)),
                image(size, slots.shape[2]),
            ] + [whole(a) for a in inputs[5:]] + [pl.BlockSpec(memory_space=pl.ANY)] * min(3, len(before))
            + [whole(a) for a in before[3:]],
            out_specs=[image(length, model), image(size, model), image(size, model)] + [whole(o) for o in outs[3:]],
            scratch_shapes=[pltpu.VMEM((size, model), F32)],
        ),
        input_output_aliases={1 + len(inputs) + k: k for k in range(len(before))},
        compiler_params=params(),
        cost_estimate=cost(4 * (hi - lo), 14),
        name="combine",
    )(place, *inputs, *before)


def backward_kernel(place, images, qkv, lse, gres, gatt, full, small, late, *refs, parts, carried, last):
    before = refs[: 3 * carried]
    *outs, rows = refs[3 * carried :]
    input_grad, acc_qkv, acc_small = outs[:3]
    b = pl.program_id(0)
    length, model = images.shape[1:]
    size = rows.shape[0]

    @pl.when(b == 0)
    def _():
        rows[...] = jnp.zeros_like(rows)
        for k, acc in enumerate((acc_qkv, acc_small)):
            acc[...] = before[1 + k][...] if carried else jnp.zeros_like(acc)

    def vector(row):
        return small[row : row + 1, :]

    def add_row(row, values):
        acc_small[row : row + 1, :] += jnp.sum(values, axis=0, keepdims=True)

    head = model // HEADS
    first = lax.broadcasted_iota(jnp.int32, (1, 2 * head), 1) < head
    real = lax.broadcasted_iota(jnp.int32, (1, size), 1) < length
    scale = 1.0 / math.sqrt(head)
    grads = [[], [], []]
    for two in range(HEADS // 2):
        lanes = lambda start: slice(start + two * 2 * head, start + (two + 1) * 2 * head)
        q2, k2, v2 = (qkv[0, :, lanes(s * model)] for s in range(3))
        g2 = gatt[0, :, lanes(0)]
        zero = jnp.zeros_like(q2)
        stack = lambda t: jnp.concatenate([jnp.where(first, t, zero), jnp.where(first, zero, t)], axis=0)
        merge = lambda t: jnp.where(first, t[:size], t[size:])
        qs, gs = stack(q2), stack(g2)
        logs = jnp.concatenate([lse[0, :, 2 * two : 2 * two + 1], lse[0, :, 2 * two + 1 : 2 * two + 2]], axis=0)
        weights = jnp.where(real, jnp.exp(dot_nt(qs, k2) * scale - logs), 0.0)
        grad_weights = dot_nt(gs, v2)
        grad_scores = weights * (grad_weights - jnp.sum(grad_weights * weights, axis=-1, keepdims=True))
        grad_scores = grad_scores.astype(BF16)
        grads[0].append((merge(dot_nn(grad_scores, k2)) * scale).astype(BF16))
        grads[1].append((dot_tn(grad_scores, qs) * scale).astype(BF16))
        grads[2].append(dot_tn(weights.astype(BF16), gs).astype(BF16))
    grad_projected = jnp.concatenate(grads[0] + grads[1] + grads[2], axis=1)
    rows[:length, :] = images[0].astype(F32)
    xhat1, rstd1 = norm_parts(rows[...])
    normed = (xhat1 * vector(4) + vector(5)).astype(BF16)
    acc_qkv[:, : 3 * model] += dot_tn(normed, grad_projected)
    grad_normed = dot_nt(grad_projected, full[:, : 3 * model])
    add_row(4, grad_normed * xhat1)
    add_row(5, grad_normed)
    add_row(32, grad_projected[:, :model].astype(F32))
    add_row(33, grad_projected[:, 2 * model :].astype(F32))
    input_grad[0] = (gres[0] + norm_back(grad_normed * vector(4), xhat1, rstd1))[:length]

    if not last:
        return

    @pl.when(b == pl.num_programs(0) - 1)
    def _():
        keep, send = outs[-2:]
        for part in range(parts):
            for k in range(2):
                start = (part * 2 + k) * 128
                source = 32 + start // model
                acc_small[9 + k : 10 + k, part * 128 : part * 128 + 128] = acc_small[
                    source : source + 1, start % model : start % model + 128
                ]
        acc_small[32:34, :] = jnp.zeros((2, model), F32)
        acc_qkv[:, 3 * model :] = acc_small[...].T + late[:, model:].astype(F32)
        depth = keep.shape[2]
        for pos in range(PIECES):
            for d in range(parts):
                owner = lax.rem(place[0] + parts - d, parts) * PIECES
                row = pl.multiple_of((owner + jnp.bitwise_xor(place[1], offset_of(pos))) * depth, depth)
                out = keep if pos < PIECES // 2 else send
                spot = pos % (PIECES // 2)
                out[spot, d, :, : 3 * model] = acc_qkv[pl.ds(row, depth), : 3 * model].astype(BF16)
                out[spot, d, :, 3 * model : 4 * model] = late[pl.ds(row, depth), :model]
                out[spot, d, :, 4 * model :] = acc_qkv[pl.ds(row, depth), 3 * model :].astype(BF16)


def backward_call(lo, hi, before, place, images, qkv, lse, gres, gatt, full, small, late, turns):
    count, length, model = images.shape
    size = qkv.shape[1]
    depth = model // (turns * PIECES)
    last = hi == count
    half = jax.ShapeDtypeStruct((PIECES // 2, turns, depth, 4 * model + SMALL), BF16)
    outs = (
        jax.ShapeDtypeStruct((count, length, model), F32),
        jax.ShapeDtypeStruct((model, 3 * model + SMALL), F32),
        jax.ShapeDtypeStruct((SMALL, model), F32),
    ) + ((half, half) if last else ())
    image = functools.partial(part_of, lo)
    inputs = (images, qkv, lse, gres, gatt, full, small, late)
    return pl.pallas_call(
        functools.partial(backward_kernel, parts=turns, carried=len(before) > 0, last=last),
        out_shape=outs,
        grid_spec=pltpu.PrefetchScalarGridSpec(
            num_scalar_prefetch=1,
            grid=(hi - lo,),
            in_specs=[
                image(length, model), image(size, 3 * model), image(size, 128), image(size, model),
                image(size, model), whole(full), whole(small), whole(late),
            ] + [pl.BlockSpec(memory_space=pl.ANY)] * min(1, len(before)) + [whole(a) for a in before[1:]],
            out_specs=[image(length, model)] + [whole(o) for o in outs[1:]],
            scratch_shapes=[pltpu.VMEM((size, model), F32)],
        ),
        input_output_aliases={1 + len(inputs) + k: k for k in range(len(before))},
        compiler_params=params(),
        cost_estimate=cost(4 * (hi - lo), 14),
        name="attention_backward",
    )(place, *inputs, *before)


def finish_kernel(place, *refs):
    pieces = refs[: PIECES // 2]
    inner_out, outer_out = refs[-2:]
    for k, piece in enumerate(pieces):

        @pl.when(pl.program_id(0) == k)
        def _():
            inner_out[0] = piece[0].astype(F32).T
            outer_out[0] = piece[1].astype(F32)


def finish_call(half, place, pieces, outs=()):
    _, block, model = pieces[0].shape
    piece = lambda i, s: jnp.bitwise_xor(s[1], offset_of(i + 4 * half))
    return pl.pallas_call(
        finish_kernel,
        out_shape=(
            jax.ShapeDtypeStruct((1, model, PIECES * block), F32),
            jax.ShapeDtypeStruct((1, PIECES * block, model), F32),
        ),
        grid_spec=pltpu.PrefetchScalarGridSpec(
            num_scalar_prefetch=1,
            grid=(PIECES // 2,),
            in_specs=[whole(p) for p in pieces] + [pl.BlockSpec(memory_space=pl.ANY)] * len(outs),
            out_specs=[
                pl.BlockSpec((1, model, block), lambda i, s: (0, 0, piece(i, s))),
                pl.BlockSpec((1, block, model), lambda i, s: (0, piece(i, s), 0)),
            ],
        ),
        input_output_aliases={1 + len(pieces) + k: k for k in range(len(outs))},
        compiler_params=params(),
        cost_estimate=cost(4, 6),
        name="finish_experts",
    )(place, *pieces, *outs)


def finish_dense_kernel(place, *refs):
    pieces = refs[:PIECES]
    qkv_out, proj_out, router_out, inner_out, outer_out, rest_out, table = refs[PIECES:]
    model = proj_out.shape[1]
    depth = pieces[0].shape[0]
    for pos in range(PIECES):
        row = pl.multiple_of(jnp.bitwise_xor(place[1], offset_of(pos)) * depth, depth)
        block = pieces[pos][...].astype(F32)
        qkv_out[pl.ds(row, depth), :] = block[:, : 3 * model]
        proj_out[pl.ds(row, depth), :] = block[:, 3 * model : 4 * model]
        table[pl.ds(row, depth), :] = block[:, 4 * model :]
    table[...] = table[...].T
    router_out[...] = table[: router_out.shape[0], :]
    rest_out[...] = table[4 : 4 + rest_out.shape[0], :]
    for c in range(inner_out.shape[1] // 128):
        inner_out[:, c * 128 : (c + 1) * 128] = table[12 + c : 13 + c, :]
    for c in range(outer_out.shape[1] // 128):
        outer_out[:, c * 128 : (c + 1) * 128] = table[28 + c : 29 + c, :]


def finish_dense_call(place, pieces, model, parts, hidden):
    rows = pieces[0].shape[0] * PIECES
    vmem = pl.BlockSpec(memory_space=pltpu.VMEM)
    return pl.pallas_call(
        finish_dense_kernel,
        out_shape=(
            jax.ShapeDtypeStruct((rows, 3 * model), F32),
            jax.ShapeDtypeStruct((rows, model), F32),
            jax.ShapeDtypeStruct((parts, rows), F32),
            jax.ShapeDtypeStruct((1, hidden), F32),
            jax.ShapeDtypeStruct((1, model), F32),
            jax.ShapeDtypeStruct((8, rows), F32),
        ),
        in_specs=[pl.BlockSpec(memory_space=pltpu.SMEM)] + [vmem] * PIECES,
        scratch_shapes=[pltpu.VMEM((rows, SMALL), F32)],
        cost_estimate=cost(2, 2),
        name="finish_dense",
    )(place, *pieces)


def join(*values):
    return lax.optimization_barrier(values)


def local(
    images, attn_norm_gain, attn_norm_bias, qkv_weight, query_value_bias, proj_weight, proj_bias,
    moe_norm_gain, moe_norm_bias, router_weight, expert_inner, expert_inner_bias, expert_outer,
    expert_outer_bias, live_count, routes, slot_ids, cotangent, *, n_replica, n_group,
):
    count, length, model = images.shape
    shard = qkv_weight.shape[0]
    hidden = expert_inner.shape[2]
    size = padded(length)
    z = lax.axis_index("group").astype(jnp.int32)
    r = lax.axis_index("replica").astype(jnp.int32) & (PIECES - 1)
    place = jnp.stack([z, r, live_count[0].astype(jnp.int32), jnp.int32(n_group)])

    def across(value, bit):
        return lax.ppermute(value, "replica", [(i, i ^ bit) for i in range(n_replica)])

    def along(value, shift):
        return lax.ppermute(value, "group", [(i, (i + shift) % n_group) for i in range(n_group)])

    def plus(*values):
        return sum(v.astype(F32) for v in values).astype(BF16)

    def both(value, bit):
        return jnp.concatenate([value, across(value, bit)], axis=0)

    def spread(value):
        return [value] + [across(value, offset_of(pos)) for pos in range(1, PIECES // 2)]

    def rest_of_replicas(value):
        bit = PIECES
        while bit < n_replica:
            value = plus(value, across(value, bit))
            bit *= 2
        return value

    shifts = list(range(1, n_group))

    vectors = (attn_norm_gain, attn_norm_bias, proj_bias, moe_norm_gain, moe_norm_bias, query_value_bias)
    mine = pack_call(place, qkv_weight, proj_weight, router_weight, vectors + (expert_inner_bias, expert_outer_bias))
    dense_z = {d: along(mine, d) for d in shifts}

    piece = cut_call(place, expert_inner, expert_outer)
    piece, dense_z = join(piece, dense_z)
    expert_z = {1: along(piece, 1)}
    dense = spread(jnp.stack([mine] + [dense_z[d] for d in range(1, n_group)]))
    dense = dense + [across(v, 1) for v in dense]

    experts = (z + n_group - jnp.arange(n_group, dtype=jnp.int32)) % n_group
    chosen = routes[:, None] == experts[None, :, None, None]
    seats = jnp.max(jnp.where(chosen, slot_ids[:, None], -1), axis=-1)
    slots_lane = jnp.pad(seats, ((0, 0), (0, 8 - n_group), (0, PAD - length)), constant_values=-1)
    slots_row = jnp.pad(
        seats.transpose(0, 2, 1), ((0, 0), (0, size - length), (0, 8 - n_group)), constant_values=-1
    )

    def first_stage(k, got):
        if k == 1:
            return both(got[0][None], 2), both(got[1][None], 4)
        return (both(got[None], 2),)

    def second_stage(k, arrays):
        if k == 1:
            return across(arrays[0], 4), across(arrays[1], 2)
        return (across(arrays[0], 4),)

    def third_stage(arrays):
        return tuple(across(a, 1) for a in arrays)

    def sources(pos, side):
        return pos // 2, (pos % 2, side)

    def sources_first(pos, side):
        x, y, core = pos & 1, pos >> 1 & 1, pos >> 2
        other, at = (x, y) if side else (y, x)
        return 4 * core + 2 * other + side, at

    outs, folds, shards = {}, {}, {}

    at_once = (2, 3)

    def fold_core(k):
        folds[k] = (outs[k][0], across(outs[k][1], 1))

    def fold_one(k):
        keep, core = folds[k]
        if k in at_once:
            quarters = [plus(keep[x, y], core[x, y]) for x, y in ((1, 0), (0, 1), (1, 1))]
            folds[k] = (keep, core) + tuple(across(q, bits) for q, bits in zip(quarters, (2, 4, 6)))
        else:
            folds[k] = (keep, core, across(plus(keep[1], core[1]), 2))

    def fold_two(k):
        keep, core, x = folds[k]
        folds[k] = (keep, core, x, across(plus(keep[0, 1], core[0, 1], x[1]), 4))

    def fold_z(k):
        keep, core, *got = folds[k]
        if k not in at_once:
            got[0] = got[0][0]
        value = rest_of_replicas(plus(keep[0, 0], core[0, 0], *got))
        shards[k] = along(value, -k) if k else value

    one, two, cores = {}, {}, {}
    one[1] = first_stage(1, expert_z[1])
    piece, expert_z[1] = join(piece, expert_z[1])
    expert_z[2] = along(piece, 2)
    one[1], images, dense = join(one[1], images, dense)
    two[1] = second_stage(1, one[1])
    cores[1] = third_stage(one[1])
    qkv, att, res, lse, tok, gates, full, small = forward_call(place, images, cotangent, dense)
    tok, gates, small, piece, one, two, cores, expert_z = join(tok, gates, small, piece, one, two, cores, expert_z)
    tables = (slots_lane, gates, small)

    weights = one[1] + two[1] + cores[1] + third_stage(two[1])
    one[2] = first_stage(2, expert_z[2])
    expert_z[3] = along(piece, 3)
    outs[0] = expert_call(0, place, tok, *tables, ((expert_inner, expert_outer), None))
    outs, tok, weights, one, expert_z = join(outs, tok, weights, one, expert_z)

    two[2] = second_stage(2, one[2])
    cores[2] = third_stage(one[2])
    one[3] = first_stage(3, expert_z[3])
    fold_core(0)
    outs[1] = expert_call(1, place, tok, *tables, (weights, sources_first))
    outs, tok, one, two, cores, folds = join(outs, tok, one, two, cores, folds)

    weights = one[2] + two[2] + cores[2] + third_stage(two[2])
    two[3] = second_stage(3, one[3])
    cores[3] = third_stage(one[3])
    fold_one(0)
    fold_core(1)
    outs[2] = expert_call(2, place, tok, *tables, (weights, sources))
    outs, tok, one, two, cores, folds = join(outs, tok, one, two, cores, folds)

    weights = one[3] + two[3] + cores[3] + third_stage(two[3])
    fold_two(0)
    fold_one(1)
    fold_core(2)
    outs[3] = expert_call(3, place, tok, *tables, (weights, sources))
    outs, folds = join(outs, folds)

    fold_z(0)
    fold_two(1)
    fold_one(2)
    fold_core(3)
    pairs = [outs[k][2] for k in range(n_group)]
    biases = [outs[k][3] for k in range(n_group)]
    block_out, gres, gatt, *_, late = combine_call(
        0, count, (), place, cotangent, att, res, tok, slots_row, full, small, pairs, biases
    )
    gres, gatt, late, folds, shards = join(gres, gatt, late, folds, shards)

    fold_z(1)
    fold_z(2)
    fold_one(3)
    input_grad, *_, keep, send = backward_call(0, count, (), place, images, qkv, lse, gres, gatt, full, small, late, n_group)
    keep, send, folds, shards = join(keep, send, folds, shards)
    fold_z(3)

    value = plus(keep, across(send, 1))
    value = plus(value[0], *(across(value[pos], offset_of(pos)) for pos in range(1, PIECES // 2)))
    value = rest_of_replicas(value)
    value, total = join(value, plus(*shards.values()))
    own_half = spread(total)
    value = plus(*([value[0]] + [along(value[d], -d) for d in range(1, n_group)]))
    value, own_half = join(value, own_half)
    value = spread(value)
    value = value + [across(v, 1) for v in value]
    grad_qkv, grad_proj, grad_router, grad_inner_bias, grad_outer_bias, rest = finish_dense_call(
        place, value, model, n_group, hidden
    )

    other_half = [across(v, 1) for v in own_half]
    grads = finish_call(0, place, own_half)
    grad_inner, grad_outer = finish_call(1, place, other_half, grads)
    return (
        block_out, input_grad, rest[0], rest[1], grad_qkv, rest[5:7].reshape(-1), grad_proj, rest[2], rest[3],
        rest[4], grad_router.T, grad_inner, grad_inner_bias, grad_outer, grad_outer_bias,
    )


def solution(mesh):
    both = ("replica", "group")
    in_specs = (
        P(both, None, None), P("group"), P("group"), P("group", None), P("group"), P("group", None),
        P("group"), P("group"), P("group"), P("group", None), P("group", None, None), P("group", None),
        P("group", None, None), P("group", None), P(both), P(both, None, None), P(both, None, None),
        P(both, None, None),
    )
    out_specs = (
        P(both, None, None), P(both, None, None), P("group"), P("group"), P("group", None), P("group"),
        P("group", None), P("group"), P("group"), P("group"), P("group", None), P("group", None, None),
        P("group", None), P("group", None, None), P("group", None),
    )
    body = functools.partial(local, n_replica=mesh.shape["replica"], n_group=mesh.shape["group"])
    return jax.shard_map(body, mesh=mesh, in_specs=in_specs, out_specs=out_specs, check_vma=False)
```

time: 495 us -> 329 us (0.66)
  waiting for transfers between devices: 153 us -> 79.9 us
  starting transfers between devices: 112 us -> 56.1 us
  local copies, waits for them, and re-layouts: 46.5 us -> 7.33 us
  other arithmetic: 15.3 us -> 25.8 us
  Pallas kernels: 158 us -> 152 us
    ppermute x66 -> x55, waiting for transfers between devices: 114 us -> 47 us  [across(): lax.ppermute(value, 'replica', [(i, i ^ bit) for i in range(n_replica)])]
    ppermute x24 -> x12, starting transfers between devices: 60.9 us -> 16 us  [along(): lax.ppermute(value, 'group', [(i, (i + shift) % n_group) for i in range(n...]
    unnamed x95 -> x80, local copies, waits for them, and re-layouts: 27.4 us -> 2.9 us
    convert_element_type x30 -> x14, other arithmetic: 8.4 us -> 22.6 us  [plus(): return sum((v.astype(F32) for v in values)).astype(BF16)]
    ppermute x66 -> x55, starting transfers between devices: 50.9 us -> 40 us  [across(): lax.ppermute(value, 'replica', [(i, i ^ bit) for i in range(n_replica)])]
    pallas_call x5 -> x8, Pallas kernels: 134 us -> 125 us  [the longest x4 76.9 us: expert_call(): pl.pallas_call(functools.partial(expert_kernel, turn=turn, sources=source...]
    ppermute x24 -> x12, waiting for transfers between devices: 39 us -> 32.9 us  [along(): lax.ppermute(value, 'group', [(i, (i + shift) % n_group) for i in range(n...]
    another operation x9 -> x0, local copies, waits for them, and re-layouts: 5.75 us -> none  [the longest x5 3.93 us: local(): column = lambda vector: vector.reshape(-1, shard).T]
  transfers between devices with their start and end apart: 90 -> 67, of which waited for: 34 -> 18; matrix products, arithmetic and copies ran while one was open for 7% -> 7% of each run, Pallas kernels for 31% -> 45%
where the time goes in v2:
time: 329 us; the launch traced here: 324 us
  Pallas kernels  152 us (46%)
  waiting for transfers between devices  79.9 us (24%)
  starting transfers between devices  56.1 us (17%)
  other arithmetic  25.8 us (8%)
  local copies, waits for them, and re-layouts  7.33 us (2%)
    pallas_call x4, Pallas kernels, expert_call(): pl.pallas_call(functools.partial(expert_kernel, turn=turn, sources=source...  76.9 us
    ppermute x55, waiting for transfers between devices, across(): lax.ppermute(value, 'replica', [(i, i ^ bit) for i in range(n_replica)])  47 us
    ppermute x55, starting transfers between devices, across(): lax.ppermute(value, 'replica', [(i, i ^ bit) for i in range(n_replica)])  40 us
    ppermute x12, waiting for transfers between devices, along(): lax.ppermute(value, 'group', [(i, (i + shift) % n_group) for i in range(n...  32.9 us
    pallas_call x1, Pallas kernels, backward_call(): pl.pallas_call(functools.partial(backward_kernel, parts=turns, carried=le...  23.8 us
    convert_element_type x14, other arithmetic, plus(): return sum((v.astype(F32) for v in values)).astype(BF16)  22.6 us
    pallas_call x1, Pallas kernels, combine_call(): pl.pallas_call(functools.partial(combine_kernel, turns=turns, lo=lo, carr...  19.4 us
    ppermute x12, starting transfers between devices, along(): lax.ppermute(value, 'group', [(i, (i + shift) % n_group) for i in range(n...  16 us
  transfers between devices with their start and end apart: 67, of which 18 were waited for; matrix products, arithmetic and copies ran while one was open for 7% of the time, Pallas kernels for 45%

profile of v2, /device:TPU:0, one launch (start us, length us, event | category | flops | bytes accessed | tf_op | source)
XLA Modules:
  0.0 324.0 jit_solution(2046311259435678416)
XLA Ops:
  3.8 5.1 %collective-permute-start.2 = (bf16[16,2176]{1,0:T(8,128)(2,1)}, bf16[16,2176]{1,0:T(8,128)(2,1)S(1)}, u32[]{:S(2)}, u32[]{:S(2)}) collective-permute-start(bf16[16,2176]{1,0:T(8,128)(2,1)} %pack_dense.1), channel_id=1, source_target_pairs={{0,3},{1,0},{2,1},{3,2},{4,7},{5,4},{6,5},{7,6},{8,11},{9,8},{10,9... | collective-permute-start | bytes 208904 | tf_op jit(solution)/shard_map/ppermute | solution.py:729
  12.5 3.4 %collective-permute-done.1 = bf16[16,2176]{1,0:T(8,128)(2,1)S(1)} collective-permute-done((bf16[16,2176]{1,0:T(8,128)(2,1)}, bf16[16,2176]{1,0:T(8,128)(2,1)S(1)}, u32[]{:S(2)}, u32[]{:S(2)}) %collective-permute-start.1) | collective-permute-done | bytes 69664 | tf_op jit(solution)/shard_map/ppermute | solution.py:729
  19.6 12.1 %collective-permute-done.3 = bf16[2,256,512]{2,1,0:T(8,128)(2,1)S(1)} collective-permute-done((bf16[2,256,512]{2,1,0:T(8,128)(2,1)}, bf16[2,256,512]{2,1,0:T(8,128)(2,1)S(1)}, u32[]{:S(2)}, u32[]{:S(2)}) %collective-permute-start.3) | collective-permute-done | bytes 524320 | tf_op jit(solution)/shard_map/ppermute | solution.py:729
  35.5 3.6 %collective-permute-done.5 = bf16[1,256,512]{2,1,0:T(8,128)(2,1)S(1)} collective-permute-done((bf16[1,256,512]{2,1,0:T(8,128)(2,1)S(1)}, bf16[1,256,512]{2,1,0:T(8,128)(2,1)S(1)}, u32[]{:S(2)}, u32[]{:S(2)}) %collective-permute-start.5) | collective-permute-done | bytes 262176 | tf_op jit(solution)/shard_map/ppermute | solution.py:726
  44.4 16.0 %attention_forward.1 = (bf16[5,208,1536]{2,1,0:T(8,128)(2,1)}, bf16[5,208,512]{2,1,0:T(8,128)(2,1)}, f32[5,208,512]{2,1,0:T(8,128)}, f32[5,208,128]{2,1,0:T(8,12...) custom-call(s32[4]{0:T(128)} %pad_add_fusion.place, ...), custom_call_target="tpu_custom_call" | custom-call | flops 13200000000 | bytes 12582912 | tf_op jit(solution)/shard_map/attention_forward/pallas_call | solution.py:235
  60.5 5.1 %collective-permute-done.17 = bf16[2,256,512]{2,1,0:T(8,128)(2,1)S(1)} collective-permute-done((bf16[2,256,512]{2,1,0:T(8,128)(2,1)}, bf16[2,256,512]{2,1,0:T(8,128)(2,1)S(1)}, u32[]{:S(2)}, u32[]{:S(2)}) %collective-permute-start.17) | collective-permute-done | bytes 524320 | tf_op jit(solution)/shard_map/ppermute | solution.py:729
  70.1 19.0 %expert.4 = (bf16[2,2,2,256,512]{4,3,2,1,0:T(8,128)(2,1)}, bf16[2,2,2,256,512]{4,3,2,1,0:T(8,128)(2,1)}, bf16[640,1024]{1,0:T(8,128)(2,1)}, f32[32,128]{1,0:T(8,128)}) custom-call(s32[4]{0:T(128)} %pad_add_fusion.place, s32[5,8,256]{2,1,0:T(8,128)} %pad.8.slots, f32[5,8,256]{2,1,0:T(8,128)} %get-tuple-element.200.gates, ...), custom_call_target="tpu_custom_call" | custom-call | flops 19800000512 | bytes 14680064 | tf_op jit(solution)/shard_map/expert/pallas_call | solution.py:361
  92.0 19.5 %expert.5 = (bf16[2,2,2,256,512]{4,3,2,1,0:T(8,128)(2,1)}, bf16[2,2,2,256,512]{4,3,2,1,0:T(8,128)(2,1)}, bf16[640,1024]{1,0:T(8,128)(2,1)}, f32[32,128]{1,0:T(8,128)}) custom-call(s32[4]{0:T(128)} %pad_add_fusion.place, s32[5,8,256]{2,1,0:T(8,128)} %pad.8.slots, f32[5,8,256]{2,1,0:T(8,128)} %get-tuple-element.200.gates, ...), custom_call_target="tpu_custom_call" | custom-call | flops 19800000512 | bytes 14680064 | tf_op jit(solution)/shard_map/expert/pallas_call | solution.py:361
  119.3 19.2 %expert.6 = (bf16[2,2,2,256,512]{4,3,2,1,0:T(8,128)(2,1)}, bf16[2,2,2,256,512]{4,3,2,1,0:T(8,128)(2,1)}, bf16[640,1024]{1,0:T(8,128)(2,1)}, f32[32,128]{1,0:T(8,128)}) custom-call(s32[4]{0:T(128)} %pad_add_fusion.place, s32[5,8,256]{2,1,0:T(8,128)} %pad.8.slots, f32[5,8,256]{2,1,0:T(8,128)} %get-tuple-element.200.gates, ...), custom_call_target="tpu_custom_call" | custom-call | flops 19800000512 | bytes 14680064 | tf_op jit(solution)/shard_map/expert/pallas_call | solution.py:361
  138.5 5.5 %collective-permute-done.29 = bf16[2,2,256,512]{3,2,1,0:T(8,128)(2,1)} collective-permute-done((bf16[2,2,256,512]{3,2,1,0:T(8,128)(2,1)S(1)}, bf16[2,2,256,512]{3,2,1,0:T(8,128)(2,1)}, u32[]{:S(2)}, u32[]{:S(2)}) %collective-permute-start.29) | collective-permute-done | bytes 1048608 | tf_op jit(solution)/shard_map/ppermute | solution.py:726
  150.7 19.2 %expert.7 = (bf16[2,2,2,256,512]{4,3,2,1,0:T(8,128)(2,1)}, bf16[2,2,2,256,512]{4,3,2,1,0:T(8,128)(2,1)}, bf16[640,1024]{1,0:T(8,128)(2,1)}, f32[32,128]{1,0:T(8,128)}) custom-call(s32[4]{0:T(128)} %pad_add_fusion.place, s32[5,8,256]{2,1,0:T(8,128)} %pad.8.slots, f32[5,8,256]{2,1,0:T(8,128)} %get-tuple-element.200.gates, ...), custom_call_target="tpu_custom_call" | custom-call | flops 19800000512 | bytes 14680064 | tf_op jit(solution)/shard_map/expert/pallas_call | solution.py:361
  169.9 5.7 %collective-permute-done.33 = bf16[2,2,256,512]{3,2,1,0:T(8,128)(2,1)} collective-permute-done((bf16[2,2,256,512]{3,2,1,0:T(8,128)(2,1)S(1)}, bf16[2,2,256,512]{3,2,1,0:T(8,128)(2,1)}, u32[]{:S(2)}, u32[]{:S(2)}) %collective-permute-start.33) | collective-permute-done | bytes 1048608 | tf_op jit(solution)/shard_map/ppermute | solution.py:726
  179.1 2.8 fusion.19
  185.4 19.4 %combine.1 = (bf16[5,197,512]{2,1,0:T(8,128)(2,1)}, f32[5,208,512]{2,1,0:T(8,128)}, bf16[5,208,512]{2,1,0:T(8,128)(2,1)}, f32[512,512]{1,0:T(8,128)}, f32[512,12...) custom-call(s32[4]{0:T(128)} %pad_add_fusion.place, bf16[5,197,512]{2,1,0:T(8,128)(2,1)} %refs_0_.5, ...), custom_call_target="tpu_custom_call" | custom-call | flops 22000001024 | bytes 14680064 | tf_op jit(solution)/shard_map/combine/pallas_call | solution.py:497
  206.3 7.8 %collective-permute-done.37 = bf16[2,256,512]{2,1,0:T(8,128)(2,1)} collective-permute-done((bf16[2,256,512]{2,1,0:T(8,128)(2,1)}, bf16[2,256,512]{2,1,0:T(8,128)(2,1)}, u32[]{:S(2)}, u32[]{:S(2)}) %collective-permute-start.37) | collective-permute-done | bytes 524320 | tf_op jit(solution)/shard_map/ppermute | solution.py:726
  214.1 3.0 fusion.13
  221.6 2.7 fusion.22
  227.9 23.8 %attention_backward.1 = (f32[5,197,512]{2,1,0:T(8,128)}, f32[512,1664]{1,0:T(8,128)}, f32[128,512]{1,0:T(8,128)}, bf16[4,4,16,2176]{3,2,1,0:T(8,128)(2,1)}, bf16[4,4,16,2176]{3,2,1,0:T(8,128)(2,1)}) custom-call(s32[4]{0:T(128)} %pad_add_fusion.place, bf16[5,197,512]{2,1,0:T(8,128)(2,1)} %images.1, bf16[5,208,1536]{2,1,0:T(8,128)(2,1)} %get-tuple-element.282.qkv, ...), custom_call_target="tpu_custom_call" | custom-call | flops 22000001024 | bytes 14680064 | tf_op jit(solution)/shard_map/attention_backward/pallas_call | solution.py:612
  258.8 11.1 %collective-permute-done.49 = bf16[2,256,512]{2,1,0:T(8,128)(2,1)S(1)} collective-permute-done((bf16[2,256,512]{2,1,0:T(8,128)(2,1)S(1)}, bf16[2,256,512]{2,1,0:T(8,128)(2,1)S(1)}, u32[]{:S(2)}, u32[]{:S(2)}) %collective-permute-start.49) | collective-permute-done | bytes 524320 | tf_op jit(solution)/shard_map/ppermute | solution.py:729
  271.9 2.7 collective-permute-start.50
  280.8 10.9 %collective-permute-done.55.refs_3_ = bf16[2,256,512]{2,1,0:T(8,128)(2,1)S(1)} collective-permute-done((bf16[2,256,512]{2,1,0:T(8,128)(2,1)S(1)}, bf16[2,256,512]{2,1,0:T(8,128)(2,1)S(1)}, u32[]{:S(2)}, u32[]{:S(2)}) %collective-permute-start.55) | collective-permute-done | bytes 524320 | tf_op jit(solution)/shard_map/ppermute | solution.py:726
  291.7 7.0 %collective-permute-done.54.refs_2_ = bf16[2,256,512]{2,1,0:T(8,128)(2,1)S(1)} collective-permute-done((bf16[2,256,512]{2,1,0:T(8,128)(2,1)S(1)}, bf16[2,256,512]{2,1,0:T(8,128)(2,1)S(1)}, u32[]{:S(2)}, u32[]{:S(2)}) %collective-permute-start.54) | collective-permute-done | bytes 524320 | tf_op jit(solution)/shard_map/ppermute | solution.py:726
  305.8 4.8 %finish_experts.2 = (f32[1,512,2048]{2,1,0:T(8,128)}, f32[1,2048,512]{2,1,0:T(8,128)}) custom-call(s32[4]{0:T(128)} %pad_add_fusion.place, bf16[2,256,512]{2,1,0:T(8,128)(2,1)} %copy-done.6, bf16[2,256,512]{2,1,0:T(8,128)(2,1)} %copy-done.18, bf16[2,256,512]{2,1,0:T(8,128)(2,1)} %copy-done.17, bf16[2,256,512]{2,1,0:T(8,128)(2,1)} %copy-done.16), custom_call_target="tpu_custom_call" | custom-call | flops 4400000000 | bytes 6291456 | tf_op jit(solution)/shard_map/finish_experts/pallas_call | solution.py:646
  318.7 4.8 %finish_experts.3 = (f32[1,512,2048]{2,1,0:T(8,128)}, f32[1,2048,512]{2,1,0:T(8,128)}) custom-call(s32[4]{0:T(128)} %pad_add_fusion.place, bf16[2,256,512]{2,1,0:T(8,128)(2,1)} %copy-done.21, bf16[2,256,512]{2,1,0:T(8,128)(2,1)} %copy-done.22, bf16[2,256,512]{2,1,0:T(8,128)(2,1)} %copy-done.23, ...), custom_call_target="tpu_custom_call", output_to_operand_aliasing={{0}: (5, {}), {1}: (6, {})} | custom-call | flops 4400000000 | bytes 6291456 | tf_op jit(solution)/shard_map/finish_experts/pallas_call | solution.py:646
  (232 shorter events, 87.4 us)
Async XLA Ops:
  40.4 25.2 %collective-permute-start.17 = (bf16[2,256,512]{2,1,0:T(8,128)(2,1)}, bf16[2,256,512]{2,1,0:T(8,128)(2,1)S(1)}, u32[]{:S(2)}, u32[]{:S(2)}) collective-permute-start(bf16[2,256,512]{2,1,0:T(8,128)(2,1)} %cut_own.1), channel_id=1, source_target_pairs={{0,2},{1,3},{2,0},{3,1},{4,6},{5,7},{6,4},{7,5},{8,10},{9,11},{10,... | collective-permute-start | bytes 1572872 | tf_op jit(solution)/shard_map/ppermute | solution.py:729
  41.2 24.4 %collective-permute-start.15 = (bf16[2,256,512]{2,1,0:T(8,128)(2,1)S(1)}, bf16[2,256,512]{2,1,0:T(8,128)(2,1)S(1)}, u32[]{:S(2)}, u32[]{:S(2)}) collective-permute-start(bf16[2,256,512]{2,1,0:T(8,128)(2,1)S(1)} %pad_maximum_fusion.2.refs_0_), channel_id=1, source_target_pairs={{0,4},{4,0},{8,12},{12,8},{16,20},{20,16},{24,28},{28,24},{1,5},{5... | collective-permute-start | bytes 1572872 | tf_op jit(solution)/shard_map/ppermute | solution.py:726
  41.3 24.2 %collective-permute-start.13 = (bf16[2,256,512]{2,1,0:T(8,128)(2,1)S(1)}, bf16[2,256,512]{2,1,0:T(8,128)(2,1)}, u32[]{:S(2)}, u32[]{:S(2)}) collective-permute-start(bf16[2,256,512]{2,1,0:T(8,128)(2,1)S(1)} %pad_maximum_fusion.2.refs_0_), channel_id=1, source_target_pairs={{0,16},{4,20},{8,24},{12,28},{16,0},{20,4},{24,8},{28,12},{1,17},{... | collective-permute-start | bytes 1572872 | tf_op jit(solution)/shard_map/ppermute | solution.py:726
  42.9 22.7 %collective-permute-start.14 = (bf16[2,256,512]{2,1,0:T(8,128)(2,1)S(1)}, bf16[2,256,512]{2,1,0:T(8,128)(2,1)}, u32[]{:S(2)}, u32[]{:S(2)}) collective-permute-start(bf16[2,256,512]{2,1,0:T(8,128)(2,1)S(1)} %pad_maximum_fusion.3.refs_1_), channel_id=1, source_target_pairs={{0,8},{4,12},{8,0},{12,4},{16,24},{20,28},{24,16},{28,20},{1,9},{5... | collective-permute-start | bytes 1572872 | tf_op jit(solution)/shard_map/ppermute | solution.py:726
  65.6 23.7 %collective-permute-start.21 = (bf16[2,256,512]{2,1,0:T(8,128)(2,1)}, bf16[2,256,512]{2,1,0:T(8,128)(2,1)S(1)}, u32[]{:S(2)}, u32[]{:S(2)}) collective-permute-start(bf16[2,256,512]{2,1,0:T(8,128)(2,1)} %cut_own.1), channel_id=1, source_target_pairs={{0,3},{1,0},{2,1},{3,2},{4,7},{5,4},{6,5},{7,6},{8,11},{9,8},{10,9... | collective-permute-start | bytes 1572872 | tf_op jit(solution)/shard_map/ppermute | solution.py:729
  89.3 25.8 %collective-permute-start.25 = (bf16[2,2,2,256,512]{4,3,2,1,0:T(8,128)(2,1)}, bf16[2,2,2,256,512]{4,3,2,1,0:T(8,128)(2,1)}, u32[]{:S(2)}, u32[]{:S(2)}) collective-permute-start(bf16[2,2,2,256,512]{4,3,2,1,0:T(8,128)(2,1)} %get-tuple-element.215), channel_id=1, source_target_pairs={{0,4},{4,0},{8,12},{12,8},{16,20},{20,16},{24,28},{28,24},{1,5},{5... | collective-permute-start | bytes 6291464 | tf_op jit(solution)/shard_map/ppermute | solution.py:726
  89.4 24.3 %collective-permute-start.24 = (bf16[2,2,256,512]{3,2,1,0:T(8,128)(2,1)S(1)}, bf16[2,2,256,512]{3,2,1,0:T(8,128)(2,1)}, u32[]{:S(2)}, u32[]{:S(2)}) collective-permute-start(bf16[2,2,256,512]{3,2,1,0:T(8,128)(2,1)S(1)} %pad_maximum_fusion.refs_0_), channel_id=1, source_target_pairs={{0,4},{4,0},{8,12},{12,8},{16,20},{20,16},{24,28},{28,24},{1,5},{5... | collective-permute-start | bytes 3145736 | tf_op jit(solution)/shard_map/ppermute | solution.py:726
  89.9 25.2 %collective-permute-start.23 = (bf16[2,2,256,512]{3,2,1,0:T(8,128)(2,1)S(1)}, bf16[2,2,256,512]{3,2,1,0:T(8,128)(2,1)}, u32[]{:S(2)}, u32[]{:S(2)}) collective-permute-start(bf16[2,2,256,512]{3,2,1,0:T(8,128)(2,1)S(1)} %pad_maximum_fusion.refs_0_), channel_id=1, source_target_pairs={{0,16},{4,20},{8,24},{12,28},{16,0},{20,4},{24,8},{28,12},{1,17},{... | collective-permute-start | bytes 3145736 | tf_op jit(solution)/shard_map/ppermute | solution.py:726
  115.2 28.9 %collective-permute-start.28 = (bf16[2,2,256,512]{3,2,1,0:T(8,128)(2,1)}, bf16[2,2,256,512]{3,2,1,0:T(8,128)(2,1)}, u32[]{:S(2)}, u32[]{:S(2)}) collective-permute-start(bf16[2,2,256,512]{3,2,1,0:T(8,128)(2,1)} %pad_maximum_fusion.1.refs_0_), channel_id=1, source_target_pairs={{0,4},{4,0},{8,12},{12,8},{16,20},{20,16},{24,28},{28,24},{1,5},{5... | collective-permute-start | bytes 3145736 | tf_op jit(solution)/shard_map/ppermute | solution.py:726
  115.7 28.4 %collective-permute-start.27 = (bf16[2,2,256,512]{3,2,1,0:T(8,128)(2,1)}, bf16[2,2,256,512]{3,2,1,0:T(8,128)(2,1)}, u32[]{:S(2)}, u32[]{:S(2)}) collective-permute-start(bf16[2,2,256,512]{3,2,1,0:T(8,128)(2,1)} %pad_maximum_fusion.1.refs_0_), channel_id=1, source_target_pairs={{0,16},{4,20},{8,24},{12,28},{16,0},{20,4},{24,8},{28,12},{1,17},{... | collective-permute-start | bytes 3145736 | tf_op jit(solution)/shard_map/ppermute | solution.py:726
  116.8 27.3 %collective-permute-start.30 = (bf16[2,2,2,256,512]{4,3,2,1,0:T(8,128)(2,1)}, bf16[2,2,2,256,512]{4,3,2,1,0:T(8,128)(2,1)}, u32[]{:S(2)}, u32[]{:S(2)}) collective-permute-start(bf16[2,2,2,256,512]{4,3,2,1,0:T(8,128)(2,1)} %get-tuple-element.236), channel_id=1, source_target_pairs={{0,4},{4,0},{8,12},{12,8},{16,20},{20,16},{24,28},{28,24},{1,5},{5... | collective-permute-start | bytes 6291464 | tf_op jit(solution)/shard_map/ppermute | solution.py:726
  118.3 25.7 %collective-permute-start.29 = (bf16[2,2,256,512]{3,2,1,0:T(8,128)(2,1)S(1)}, bf16[2,2,256,512]{3,2,1,0:T(8,128)(2,1)}, u32[]{:S(2)}, u32[]{:S(2)}) collective-permute-start(bf16[2,2,256,512]{3,2,1,0:T(8,128)(2,1)S(1)} %fusion), channel_id=1, source_target_pairs={{0,8},{4,12},{8,0},{12,4},{16,24},{20,28},{24,16},{28,20},{1,9},{5... | collective-permute-start | bytes 3145736 | tf_op jit(solution)/shard_map/ppermute | solution.py:726
  148.3 27.3 %collective-permute-start.34 = (bf16[2,2,2,256,512]{4,3,2,1,0:T(8,128)(2,1)}, bf16[2,2,2,256,512]{4,3,2,1,0:T(8,128)(2,1)}, u32[]{:S(2)}, u32[]{:S(2)}) collective-permute-start(bf16[2,2,2,256,512]{4,3,2,1,0:T(8,128)(2,1)} %get-tuple-element.257), channel_id=1, source_target_pairs={{0,4},{4,0},{8,12},{12,8},{16,20},{20,16},{24,28},{28,24},{1,5},{5... | collective-permute-start | bytes 6291464 | tf_op jit(solution)/shard_map/ppermute | solution.py:726
  150.1 25.5 %collective-permute-start.33 = (bf16[2,2,256,512]{3,2,1,0:T(8,128)(2,1)S(1)}, bf16[2,2,256,512]{3,2,1,0:T(8,128)(2,1)}, u32[]{:S(2)}, u32[]{:S(2)}) collective-permute-start(bf16[2,2,256,512]{3,2,1,0:T(8,128)(2,1)S(1)} %fusion.1), channel_id=1, source_target_pairs={{0,8},{4,12},{8,0},{12,4},{16,24},{20,28},{24,16},{28,20},{1,9},{5... | collective-permute-start | bytes 3145736 | tf_op jit(solution)/shard_map/ppermute | solution.py:726
  178.0 28.3 %collective-permute-start.35 = (bf16[2,256,512]{2,1,0:T(8,128)(2,1)}, bf16[2,256,512]{2,1,0:T(8,128)(2,1)S(1)}, u32[]{:S(2)}, u32[]{:S(2)}) collective-permute-start(bf16[2,256,512]{2,1,0:T(8,128)(2,1)} %fusion.6), channel_id=1, source_target_pairs={{0,16},{4,20},{8,24},{12,28},{16,0},{20,4},{24,8},{28,12},{1,17},{... | collective-permute-start | bytes 1572872 | tf_op jit(solution)/shard_map/ppermute | solution.py:726
  181.9 24.4 %collective-permute-start.38 = (bf16[2,256,512]{2,1,0:T(8,128)(2,1)}, bf16[2,256,512]{2,1,0:T(8,128)(2,1)}, u32[]{:S(2)}, u32[]{:S(2)}) collective-permute-start(bf16[2,256,512]{2,1,0:T(8,128)(2,1)} %get-tuple-element.346), channel_id=1, source_target_pairs={{0,24},{4,28},{8,16},{12,20},{16,8},{20,12},{24,0},{28,4},{1,25},{... | collective-permute-start | bytes 1572872 | tf_op jit(solution)/shard_map/ppermute | solution.py:726
  182.8 31.3 %collective-permute-start.37 = (bf16[2,256,512]{2,1,0:T(8,128)(2,1)}, bf16[2,256,512]{2,1,0:T(8,128)(2,1)}, u32[]{:S(2)}, u32[]{:S(2)}) collective-permute-start(bf16[2,256,512]{2,1,0:T(8,128)(2,1)} %get-tuple-element.347), channel_id=1, source_target_pairs={{0,16},{4,20},{8,24},{12,28},{16,0},{20,4},{24,8},{28,12},{1,17},{... | collective-permute-start | bytes 1572872 | tf_op jit(solution)/shard_map/ppermute | solution.py:726
  184.3 29.8 %collective-permute-start.36 = (bf16[2,256,512]{2,1,0:T(8,128)(2,1)}, bf16[2,256,512]{2,1,0:T(8,128)(2,1)}, u32[]{:S(2)}, u32[]{:S(2)}) collective-permute-start(bf16[2,256,512]{2,1,0:T(8,128)(2,1)} %get-tuple-element.348), channel_id=1, source_target_pairs={{0,8},{4,12},{8,0},{12,4},{16,24},{20,28},{24,16},{28,20},{1,9},{5... | collective-permute-start | bytes 1572872 | tf_op jit(solution)/shard_map/ppermute | solution.py:726
  185.4 28.8 %collective-permute-start.39 = (bf16[2,2,2,256,512]{4,3,2,1,0:T(8,128)(2,1)}, bf16[2,2,2,256,512]{4,3,2,1,0:T(8,128)(2,1)}, u32[]{:S(2)}, u32[]{:S(2)}) collective-permute-start(bf16[2,2,2,256,512]{4,3,2,1,0:T(8,128)(2,1)} %get-tuple-element.297), channel_id=1, source_target_pairs={{0,4},{4,0},{8,12},{12,8},{16,20},{20,16},{24,28},{28,24},{1,5},{5... | collective-permute-start | bytes 6291464 | tf_op jit(solution)/shard_map/ppermute | solution.py:726
  217.1 34.6 %collective-permute-start.44 = (bf16[2,256,512]{2,1,0:T(8,128)(2,1)}, bf16[2,256,512]{2,1,0:T(8,128)(2,1)S(1)}, u32[]{:S(2)}, u32[]{:S(2)}) collective-permute-start(bf16[2,256,512]{2,1,0:T(8,128)(2,1)} %fusion.13), channel_id=1, source_target_pairs={{0,2},{1,3},{2,0},{3,1},{4,6},{5,7},{6,4},{7,5},{8,10},{9,11},{10,... | collective-permute-start | bytes 1572872 | tf_op jit(solution)/shard_map/ppermute | solution.py:729
  219.5 32.1 %collective-permute-start.43 = (bf16[2,256,512]{2,1,0:T(8,128)(2,1)}, bf16[2,256,512]{2,1,0:T(8,128)(2,1)S(1)}, u32[]{:S(2)}, u32[]{:S(2)}) collective-permute-start(bf16[2,256,512]{2,1,0:T(8,128)(2,1)} %fusion.3), channel_id=1, source_target_pairs={{0,3},{1,0},{2,1},{3,2},{4,7},{5,4},{6,5},{7,6},{8,11},{9,8},{10,9... | collective-permute-start | bytes 1572872 | tf_op jit(solution)/shard_map/ppermute | solution.py:729
  224.4 27.3 %collective-permute-start.42 = (bf16[2,256,512]{2,1,0:T(8,128)(2,1)}, bf16[2,256,512]{2,1,0:T(8,128)(2,1)}, u32[]{:S(2)}, u32[]{:S(2)}) collective-permute-start(bf16[2,256,512]{2,1,0:T(8,128)(2,1)} %get-tuple-element.343), channel_id=1, source_target_pairs={{0,24},{4,28},{8,16},{12,20},{16,8},{20,12},{24,0},{28,4},{1,25},{... | collective-permute-start | bytes 1572872 | tf_op jit(solution)/shard_map/ppermute | solution.py:726
  225.8 25.8 %collective-permute-start.41 = (bf16[2,256,512]{2,1,0:T(8,128)(2,1)}, bf16[2,256,512]{2,1,0:T(8,128)(2,1)}, u32[]{:S(2)}, u32[]{:S(2)}) collective-permute-start(bf16[2,256,512]{2,1,0:T(8,128)(2,1)} %get-tuple-element.344), channel_id=1, source_target_pairs={{0,16},{4,20},{8,24},{12,28},{16,0},{20,4},{24,8},{28,12},{1,17},{... | collective-permute-start | bytes 1572872 | tf_op jit(solution)/shard_map/ppermute | solution.py:726
  226.4 25.3 %collective-permute-start.40 = (bf16[2,256,512]{2,1,0:T(8,128)(2,1)}, bf16[2,256,512]{2,1,0:T(8,128)(2,1)}, u32[]{:S(2)}, u32[]{:S(2)}) collective-permute-start(bf16[2,256,512]{2,1,0:T(8,128)(2,1)} %get-tuple-element.345), channel_id=1, source_target_pairs={{0,8},{4,12},{8,0},{12,4},{16,24},{20,28},{24,16},{28,20},{1,9},{5... | collective-permute-start | bytes 1572872 | tf_op jit(solution)/shard_map/ppermute | solution.py:726
  (83 other events, 886.0 us)

commit v3 on v2

--- a/solution.py
+++ b/solution.py
@@ -59,7 +59,7 @@
     return v * phi, phi + v * density
 
 
-def params(megabytes=60):
+def params(megabytes=62):
     return pltpu.CompilerParams(vmem_limit_bytes=megabytes * MIB)
 
 
@@ -72,7 +72,7 @@
 
 
 def pack_kernel(place, qkv, proj, router, *refs):
-    *vectors, out, lines, turned = refs
+    *vectors, out, table, lines, turned = refs
     depth = out.shape[0]
     row = pl.multiple_of(place[1] * depth, depth)
     width = qkv.shape[1] + proj.shape[1]
@@ -90,6 +90,9 @@
     out[:, : qkv.shape[1]] = qkv[pl.ds(row, depth), :]
     out[:, qkv.shape[1] : width] = proj[pl.ds(row, depth), :]
     out[:, width:] = turned[pl.ds(row, depth), :].astype(BF16)
+    table[:, : qkv.shape[1]] = qkv[...]
+    table[:, qkv.shape[1] : width] = proj[...]
+    table[:, width:] = turned[...].astype(BF16)
 
 
 def pack_call(place, qkv, proj, router, vectors):
@@ -97,9 +100,11 @@
     vmem = pl.BlockSpec(memory_space=pltpu.VMEM)
     return pl.pallas_call(
         pack_kernel,
-        out_shape=jax.ShapeDtypeStruct((shard // PIECES, qkv.shape[1] + proj.shape[1] + SMALL), BF16),
+        out_shape=tuple(
+            jax.ShapeDtypeStruct((rows, qkv.shape[1] + proj.shape[1] + SMALL), BF16) for rows in (shard // PIECES, shard)
+        ),
         in_specs=[pl.BlockSpec(memory_space=pltpu.SMEM)] + [vmem] * (3 + len(vectors)),
-        out_specs=vmem,
+        out_specs=(vmem, vmem),
         scratch_shapes=[pltpu.VMEM((SMALL, shard), F32), pltpu.VMEM((shard, SMALL), F32)],
         cost_estimate=cost(2, 1),
         name="pack_dense",
@@ -136,20 +141,22 @@
     place, images, cot, *refs,
 ):
     dense = refs[:PIECES]
-    qkv_out, att_out, res_out, lse_out, tok_out, gates_out, full_out, small_out, rows = refs[PIECES:]
+    own, qkv_out, att_out, res_out, lse_out, tok_out, gates_out, full_out, small_out, rows = refs[PIECES:]
     model = images.shape[2]
     length = images.shape[1]
     size = rows.shape[0]
-    parts, depth = dense[0].shape[:2]
+    parts = dense[0].shape[0] + 1
+    depth = dense[0].shape[1]
 
     @pl.when(pl.program_id(0) == 0)
     def _():
         z, r = place[0], place[1]
         for pos in range(PIECES):
-            for d in range(parts):
+            for d in range(1, parts):
                 owner = lax.rem(z + parts - d, parts) * PIECES
                 row = pl.multiple_of((owner + jnp.bitwise_xor(r, offset_of(pos))) * depth, depth)
-                full_out[pl.ds(row, depth), :] = dense[pos][d]
+                full_out[pl.ds(row, depth), :] = dense[pos][d - 1]
+        full_out[pl.ds(pl.multiple_of(z * PIECES * depth, depth), PIECES * depth), :] = own[...]
         small_out[...] = full_out[:, 4 * model :].astype(F32).T
         rows[...] = jnp.zeros_like(rows)
 
@@ -219,7 +226,7 @@
     return pl.BlockSpec((1,) + dims, lambda i, *_: (i, 0, 0))
 
 
-def forward_call(place, images, cot, dense):
+def forward_call(place, images, cot, dense, own):
     count, length, model = images.shape
     size = padded(length)
     outs = (
@@ -238,7 +245,7 @@
         grid_spec=pltpu.PrefetchScalarGridSpec(
             num_scalar_prefetch=1,
             grid=(count,),
-            in_specs=[image(length, model), image(length, model)] + [whole(d) for d in dense],
+            in_specs=[image(length, model), image(length, model)] + [whole(d) for d in (*dense, own)],
             out_specs=[
                 image(size, 3 * model), image(size, model), image(size, model), image(size, 128),
                 pl.BlockSpec((PAD, 2 * model), lambda i, *_: (i, 0)),
@@ -249,7 +256,102 @@
         compiler_params=params(),
         cost_estimate=cost(12, 12),
         name="attention_forward",
-    )(place, images, cot, *dense)
+    )(place, images, cot, *dense, own)
+
+
+def blend_loads(jobs, arrays, loaded, sems):
+    copies = []
+    for _, terms in jobs:
+        for which, index in terms:
+            spot = len(copies)
+            source = arrays[which].at[index] if index else arrays[which]
+            copies.append(pltpu.make_async_copy(source, loaded.at[spot], sems.at[spot]))
+    return copies
+
+
+def blend_stores(jobs, outs, loaded, summed, sems):
+    copies, spot, sums = [], 0, 0
+    for out, (kind, terms) in zip(outs, jobs):
+        if kind == "collect":
+            pairs = [(loaded.at[spot + k], out.at[k]) for k in range(len(terms))]
+        else:
+            pairs = [(summed.at[sums], out)]
+            sums += 1
+        spot += len(terms)
+        copies.append([pltpu.make_async_copy(a, b, sems.at[sum(map(len, copies)) + k]) for k, (a, b) in enumerate(pairs)])
+    return copies
+
+
+def blend_work(jobs, loads, stores, loaded, summed):
+    spot = sums = 0
+    for (kind, terms), copies in zip(jobs, stores):
+        total = None
+        for k in range(len(terms)):
+            loads[spot].wait()
+            if kind == "collect":
+                copies[k].start()
+            else:
+                value = loaded[spot].astype(F32)
+                total = value if total is None else total + value
+            spot += 1
+        if kind == "sum":
+            summed[sums] = total.astype(BF16)
+            copies[0].start()
+            sums += 1
+
+
+def blend_kernel(*refs, jobs, count_in):
+    arrays = refs[:count_in]
+    outs = refs[count_in : count_in + len(jobs)]
+    loaded, summed, in_sems, out_sems = refs[count_in + len(jobs) :]
+    loads = blend_loads(jobs, arrays, loaded, in_sems)
+    for copy in loads:
+        copy.start()
+    stores = blend_stores(jobs, outs, loaded, summed, out_sems)
+    blend_work(jobs, loads, stores, loaded, summed)
+    for copies in stores:
+        for copy in copies:
+            copy.wait()
+
+
+def blend_plan(jobs):
+    arrays, plan, shapes = [], [], []
+    for kind, terms in jobs:
+        listed = []
+        for array, index in terms:
+            known = [k for k, a in enumerate(arrays) if a is array]
+            if not known:
+                arrays.append(array)
+                known = [len(arrays) - 1]
+            listed.append((known[0], index))
+        unit = terms[0][0].shape[len(terms[0][1]) :]
+        shapes.append(jax.ShapeDtypeStruct(((len(terms),) if kind == "collect" else ()) + unit, BF16))
+        plan.append((kind, tuple(listed)))
+    units = sum(len(terms) for _, terms in plan)
+    sums = sum(kind == "sum" for kind, _ in plan)
+    stores = sums + sum(len(terms) for kind, terms in plan if kind == "collect")
+    scratch = [
+        pltpu.VMEM((units,) + unit, BF16),
+        pltpu.VMEM((max(sums, 1),) + unit, BF16),
+        pltpu.SemaphoreType.DMA((units,)),
+        pltpu.SemaphoreType.DMA((stores,)),
+    ]
+    return arrays, tuple(plan), shapes, scratch
+
+
+def blend_call(*jobs):
+    arrays, plan, shapes, scratch = blend_plan(jobs)
+    anywhere = pl.BlockSpec(memory_space=pl.ANY)
+    return pl.pallas_call(
+        functools.partial(blend_kernel, jobs=plan, count_in=len(arrays)),
+        out_shape=tuple(shapes),
+        in_specs=[anywhere] * len(arrays),
+        out_specs=(anywhere,) * len(shapes),
+        scratch_shapes=scratch,
+        compiler_params=params(),
+        cost_estimate=cost(3, 3),
+        name="blend",
+    )(*arrays)
 
 
 def expert_kernel(place, slots, gates, small, tok, *refs, turn, sources, count_in):
@@ -395,14 +497,26 @@
     )
 
 
-def combine_kernel(place, *refs, turns, lo, carried, last):
+def combine_kernel(place, *refs, turns, jobs, count_in):
     cot, att, res, tok, slots, full, small = refs[:7]
     pairs = refs[7 : 7 + turns]
     biases = refs[7 + turns : 7 + 2 * turns]
-    before = refs[7 + 2 * turns : 7 + 2 * turns + 6 * carried]
-    *outs, cots = refs[7 + 2 * turns + 6 * carried :]
-    block_out, gres_out, gatt_out, acc_proj, acc_router, acc_small = outs[:6]
+    arrays = refs[7 + 2 * turns : 7 + 2 * turns + count_in]
+    block_out, gres_out, gatt_out, late_out, *side_outs = refs[7 + 2 * turns + count_in : -8]
+    cots, acc_proj, acc_router, acc_small, loaded, summed, in_sems, out_sems = refs[-8:]
     b = pl.program_id(0)
+    loads = blend_loads(jobs, arrays, loaded, in_sems)
+    stores = blend_stores(jobs, side_outs, loaded, summed, out_sems)
+
+    @pl.when(b == 0)
+    def _():
+        for copy in loads:
+            copy.start()
+
+    @pl.when(b == 1)
+    def _():
+        blend_work(jobs, loads, stores, loaded, summed)
+
     length, model = cot.shape[1:]
     size = cots.shape[0]
     parts = turns
@@ -410,8 +524,8 @@
     @pl.when(b == 0)
     def _():
         cots[...] = jnp.zeros_like(cots)
-        for k, acc in enumerate((acc_proj, acc_router, acc_small)):
-            acc[...] = before[3 + k][...] if carried else jnp.zeros_like(acc)
+        for acc in (acc_proj, acc_router, acc_small):
+            acc[...] = jnp.zeros_like(acc)
 
     def vector(row):
         return small[row : row + 1, :]
@@ -419,7 +533,7 @@
     def add_row(row, values):
         acc_small[row : row + 1, :] += jnp.sum(values, axis=0, keepdims=True)
 
-    live = (lo + b < place[2]).astype(F32)
+    live = (b < place[2]).astype(F32)
     cots[:length, :] = cot[0].astype(F32) * live
     grad_out = cots[...]
     residual = res[0]
@@ -462,12 +576,11 @@
     acc_proj[...] += dot_tn(att[0], branch)
     gatt_out[0] = dot_nt(branch, full[:, 3 * model : 4 * model]).astype(BF16)
 
-    if not last:
-        return
-
     @pl.when(b == pl.num_programs(0) - 1)
     def _():
-        late_out = outs[-1]
+        for copies in stores:
+            for copy in copies:
+                copy.wait()
         for j in range(turns):
             expert = lax.rem(place[0] + parts - j, parts)
             acc_small[12:32, pl.ds(pl.multiple_of(expert * 128, 128), 128)] = biases[j][0:20, :]
@@ -475,51 +588,47 @@
         late_out[:, model:] = (acc_router[...] + acc_small[...].T).astype(BF16)
 
 
-def part_of(lo, *dims):
-    return pl.BlockSpec((1,) + dims, lambda i, *_: (lo + i, 0, 0))
-
-
-def combine_call(lo, hi, before, place, cot, att, res, tok, slots, full, small, pairs, biases):
+def combine_call(jobs, place, cot, att, res, tok, slots, full, small, pairs, biases):
     count, length, model = cot.shape
     size = att.shape[1]
     turns = len(pairs)
-    last = hi == count
+    arrays, plan, shapes, scratch = blend_plan(jobs)
+    anywhere = pl.BlockSpec(memory_space=pl.ANY)
     outs = (
         jax.ShapeDtypeStruct((count, length, model), BF16),
         jax.ShapeDtypeStruct((count, size, model), F32),
         jax.ShapeDtypeStruct((count, size, model), BF16),
-        jax.ShapeDtypeStruct((model, model), F32),
-        jax.ShapeDtypeStruct((model, SMALL), F32),
-        jax.ShapeDtypeStruct((SMALL, model), F32),
-    ) + ((jax.ShapeDtypeStruct((model, model + SMALL), BF16),) if last else ())
-    image = functools.partial(part_of, lo)
-    inputs = (cot, att, res, tok, slots, full, small, *pairs, *biases)
+        jax.ShapeDtypeStruct((model, model + SMALL), BF16),
+    )
     return pl.pallas_call(
-        functools.partial(combine_kernel, turns=turns, lo=lo, carried=len(before) > 0, last=last),
-        out_shape=outs,
+        functools.partial(combine_kernel, turns=turns, jobs=plan, count_in=len(arrays)),
+        out_shape=outs + tuple(shapes),
         grid_spec=pltpu.PrefetchScalarGridSpec(
             num_scalar_prefetch=1,
-            grid=(hi - lo,),
+            grid=(count,),
             in_specs=[
                 image(length, model), image(size, model), image(size, model),
-                pl.BlockSpec((PAD, 2 * model), lambda i, *_: (lo + i, 0)),
-                image(size, slots.shape[2]),
-            ] + [whole(a) for a in inputs[5:]] + [pl.BlockSpec(memory_space=pl.ANY)] * min(3, len(before))
-            + [whole(a) for a in before[3:]],
-            out_specs=[image(length, model), image(size, model), image(size, model)] + [whole(o) for o in outs[3:]],
-            scratch_shapes=[pltpu.VMEM((size, model), F32)],
+                pl.BlockSpec((PAD, 2 * model), lambda i, *_: (i, 0)),
+                image(size, slots.shape[2]), whole(full), whole(small),
+            ] + [whole(a) for a in (*pairs, *biases)] + [anywhere] * len(arrays),
+            out_specs=[image(length, model), image(size, model), image(size, model), whole(outs[3])] + [anywhere] * len(shapes),
+            scratch_shapes=[
+                pltpu.VMEM((size, model), F32),
+                pltpu.VMEM((model, model), F32),
+                pltpu.VMEM((model, SMALL), F32),
+                pltpu.VMEM((SMALL, model), F32),
+            ] + scratch,
         ),
-        input_output_aliases={1 + len(inputs) + k: k for k in range(len(before))},
         compiler_params=params(),
-        cost_estimate=cost(4 * (hi - lo), 14),
+        cost_estimate=cost(18, 14),
         name="combine",
-    )(place, *inputs, *before)
-
-
-def backward_kernel(place, images, qkv, lse, gres, gatt, full, small, late, *refs, parts, carried, last):
-    before = refs[: 3 * carried]
-    *outs, rows = refs[3 * carried :]
-    input_grad, acc_qkv, acc_small = outs[:3]
+    )(place, cot, att, res, tok, slots, full, small, *pairs, *biases, *arrays)
+
+
+def backward_kernel(
+    place, images, qkv, lse, gres, gatt, full, small, late, input_grad, keep, send, rows, acc_qkv, acc_small,
+):
+    parts = keep.shape[1]
     b = pl.program_id(0)
     length, model = images.shape[1:]
     size = rows.shape[0]
@@ -527,8 +636,8 @@
     @pl.when(b == 0)
     def _():
         rows[...] = jnp.zeros_like(rows)
-        for k, acc in enumerate((acc_qkv, acc_small)):
-            acc[...] = before[1 + k][...] if carried else jnp.zeros_like(acc)
+        acc_qkv[...] = jnp.zeros_like(acc_qkv)
+        acc_small[...] = jnp.zeros_like(acc_small)
 
     def vector(row):
         return small[row : row + 1, :]
@@ -569,12 +678,8 @@
     add_row(33, grad_projected[:, 2 * model :].astype(F32))
     input_grad[0] = (gres[0] + norm_back(grad_normed * vector(4), xhat1, rstd1))[:length]
 
-    if not last:
-        return
-
     @pl.when(b == pl.num_programs(0) - 1)
     def _():
-        keep, send = outs[-2:]
         for part in range(parts):
             for k in range(2):
                 start = (part * 2 + k) * 128
@@ -596,69 +701,75 @@
                 out[spot, d, :, 4 * model :] = acc_qkv[pl.ds(row, depth), 3 * model :].astype(BF16)
 
 
-def backward_call(lo, hi, before, place, images, qkv, lse, gres, gatt, full, small, late, turns):
+def backward_call(place, images, qkv, lse, gres, gatt, full, small, late, parts):
     count, length, model = images.shape
     size = qkv.shape[1]
-    depth = model // (turns * PIECES)
-    last = hi == count
-    half = jax.ShapeDtypeStruct((PIECES // 2, turns, depth, 4 * model + SMALL), BF16)
-    outs = (
-        jax.ShapeDtypeStruct((count, length, model), F32),
-        jax.ShapeDtypeStruct((model, 3 * model + SMALL), F32),
-        jax.ShapeDtypeStruct((SMALL, model), F32),
-    ) + ((half, half) if last else ())
-    image = functools.partial(part_of, lo)
-    inputs = (images, qkv, lse, gres, gatt, full, small, late)
+    half = jax.ShapeDtypeStruct((PIECES // 2, parts, model // (parts * PIECES), 4 * model + SMALL), BF16)
+    outs = (jax.ShapeDtypeStruct((count, length, model), F32), half, half)
     return pl.pallas_call(
-        functools.partial(backward_kernel, parts=turns, carried=len(before) > 0, last=last),
+        backward_kernel,
         out_shape=outs,
         grid_spec=pltpu.PrefetchScalarGridSpec(
             num_scalar_prefetch=1,
-            grid=(hi - lo,),
+            grid=(count,),
             in_specs=[
                 image(length, model), image(size, 3 * model), image(size, 128), image(size, model),
                 image(size, model), whole(full), whole(small), whole(late),
-            ] + [pl.BlockSpec(memory_space=pl.ANY)] * min(1, len(before)) + [whole(a) for a in before[1:]],
-            out_specs=[image(length, model)] + [whole(o) for o in outs[1:]],
-            scratch_shapes=[pltpu.VMEM((size, model), F32)],
+            ],
+            out_specs=[image(length, model), whole(half), whole(half)],
+            scratch_shapes=[
+                pltpu.VMEM((size, model), F32),
+                pltpu.VMEM((model, 3 * model + SMALL), F32),
+                pltpu.VMEM((SMALL, model), F32),
+            ],
         ),
-        input_output_aliases={1 + len(inputs) + k: k for k in range(len(before))},
         compiler_params=params(),
-        cost_estimate=cost(4 * (hi - lo), 14),
+        cost_estimate=cost(22, 14),
         name="attention_backward",
-    )(place, *inputs, *before)
-
-
-def finish_kernel(place, *refs):
+    )(place, images, qkv, lse, gres, gatt, full, small, late)
+
+
+def finish_kernel(place, *refs, half):
     pieces = refs[: PIECES // 2]
-    inner_out, outer_out = refs[-2:]
-    for k, piece in enumerate(pieces):
-
-        @pl.when(pl.program_id(0) == k)
-        def _():
-            inner_out[0] = piece[0].astype(F32).T
-            outer_out[0] = piece[1].astype(F32)
+    inner_out, outer_out, loaded, inner, outer, in_sems, out_sems = refs[-7:]
+    block = outer.shape[1]
+    loads = [pltpu.make_async_copy(p, loaded.at[k], in_sems.at[k]) for k, p in enumerate(pieces)]
+    for copy in loads:
+        copy.start()
+    stores = []
+    for k, copy in enumerate(loads):
+        copy.wait()
+        piece = jnp.bitwise_xor(place[1], offset_of(k + half * PIECES // 2))
+        spot = pl.ds(pl.multiple_of(piece * block, block), block)
+        inner[k] = loaded[k, 0].astype(F32).T
+        outer[k] = loaded[k, 1].astype(F32)
+        for side, (source, target) in enumerate(((inner.at[k], inner_out.at[0, :, spot]), (outer.at[k], outer_out.at[0, spot]))):
+            stores.append(pltpu.make_async_copy(source, target, out_sems.at[k, side]))
+            stores[-1].start()
+    for copy in stores:
+        copy.wait()
 
 
 def finish_call(half, place, pieces, outs=()):
     _, block, model = pieces[0].shape
-    piece = lambda i, s: jnp.bitwise_xor(s[1], offset_of(i + 4 * half))
+    count = len(pieces)
+    anywhere = pl.BlockSpec(memory_space=pl.ANY)
     return pl.pallas_call(
-        finish_kernel,
+        functools.partial(finish_kernel, half=half),
         out_shape=(
             jax.ShapeDtypeStruct((1, model, PIECES * block), F32),
             jax.ShapeDtypeStruct((1, PIECES * block, model), F32),
         ),
-        grid_spec=pltpu.PrefetchScalarGridSpec(
-            num_scalar_prefetch=1,
-            grid=(PIECES // 2,),
-            in_specs=[whole(p) for p in pieces] + [pl.BlockSpec(memory_space=pl.ANY)] * len(outs),
-            out_specs=[
-                pl.BlockSpec((1, model, block), lambda i, s: (0, 0, piece(i, s))),
-                pl.BlockSpec((1, block, model), lambda i, s: (0, piece(i, s), 0)),
-            ],
-        ),
-        input_output_aliases={1 + len(pieces) + k: k for k in range(len(outs))},
+        in_specs=[pl.BlockSpec(memory_space=pltpu.SMEM)] + [anywhere] * (count + len(outs)),
+        out_specs=(anywhere, anywhere),
+        scratch_shapes=[
+            pltpu.VMEM((count, 2, block, model), BF16),
+            pltpu.VMEM((count, model, block), F32),
+            pltpu.VMEM((count, block, model), F32),
+            pltpu.SemaphoreType.DMA((count,)),
+            pltpu.SemaphoreType.DMA((count, 2)),
+        ],
+        input_output_aliases={1 + count + k: k for k in range(len(outs))},
         compiler_params=params(),
         cost_estimate=cost(4, 6),
         name="finish_experts",
@@ -666,19 +777,22 @@
 
 
 def finish_dense_kernel(place, *refs):
-    pieces = refs[:PIECES]
-    qkv_out, proj_out, router_out, inner_out, outer_out, rest_out, table = refs[PIECES:]
+    pieces = refs[:2]
+    qkv_out, proj_out, router_out, inner_out, outer_out, *vector_outs, pair_out, table = refs[2:]
     model = proj_out.shape[1]
-    depth = pieces[0].shape[0]
+    depth = pieces[0].shape[1]
     for pos in range(PIECES):
         row = pl.multiple_of(jnp.bitwise_xor(place[1], offset_of(pos)) * depth, depth)
-        block = pieces[pos][...].astype(F32)
+        block = pieces[pos // (PIECES // 2)][pos % (PIECES // 2)].astype(F32)
         qkv_out[pl.ds(row, depth), :] = block[:, : 3 * model]
         proj_out[pl.ds(row, depth), :] = block[:, 3 * model : 4 * model]
         table[pl.ds(row, depth), :] = block[:, 4 * model :]
     table[...] = table[...].T
     router_out[...] = table[: router_out.shape[0], :]
-    rest_out[...] = table[4 : 4 + rest_out.shape[0], :]
+    for k, out in enumerate(vector_outs):
+        out[...] = table[4 + k, :]
+    for k in range(2):
+        pair_out[pl.ds(k * 128, 128)] = table[9 + k, :]
     for c in range(inner_out.shape[1] // 128):
         inner_out[:, c * 128 : (c + 1) * 128] = table[12 + c : 13 + c, :]
     for c in range(outer_out.shape[1] // 128):
@@ -686,7 +800,7 @@
 
 
 def finish_dense_call(place, pieces, model, parts, hidden):
-    rows = pieces[0].shape[0] * PIECES
+    rows = pieces[0].shape[1] * PIECES
     vmem = pl.BlockSpec(memory_space=pltpu.VMEM)
     return pl.pallas_call(
         finish_dense_kernel,
@@ -696,9 +810,9 @@
             jax.ShapeDtypeStruct((parts, rows), F32),
             jax.ShapeDtypeStruct((1, hidden), F32),
             jax.ShapeDtypeStruct((1, model), F32),
-            jax.ShapeDtypeStruct((8, rows), F32),
-        ),
-        in_specs=[pl.BlockSpec(memory_space=pltpu.SMEM)] + [vmem] * PIECES,
+        )
+        + tuple(jax.ShapeDtypeStruct((n,), F32) for n in (rows, rows, rows, rows, rows, 2 * rows)),
+        in_specs=[pl.BlockSpec(memory_space=pltpu.SMEM)] + [vmem] * 2,
         scratch_shapes=[pltpu.VMEM((rows, SMALL), F32)],
         cost_estimate=cost(2, 2),
         name="finish_dense",
@@ -747,13 +861,15 @@
     shifts = list(range(1, n_group))
 
     vectors = (attn_norm_gain, attn_norm_bias, proj_bias, moe_norm_gain, moe_norm_bias, query_value_bias)
-    mine = pack_call(place, qkv_weight, proj_weight, router_weight, vectors + (expert_inner_bias, expert_outer_bias))
+    mine, own_table = pack_call(
+        place, qkv_weight, proj_weight, router_weight, vectors + (expert_inner_bias, expert_outer_bias)
+    )
     dense_z = {d: along(mine, d) for d in shifts}
 
     piece = cut_call(place, expert_inner, expert_outer)
     piece, dense_z = join(piece, dense_z)
     expert_z = {1: along(piece, 1)}
-    dense = spread(jnp.stack([mine] + [dense_z[d] for d in range(1, n_group)]))
+    dense = spread(jnp.stack([dense_z[d] for d in shifts]))
     dense = dense + [across(v, 1) for v in dense]
 
     experts = (z + n_group - jnp.arange(n_group, dtype=jnp.int32)) % n_group
@@ -764,129 +880,104 @@
         seats.transpose(0, 2, 1), ((0, 0), (0, size - length), (0, 8 - n_group)), constant_values=-1
     )
 
-    def first_stage(k, got):
-        if k == 1:
-            return both(got[0][None], 2), both(got[1][None], 4)
-        return (both(got[None], 2),)
-
-    def second_stage(k, arrays):
-        if k == 1:
-            return across(arrays[0], 4), across(arrays[1], 2)
-        return (across(arrays[0], 4),)
-
-    def third_stage(arrays):
-        return tuple(across(a, 1) for a in arrays)
+    def collected(pieces):
+        return ("collect", [(p, ()) for p in pieces])
 
     def sources(pos, side):
-        return pos // 2, (pos % 2, side)
-
-    def sources_first(pos, side):
-        x, y, core = pos & 1, pos >> 1 & 1, pos >> 2
-        other, at = (x, y) if side else (y, x)
-        return 4 * core + 2 * other + side, at
-
-    outs, folds, shards = {}, {}, {}
-
-    at_once = (2, 3)
-
-    def fold_core(k):
-        folds[k] = (outs[k][0], across(outs[k][1], 1))
-
-    def fold_one(k):
-        keep, core = folds[k]
-        if k in at_once:
-            quarters = [plus(keep[x, y], core[x, y]) for x, y in ((1, 0), (0, 1), (1, 1))]
-            folds[k] = (keep, core) + tuple(across(q, bits) for q, bits in zip(quarters, (2, 4, 6)))
-        else:
-            folds[k] = (keep, core, across(plus(keep[1], core[1]), 2))
-
-    def fold_two(k):
-        keep, core, x = folds[k]
-        folds[k] = (keep, core, x, across(plus(keep[0, 1], core[0, 1], x[1]), 4))
-
-    def fold_z(k):
-        keep, core, *got = folds[k]
-        if k not in at_once:
-            got[0] = got[0][0]
-        value = rest_of_replicas(plus(keep[0, 0], core[0, 0], *got))
-        shards[k] = along(value, -k) if k else value
-
-    one, two, cores = {}, {}, {}
-    one[1] = first_stage(1, expert_z[1])
+        return pos // (PIECES // 2), (pos % (PIECES // 2), side)
+
+    outs, cores, chips, shards = {}, {}, {}, {}
+    places = ((1, 0), (0, 1), (1, 1))
+
+    def quarters(k):
+        return [("sum", [(outs[k][0], at), (cores[k], at)]) for at in places]
+
+    def own_quarter(k):
+        return ("sum", [(outs[k][0], (0, 0)), (cores[k], (0, 0))] + [(v, ()) for v in chips[k]])
+
+    def send_chips(values):
+        return [across(v, offset_of(pos)) for pos, v in zip(range(1, PIECES // 2), values)]
+
+    def send_shard(k, value):
+        value = rest_of_replicas(value)
+        return along(value, -k) if k else value
+
+    spread_1 = spread(expert_z[1])
     piece, expert_z[1] = join(piece, expert_z[1])
     expert_z[2] = along(piece, 2)
-    one[1], images, dense = join(one[1], images, dense)
-    two[1] = second_stage(1, one[1])
-    cores[1] = third_stage(one[1])
-    qkv, att, res, lse, tok, gates, full, small = forward_call(place, images, cotangent, dense)
-    tok, gates, small, piece, one, two, cores, expert_z = join(tok, gates, small, piece, one, two, cores, expert_z)
+    qkv, att, res, lse, tok, gates, full, small = forward_call(place, images, cotangent, dense, own_table)
+    tok, gates, small, piece, spread_1, expert_z = join(tok, gates, small, piece, spread_1, expert_z)
     tables = (slots_lane, gates, small)
 
-    weights = one[1] + two[1] + cores[1] + third_stage(two[1])
-    one[2] = first_stage(2, expert_z[2])
+    half, = blend_call(collected(spread_1))
+    weights = (half, across(half, 1))
+    spread_2 = spread(expert_z[2])
     expert_z[3] = along(piece, 3)
     outs[0] = expert_call(0, place, tok, *tables, ((expert_inner, expert_outer), None))
-    outs, tok, weights, one, expert_z = join(outs, tok, weights, one, expert_z)
-
-    two[2] = second_stage(2, one[2])
-    cores[2] = third_stage(one[2])
-    one[3] = first_stage(3, expert_z[3])
-    fold_core(0)
-    outs[1] = expert_call(1, place, tok, *tables, (weights, sources_first))
-    outs, tok, one, two, cores, folds = join(outs, tok, one, two, cores, folds)
-
-    weights = one[2] + two[2] + cores[2] + third_stage(two[2])
-    two[3] = second_stage(3, one[3])
-    cores[3] = third_stage(one[3])
-    fold_one(0)
-    fold_core(1)
-    outs[2] = expert_call(2, place, tok, *tables, (weights, sources))
-    outs, tok, one, two, cores, folds = join(outs, tok, one, two, cores, folds)
-
-    weights = one[3] + two[3] + cores[3] + third_stage(two[3])
-    fold_two(0)
-    fold_one(1)
-    fold_core(2)
-    outs[3] = expert_call(3, place, tok, *tables, (weights, sources))
-    outs, folds = join(outs, folds)
-
-    fold_z(0)
-    fold_two(1)
-    fold_one(2)
-    fold_core(3)
+    outs, tok, weights, spread_2, expert_z = join(outs, tok, weights, spread_2, expert_z)
+
+    cores[0] = across(outs[0][1], 1)
+    half, = blend_call(collected(spread_2))
+    weights_2 = (half, across(half, 1))
+    spread_3 = spread(expert_z[3])
+    outs[1] = expert_call(1, place, tok, *tables, (weights, sources))
+    outs, tok, cores, weights_2, spread_3 = join(outs, tok, cores, weights_2, spread_3)
+
+    cores[1] = across(outs[1][1], 1)
+    half, *parts = blend_call(collected(spread_3), *quarters(0))
+    weights_3 = (half, across(half, 1))
+    chips[0] = send_chips(parts)
+    outs[2] = expert_call(2, place, tok, *tables, (weights_2, sources))
+    outs, tok, cores, chips, weights_3 = join(outs, tok, cores, chips, weights_3)
+
+    cores[2] = across(outs[2][1], 1)
+    chips[1] = send_chips(blend_call(*quarters(1)))
+    outs[3] = expert_call(3, place, tok, *tables, (weights_3, sources))
+    outs, cores, chips, shards = join(outs, cores, chips, shards)
+
+    cores[3] = across(outs[3][1], 1)
+    chips[2] = send_chips(blend_call(*quarters(2)))
     pairs = [outs[k][2] for k in range(n_group)]
     biases = [outs[k][3] for k in range(n_group)]
-    block_out, gres, gatt, *_, late = combine_call(
-        0, count, (), place, cotangent, att, res, tok, slots_row, full, small, pairs, biases
-    )
-    gres, gatt, late, folds, shards = join(gres, gatt, late, folds, shards)
-
-    fold_z(1)
-    fold_z(2)
-    fold_one(3)
-    input_grad, *_, keep, send = backward_call(0, count, (), place, images, qkv, lse, gres, gatt, full, small, late, n_group)
-    keep, send, folds, shards = join(keep, send, folds, shards)
-    fold_z(3)
+    block_out, gres, gatt, late, shards[0], shards[1] = combine_call(
+        (own_quarter(0), own_quarter(1)), place, cotangent, att, res, tok, slots_row, full, small, pairs, biases
+    )
+    gres, gatt, late, cores, chips, shards = join(gres, gatt, late, cores, chips, shards)
+
+    *parts, shards[2] = blend_call(*quarters(3), own_quarter(2))
+    chips[3] = send_chips(parts)
+    passed = along(rest_of_replicas(shards.pop(2)), 1)
+    for k in range(2):
+        shards[k] = send_shard(k, shards[k])
+    input_grad, keep, send = backward_call(place, images, qkv, lse, gres, gatt, full, small, late, n_group)
+    keep, send, chips, shards, passed = join(keep, send, chips, shards, passed)
+    if n_replica == PIECES:
+        value, = blend_call(("sum", own_quarter(3)[1] + [(passed, ())]))
+    else:
+        value = plus(rest_of_replicas(*blend_call(own_quarter(3))), passed)
+    shards[3] = along(value, 1)
 
     value = plus(keep, across(send, 1))
     value = plus(value[0], *(across(value[pos], offset_of(pos)) for pos in range(1, PIECES // 2)))
     value = rest_of_replicas(value)
-    value, total = join(value, plus(*shards.values()))
+    total, = blend_call(("sum", [(v, ()) for v in shards.values()]))
+    value, total = join(value, total)
     own_half = spread(total)
     value = plus(*([value[0]] + [along(value[d], -d) for d in range(1, n_group)]))
     value, own_half = join(value, own_half)
     value = spread(value)
-    value = value + [across(v, 1) for v in value]
-    grad_qkv, grad_proj, grad_router, grad_inner_bias, grad_outer_bias, rest = finish_dense_call(
-        place, value, model, n_group, hidden
-    )
-
     other_half = [across(v, 1) for v in own_half]
     grads = finish_call(0, place, own_half)
     grad_inner, grad_outer = finish_call(1, place, other_half, grads)
+    value, grad_inner, grad_outer = join(value, grad_inner, grad_outer)
+    value = jnp.stack(value)
+    value = (value, across(value, 1))
+    grad_qkv, grad_proj, grad_router, grad_inner_bias, grad_outer_bias, *rest = finish_dense_call(
+        place, value, model, n_group, hidden
+    )
     return (
-        block_out, input_grad, rest[0], rest[1], grad_qkv, rest[5:7].reshape(-1), grad_proj, rest[2], rest[3],
-        rest[4], grad_router.T, grad_inner, grad_inner_bias, grad_outer, grad_outer_bias,
+        block_out, input_grad, rest[0], rest[1], grad_qkv, rest[5], grad_proj, rest[2], rest[3], rest[4],
+        grad_router.T, grad_inner, grad_inner_bias, grad_outer, grad_outer_bias,
     )
 
 

time: 329 us -> 317 us (0.964)
  Pallas kernels: 152 us -> 175 us
  other arithmetic: 25.8 us -> 4 us
  waiting for transfers between devices: 79.9 us -> 63.7 us
  starting transfers between devices: 56.1 us -> 62.7 us
    pallas_call x5 -> x13, Pallas kernels: 54.7 us -> 77.6 us  [the longest x8 24.9 us: blend_call(): pl.pallas_call(functools.partial(blend_kernel, jobs=plan, count_in=len(ar...]
    ppermute x12, waiting for transfers between devices: 32.9 us -> 11.7 us  [along(): lax.ppermute(value, 'group', [(i, (i + shift) % n_group) for i in range(n...]
    convert_element_type x14 -> x3, other arithmetic: 22.6 us -> 3.14 us  [plus(): return sum((v.astype(F32) for v in values)).astype(BF16)]
    ppermute x55 -> x50, waiting for transfers between devices: 47 us -> 52 us  [across(): lax.ppermute(value, 'replica', [(i, i ^ bit) for i in range(n_replica)])]
    ppermute x12, starting transfers between devices: 16 us -> 20.9 us  [along(): lax.ppermute(value, 'group', [(i, (i + shift) % n_group) for i in range(n...]
    ppermute x55 -> x50, starting transfers between devices: 40 us -> 41.8 us  [across(): lax.ppermute(value, 'replica', [(i, i ^ bit) for i in range(n_replica)])]
  transfers between devices with their start and end apart: 67 -> 62, of which waited for: 18 -> 24; matrix products, arithmetic and copies ran while one was open for 7% -> 1% of each run, Pallas kernels for 45% -> 53%
where the time goes in v3:
time: 317 us; the launch traced here: 312 us
  Pallas kernels  175 us (55%)
  waiting for transfers between devices  63.7 us (20%)
  starting transfers between devices  62.7 us (20%)
  local copies, waits for them, and re-layouts  4.26 us (1%)
  other arithmetic  4 us (1%)
    pallas_call x4, Pallas kernels, expert_call(): pl.pallas_call(functools.partial(expert_kernel, turn=turn, sources=source...  76.8 us
    ppermute x50, waiting for transfers between devices, across(): lax.ppermute(value, 'replica', [(i, i ^ bit) for i in range(n_replica)])  52 us
    ppermute x50, starting transfers between devices, across(): lax.ppermute(value, 'replica', [(i, i ^ bit) for i in range(n_replica)])  41.8 us
    pallas_call x8, Pallas kernels, blend_call(): pl.pallas_call(functools.partial(blend_kernel, jobs=plan, count_in=len(ar...  24.9 us
    pallas_call x1, Pallas kernels, backward_call(): pl.pallas_call(backward_kernel, out_shape=outs, grid_spec=pltpu.PrefetchS...  22.5 us
    ppermute x12, starting transfers between devices, along(): lax.ppermute(value, 'group', [(i, (i + shift) % n_group) for i in range(n...  20.9 us
    pallas_call x1, Pallas kernels, combine_call(): pl.pallas_call(functools.partial(combine_kernel, turns=turns, jobs=plan,...  20.2 us
    pallas_call x1, Pallas kernels, forward_call(): pl.pallas_call(forward_kernel, out_shape=outs, grid_spec=pltpu.PrefetchSc...  16.1 us
  transfers between devices with their start and end apart: 62, of which 24 were waited for; matrix products, arithmetic and copies ran while one was open for 1% of the time, Pallas kernels for 53%

profile of v3, /device:TPU:0, one launch (start us, length us, event | category | flops | bytes accessed | tf_op | source)
XLA Modules:
  0.0 312.3 jit_solution(6850118341331094553)
XLA Ops:
  4.1 3.0 collective-permute-start
  11.0 2.6 cut_own.1
  20.1 4.6 %collective-permute-done.3.refs_1_ = bf16[3,16,2176]{2,1,0:T(8,128)(2,1)S(1)} collective-permute-done((bf16[3,16,2176]{2,1,0:T(8,128)(2,1)S(1)}, bf16[3,16,2176]{2,1,0:T(8,128)(2,1)S(1)}, u32[]{:S(2)}, u32[]{:S(2)}) %collective-permute-start.3) | collective-permute-done | bytes 208928 | tf_op jit(solution)/shard_map/ppermute | solution.py:840
  24.7 4.2 %collective-permute-done.4.refs_2_ = bf16[3,16,2176]{2,1,0:T(8,128)(2,1)S(1)} collective-permute-done((bf16[3,16,2176]{2,1,0:T(8,128)(2,1)S(1)}, bf16[3,16,2176]{2,1,0:T(8,128)(2,1)S(1)}, u32[]{:S(2)}, u32[]{:S(2)}) %collective-permute-start.4) | collective-permute-done | bytes 208928 | tf_op jit(solution)/shard_map/ppermute | solution.py:840
  34.7 16.1 %attention_forward.1 = (bf16[5,208,1536]{2,1,0:T(8,128)(2,1)}, bf16[5,208,512]{2,1,0:T(8,128)(2,1)}, f32[5,208,512]{2,1,0:T(8,128)}, f32[5,208,128]{2,1,0:T(8,12...) custom-call(s32[4]{0:T(128)} %pad_add_fusion.place, ...), custom_call_target="tpu_custom_call" | custom-call | flops 13200000000 | bytes 12582912 | tf_op jit(solution)/shard_map/attention_forward/pallas_call | solution.py:242
  50.8 3.6 %collective-permute-done.12.refs_2_ = bf16[2,256,512]{2,1,0:T(8,128)(2,1)} collective-permute-done((bf16[2,256,512]{2,1,0:T(8,128)(2,1)S(1)}, bf16[2,256,512]{2,1,0:T(8,128)(2,1)}, u32[]{:S(2)}, u32[]{:S(2)}) %collective-permute-start.12) | collective-permute-done | bytes 524320 | tf_op jit(solution)/shard_map/ppermute | solution.py:840
  55.8 2.7 blend.8.refs_0_
  65.2 19.0 %expert.4 = (bf16[2,2,2,256,512]{4,3,2,1,0:T(8,128)(2,1)}, bf16[2,2,2,256,512]{4,3,2,1,0:T(8,128)(2,1)}, bf16[640,1024]{1,0:T(8,128)(2,1)}, f32[32,128]{1,0:T(8,128)}) custom-call(s32[4]{0:T(128)} %pad_add_fusion.place, s32[5,8,256]{2,1,0:T(8,128)} %pad.8.slots, f32[5,8,256]{2,1,0:T(8,128)} %get-tuple-element.203.gates, ...), custom_call_target="tpu_custom_call" | custom-call | flops 19800000512 | bytes 14680064 | tf_op jit(solution)/shard_map/expert/pallas_call | solution.py:463
  92.2 19.4 %expert.5 = (bf16[2,2,2,256,512]{4,3,2,1,0:T(8,128)(2,1)}, bf16[2,2,2,256,512]{4,3,2,1,0:T(8,128)(2,1)}, bf16[640,1024]{1,0:T(8,128)(2,1)}, f32[32,128]{1,0:T(8,128)}) custom-call(s32[4]{0:T(128)} %pad_add_fusion.place, s32[5,8,256]{2,1,0:T(8,128)} %pad.8.slots, f32[5,8,256]{2,1,0:T(8,128)} %get-tuple-element.203.gates, ...), custom_call_target="tpu_custom_call" | custom-call | flops 19800000512 | bytes 14680064 | tf_op jit(solution)/shard_map/expert/pallas_call | solution.py:463
  114.9 4.4 %blend.10 = (bf16[4,2,256,512]{3,2,1,0:T(8,128)(2,1)}, bf16[2,256,512]{2,1,0:T(8,128)(2,1)}, bf16[2,256,512]{2,1,0:T(8,128)(2,1)}, bf16[2,256,512]{2,1,0:T(8,128)(2,1)}) custom-call(bf16[2,256,512]{2,1,0:T(8,128)(2,1)} %copy-done.12, bf16[2,256,512]{2,1,0:T(8,128)(2,1)} %copy-done.23, bf16[2,256,512]{2,1,0:T(8,128)(2,1)} %copy-done.24, ...), custom_call_target="tpu_custom_call" | custom-call | flops 3300000000 | bytes 3145728 | tf_op jit(solution)/shard_map/blend/pallas_call | solution.py:345
  124.4 19.2 %expert.6 = (bf16[2,2,2,256,512]{4,3,2,1,0:T(8,128)(2,1)}, bf16[2,2,2,256,512]{4,3,2,1,0:T(8,128)(2,1)}, bf16[640,1024]{1,0:T(8,128)(2,1)}, f32[32,128]{1,0:T(8,128)}) custom-call(s32[4]{0:T(128)} %pad_add_fusion.place, s32[5,8,256]{2,1,0:T(8,128)} %pad.8.slots, f32[5,8,256]{2,1,0:T(8,128)} %get-tuple-element.203.gates, ...), custom_call_target="tpu_custom_call" | custom-call | flops 19800000512 | bytes 14680064 | tf_op jit(solution)/shard_map/expert/pallas_call | solution.py:463
  143.7 2.9 collective-permute-done.27.refs_18_
  147.6 2.9 blend.11
  154.1 19.2 %expert.7 = (bf16[2,2,2,256,512]{4,3,2,1,0:T(8,128)(2,1)}, bf16[2,2,2,256,512]{4,3,2,1,0:T(8,128)(2,1)}, bf16[640,1024]{1,0:T(8,128)(2,1)}, f32[32,128]{1,0:T(8,128)}) custom-call(s32[4]{0:T(128)} %pad_add_fusion.place, s32[5,8,256]{2,1,0:T(8,128)} %pad.8.slots, f32[5,8,256]{2,1,0:T(8,128)} %get-tuple-element.203.gates, ...), custom_call_target="tpu_custom_call" | custom-call | flops 19800000512 | bytes 14680064 | tf_op jit(solution)/shard_map/expert/pallas_call | solution.py:463
  177.1 3.0 blend.12
  183.7 20.2 %combine.1 = (bf16[5,197,512]{2,1,0:T(8,128)(2,1)}, f32[5,208,512]{2,1,0:T(8,128)}, bf16[5,208,512]{2,1,0:T(8,128)(2,1)}, bf16[512,640]{1,0:T(8,128)(2,1)}, bf16...) custom-call(s32[4]{0:T(128)} %pad_add_fusion.place, bf16[5,197,512]{2,1,0:T(8,128)(2,1)} %refs_0_.5, ...), custom_call_target="tpu_custom_call" | custom-call | flops 19800000512 | bytes 14680064 | tf_op jit(solution)/shard_map/combine/pallas_call | solution.py:603
  207.3 4.3 %blend.13 = (bf16[2,256,512]{2,1,0:T(8,128)(2,1)}, bf16[2,256,512]{2,1,0:T(8,128)(2,1)}, bf16[2,256,512]{2,1,0:T(8,128)(2,1)}, bf16[2,256,512]{2,1,0:T(8,128)(2,1)}) custom-call(bf16[2,2,2,256,512]{4,3,2,1,0:T(8,128)(2,1)} %get-tuple-element.322.refs_0_, bf16[2,2,2,256,512]{4,3,2,1,0:T(8,128)(2,1)} %collective-permute-done.34.refs_1_, ...), custom_call_target="tpu_custom_call" | custom-call | flops 3300000000 | bytes 3145728 | tf_op jit(solution)/shard_map/blend/pallas_call | solution.py:345
  217.5 22.5 %attention_backward.1 = (f32[5,197,512]{2,1,0:T(8,128)}, bf16[4,4,16,2176]{3,2,1,0:T(8,128)(2,1)}, bf16[4,4,16,2176]{3,2,1,0:T(8,128)(2,1)}) custom-call(s32[4]{0:T(128)} %pad_add_fusion.place, bf16[5,197,512]{2,1,0:T(8,128)(2,1)} %images.3, bf16[5,208,1536]{2,1,0:T(8,128)(2,1)} %get-tuple-element.300.qkv, f32[5,208,128]{2,1,0:T(8,128)} %get-tuple-element.301.lse, ...), custom_call_target="tpu_custom_call" | custom-call | flops 24199999488 | bytes 14680064 | tf_op jit(solution)/shard_map/attention_backward/pallas_call | solution.py:709
  240.8 2.8 blend.14
  250.8 9.1 %collective-permute-done.47.refs_2_ = bf16[2,256,512]{2,1,0:T(8,128)(2,1)} collective-permute-done((bf16[2,256,512]{2,1,0:T(8,128)(2,1)}, bf16[2,256,512]{2,1,0:T(8,128)(2,1)}, u32[]{:S(2)}, u32[]{:S(2)}) %collective-permute-start.47) | collective-permute-done | bytes 524320 | tf_op jit(solution)/shard_map/ppermute | solution.py:843
  273.0 11.5 %collective-permute-done.51.refs_1_ = bf16[2,256,512]{2,1,0:T(8,128)(2,1)S(1)} collective-permute-done((bf16[2,256,512]{2,1,0:T(8,128)(2,1)}, bf16[2,256,512]{2,1,0:T(8,128)(2,1)S(1)}, u32[]{:S(2)}, u32[]{:S(2)}) %collective-permute-start.51) | collective-permute-done | bytes 524320 | tf_op jit(solution)/shard_map/ppermute | solution.py:840
  284.6 10.1 %collective-permute-done.52.refs_2_ = bf16[2,256,512]{2,1,0:T(8,128)(2,1)S(1)} collective-permute-done((bf16[2,256,512]{2,1,0:T(8,128)(2,1)}, bf16[2,256,512]{2,1,0:T(8,128)(2,1)S(1)}, u32[]{:S(2)}, u32[]{:S(2)}) %collective-permute-start.52) | collective-permute-done | bytes 524320 | tf_op jit(solution)/shard_map/ppermute | solution.py:840
  296.7 3.9 %finish_experts.2 = (f32[1,512,2048]{2,1,0:T(8,128)}, f32[1,2048,512]{2,1,0:T(8,128)}) custom-call(s32[4]{0:T(128)} %pad_add_fusion.place, bf16[2,256,512]{2,1,0:T(8,128)(2,1)} %blend.15.refs_0_, bf16[2,256,512]{2,1,0:T(8,128)(2,1)} %copy-done.17, bf16[2,256,512]{2,1,0:T(8,128)(2,1)} %copy-done.16, bf16[2,256,512]{2,1,0:T(8,128)(2,1)} %copy-done.18), custom_call_target="tpu_custom_call" | custom-call | flops 4400000000 | bytes 6291456 | tf_op jit(solution)/shard_map/finish_experts/pallas_call | solution.py:757
  303.3 3.9 %finish_experts.3 = (f32[1,512,2048]{2,1,0:T(8,128)}, f32[1,2048,512]{2,1,0:T(8,128)}) custom-call(s32[4]{0:T(128)} %pad_add_fusion.place, bf16[2,256,512]{2,1,0:T(8,128)(2,1)} %collective-permute-done.57.refs_0_, bf16[2,256,512]{2,1,0:T(8,128)(2,1)} %collective-permute-done.58.refs_1_, ...), custom_call_target="tpu_custom_call", output_to_operand_aliasing={{0}: (5, {}), {1}: (6, {})} | custom-call | flops 4400000000 | bytes 6291456 | tf_op jit(solution)/shard_map/finish_experts/pallas_call | solution.py:757
  (199 shorter events, 94.8 us)
Async XLA Ops:
  30.3 25.4 %collective-permute-start.14 = (bf16[2,256,512]{2,1,0:T(8,128)(2,1)}, bf16[2,256,512]{2,1,0:T(8,128)(2,1)S(1)}, u32[]{:S(2)}, u32[]{:S(2)}) collective-permute-start(bf16[2,256,512]{2,1,0:T(8,128)(2,1)} %cut_own.1), channel_id=1, source_target_pairs={{0,2},{1,3},{2,0},{3,1},{4,6},{5,7},{6,4},{7,5},{8,10},{9,11},{10,... | collective-permute-start | bytes 1572872 | tf_op jit(solution)/shard_map/ppermute | solution.py:843
  58.4 27.1 %collective-permute-start.15 = (bf16[4,2,256,512]{3,2,1,0:T(8,128)(2,1)}, bf16[4,2,256,512]{3,2,1,0:T(8,128)(2,1)}, u32[]{:S(2)}, u32[]{:S(2)}) collective-permute-start(bf16[4,2,256,512]{3,2,1,0:T(8,128)(2,1)} %blend.8.refs_0_), channel_id=1, source_target_pairs={{0,4},{4,0},{8,12},{12,8},{16,20},{20,16},{24,28},{28,24},{1,5},{5... | collective-permute-start | bytes 6291464 | tf_op jit(solution)/shard_map/ppermute | solution.py:840
  59.3 24.9 %collective-permute-start.16 = (bf16[2,256,512]{2,1,0:T(8,128)(2,1)S(1)}, bf16[2,256,512]{2,1,0:T(8,128)(2,1)}, u32[]{:S(2)}, u32[]{:S(2)}) collective-permute-start(bf16[2,256,512]{2,1,0:T(8,128)(2,1)S(1)} %collective-permute-done.14.refs_0_), channel_id=1, source_target_pairs={{0,8},{4,12},{8,0},{12,4},{16,24},{20,28},{24,16},{28,20},{1,9},{5... | collective-permute-start | bytes 1572872 | tf_op jit(solution)/shard_map/ppermute | solution.py:840
  60.2 24.2 %collective-permute-start.17 = (bf16[2,256,512]{2,1,0:T(8,128)(2,1)S(1)}, bf16[2,256,512]{2,1,0:T(8,128)(2,1)}, u32[]{:S(2)}, u32[]{:S(2)}) collective-permute-start(bf16[2,256,512]{2,1,0:T(8,128)(2,1)S(1)} %collective-permute-done.14.refs_0_), channel_id=1, source_target_pairs={{0,16},{4,20},{8,24},{12,28},{16,0},{20,4},{24,8},{28,12},{1,17},{... | collective-permute-start | bytes 1572872 | tf_op jit(solution)/shard_map/ppermute | solution.py:840
  61.6 24.0 %collective-permute-start.18 = (bf16[2,256,512]{2,1,0:T(8,128)(2,1)S(1)}, bf16[2,256,512]{2,1,0:T(8,128)(2,1)}, u32[]{:S(2)}, u32[]{:S(2)}) collective-permute-start(bf16[2,256,512]{2,1,0:T(8,128)(2,1)S(1)} %collective-permute-done.14.refs_0_), channel_id=1, source_target_pairs={{0,24},{4,28},{8,16},{12,20},{16,8},{20,12},{24,0},{28,4},{1,25},{... | collective-permute-start | bytes 1572872 | tf_op jit(solution)/shard_map/ppermute | solution.py:840
  85.6 29.3 %collective-permute-start.20 = (bf16[2,2,2,256,512]{4,3,2,1,0:T(8,128)(2,1)}, bf16[2,2,2,256,512]{4,3,2,1,0:T(8,128)(2,1)}, u32[]{:S(2)}, u32[]{:S(2)}) collective-permute-start(bf16[2,2,2,256,512]{4,3,2,1,0:T(8,128)(2,1)} %get-tuple-element.217), channel_id=1, source_target_pairs={{0,4},{4,0},{8,12},{12,8},{16,20},{20,16},{24,28},{28,24},{1,5},{5... | collective-permute-start | bytes 6291464 | tf_op jit(solution)/shard_map/ppermute | solution.py:840
  88.3 26.6 %collective-permute-start.21 = (bf16[4,2,256,512]{3,2,1,0:T(8,128)(2,1)}, bf16[4,2,256,512]{3,2,1,0:T(8,128)(2,1)}, u32[]{:S(2)}, u32[]{:S(2)}) collective-permute-start(bf16[4,2,256,512]{3,2,1,0:T(8,128)(2,1)} %blend.9.refs_0_), channel_id=1, source_target_pairs={{0,4},{4,0},{8,12},{12,8},{16,20},{20,16},{24,28},{28,24},{1,5},{5... | collective-permute-start | bytes 6291464 | tf_op jit(solution)/shard_map/ppermute | solution.py:840
  91.0 23.8 %collective-permute-start.24 = (bf16[2,256,512]{2,1,0:T(8,128)(2,1)S(1)}, bf16[2,256,512]{2,1,0:T(8,128)(2,1)}, u32[]{:S(2)}, u32[]{:S(2)}) collective-permute-start(bf16[2,256,512]{2,1,0:T(8,128)(2,1)S(1)} %collective-permute-done.19.refs_0_), channel_id=1, source_target_pairs={{0,24},{4,28},{8,16},{12,20},{16,8},{20,12},{24,0},{28,4},{1,25},{... | collective-permute-start | bytes 1572872 | tf_op jit(solution)/shard_map/ppermute | solution.py:840
  114.9 32.7 %collective-permute-start.25 = (bf16[2,2,2,256,512]{4,3,2,1,0:T(8,128)(2,1)}, bf16[2,2,2,256,512]{4,3,2,1,0:T(8,128)(2,1)}, u32[]{:S(2)}, u32[]{:S(2)}) collective-permute-start(bf16[2,2,2,256,512]{4,3,2,1,0:T(8,128)(2,1)} %get-tuple-element.236), channel_id=1, source_target_pairs={{0,4},{4,0},{8,12},{12,8},{16,20},{20,16},{24,28},{28,24},{1,5},{5... | collective-permute-start | bytes 6291464 | tf_op jit(solution)/shard_map/ppermute | solution.py:840
  119.3 28.2 %collective-permute-start.29 = (bf16[4,2,256,512]{3,2,1,0:T(8,128)(2,1)}, bf16[4,2,256,512]{3,2,1,0:T(8,128)(2,1)}, u32[]{:S(2)}, u32[]{:S(2)}) collective-permute-start(bf16[4,2,256,512]{3,2,1,0:T(8,128)(2,1)} %get-tuple-element.267.refs_0_), channel_id=1, source_target_pairs={{0,4},{4,0},{8,12},{12,8},{16,20},{20,16},{24,28},{28,24},{1,5},{5... | collective-permute-start | bytes 6291464 | tf_op jit(solution)/shard_map/ppermute | solution.py:840
  121.9 24.7 %collective-permute-start.27 = (bf16[2,256,512]{2,1,0:T(8,128)(2,1)}, bf16[2,256,512]{2,1,0:T(8,128)(2,1)S(1)}, u32[]{:S(2)}, u32[]{:S(2)}) collective-permute-start(bf16[2,256,512]{2,1,0:T(8,128)(2,1)} %get-tuple-element.252), channel_id=1, source_target_pairs={{0,16},{4,20},{8,24},{12,28},{16,0},{20,4},{24,8},{28,12},{1,17},{... | collective-permute-start | bytes 1572872 | tf_op jit(solution)/shard_map/ppermute | solution.py:840
  123.4 24.1 %collective-permute-start.28 = (bf16[2,256,512]{2,1,0:T(8,128)(2,1)}, bf16[2,256,512]{2,1,0:T(8,128)(2,1)S(1)}, u32[]{:S(2)}, u32[]{:S(2)}) collective-permute-start(bf16[2,256,512]{2,1,0:T(8,128)(2,1)} %get-tuple-element.253), channel_id=1, source_target_pairs={{0,24},{4,28},{8,16},{12,20},{16,8},{20,12},{24,0},{28,4},{1,25},{... | collective-permute-start | bytes 1572872 | tf_op jit(solution)/shard_map/ppermute | solution.py:840
  147.5 29.6 %collective-permute-start.30 = (bf16[2,2,2,256,512]{4,3,2,1,0:T(8,128)(2,1)}, bf16[2,2,2,256,512]{4,3,2,1,0:T(8,128)(2,1)}, u32[]{:S(2)}, u32[]{:S(2)}) collective-permute-start(bf16[2,2,2,256,512]{4,3,2,1,0:T(8,128)(2,1)} %get-tuple-element.264), channel_id=1, source_target_pairs={{0,4},{4,0},{8,12},{12,8},{16,20},{20,16},{24,28},{28,24},{1,5},{5... | collective-permute-start | bytes 6291464 | tf_op jit(solution)/shard_map/ppermute | solution.py:840
  151.8 24.2 %collective-permute-start.32 = (bf16[2,256,512]{2,1,0:T(8,128)(2,1)}, bf16[2,256,512]{2,1,0:T(8,128)(2,1)S(1)}, u32[]{:S(2)}, u32[]{:S(2)}) collective-permute-start(bf16[2,256,512]{2,1,0:T(8,128)(2,1)} %get-tuple-element.279), channel_id=1, source_target_pairs={{0,16},{4,20},{8,24},{12,28},{16,0},{20,4},{24,8},{28,12},{1,17},{... | collective-permute-start | bytes 1572872 | tf_op jit(solution)/shard_map/ppermute | solution.py:840
  153.1 24.0 %collective-permute-start.33 = (bf16[2,256,512]{2,1,0:T(8,128)(2,1)}, bf16[2,256,512]{2,1,0:T(8,128)(2,1)S(1)}, u32[]{:S(2)}, u32[]{:S(2)}) collective-permute-start(bf16[2,256,512]{2,1,0:T(8,128)(2,1)} %get-tuple-element.280), channel_id=1, source_target_pairs={{0,24},{4,28},{8,16},{12,20},{16,8},{20,12},{24,0},{28,4},{1,25},{... | collective-permute-start | bytes 1572872 | tf_op jit(solution)/shard_map/ppermute | solution.py:840
  177.1 29.4 %collective-permute-start.34 = (bf16[2,2,2,256,512]{4,3,2,1,0:T(8,128)(2,1)}, bf16[2,2,2,256,512]{4,3,2,1,0:T(8,128)(2,1)}, u32[]{:S(2)}, u32[]{:S(2)}) collective-permute-start(bf16[2,2,2,256,512]{4,3,2,1,0:T(8,128)(2,1)} %get-tuple-element.306), channel_id=1, source_target_pairs={{0,4},{4,0},{8,12},{12,8},{16,20},{20,16},{24,28},{28,24},{1,5},{5... | collective-permute-start | bytes 6291464 | tf_op jit(solution)/shard_map/ppermute | solution.py:840
  180.2 23.8 %collective-permute-start.35 = (bf16[2,256,512]{2,1,0:T(8,128)(2,1)}, bf16[2,256,512]{2,1,0:T(8,128)(2,1)S(1)}, u32[]{:S(2)}, u32[]{:S(2)}) collective-permute-start(bf16[2,256,512]{2,1,0:T(8,128)(2,1)} %get-tuple-element.308), channel_id=1, source_target_pairs={{0,8},{4,12},{8,0},{12,4},{16,24},{20,28},{24,16},{28,20},{1,9},{5... | collective-permute-start | bytes 1572872 | tf_op jit(solution)/shard_map/ppermute | solution.py:840
  181.1 24.4 %collective-permute-start.36 = (bf16[2,256,512]{2,1,0:T(8,128)(2,1)}, bf16[2,256,512]{2,1,0:T(8,128)(2,1)S(1)}, u32[]{:S(2)}, u32[]{:S(2)}) collective-permute-start(bf16[2,256,512]{2,1,0:T(8,128)(2,1)} %get-tuple-element.309), channel_id=1, source_target_pairs={{0,16},{4,20},{8,24},{12,28},{16,0},{20,4},{24,8},{28,12},{1,17},{... | collective-permute-start | bytes 1572872 | tf_op jit(solution)/shard_map/ppermute | solution.py:840
  182.7 23.8 %collective-permute-start.37 = (bf16[2,256,512]{2,1,0:T(8,128)(2,1)}, bf16[2,256,512]{2,1,0:T(8,128)(2,1)S(1)}, u32[]{:S(2)}, u32[]{:S(2)}) collective-permute-start(bf16[2,256,512]{2,1,0:T(8,128)(2,1)} %get-tuple-element.310), channel_id=1, source_target_pairs={{0,24},{4,28},{8,16},{12,20},{16,8},{20,12},{24,0},{28,4},{1,25},{... | collective-permute-start | bytes 1572872 | tf_op jit(solution)/shard_map/ppermute | solution.py:840
  211.6 28.4 %collective-permute-start.38 = (bf16[2,256,512]{2,1,0:T(8,128)(2,1)}, bf16[2,256,512]{2,1,0:T(8,128)(2,1)S(1)}, u32[]{:S(2)}, u32[]{:S(2)}) collective-permute-start(bf16[2,256,512]{2,1,0:T(8,128)(2,1)} %get-tuple-element.325), channel_id=1, source_target_pairs={{0,8},{4,12},{8,0},{12,4},{16,24},{20,28},{24,16},{28,20},{1,9},{5... | collective-permute-start | bytes 1572872 | tf_op jit(solution)/shard_map/ppermute | solution.py:840
  212.8 27.2 %collective-permute-start.39 = (bf16[2,256,512]{2,1,0:T(8,128)(2,1)}, bf16[2,256,512]{2,1,0:T(8,128)(2,1)}, u32[]{:S(2)}, u32[]{:S(2)}) collective-permute-start(bf16[2,256,512]{2,1,0:T(8,128)(2,1)} %get-tuple-element.326), channel_id=1, source_target_pairs={{0,16},{4,20},{8,24},{12,28},{16,0},{20,4},{24,8},{28,12},{1,17},{... | collective-permute-start | bytes 1572872 | tf_op jit(solution)/shard_map/ppermute | solution.py:840
  214.1 25.9 %collective-permute-start.40 = (bf16[2,256,512]{2,1,0:T(8,128)(2,1)}, bf16[2,256,512]{2,1,0:T(8,128)(2,1)}, u32[]{:S(2)}, u32[]{:S(2)}) collective-permute-start(bf16[2,256,512]{2,1,0:T(8,128)(2,1)} %get-tuple-element.327), channel_id=1, source_target_pairs={{0,24},{4,28},{8,16},{12,20},{16,8},{20,12},{24,0},{28,4},{1,25},{... | collective-permute-start | bytes 1572872 | tf_op jit(solution)/shard_map/ppermute | solution.py:840
  215.2 24.9 %collective-permute-start.41 = (bf16[2,256,512]{2,1,0:T(8,128)(2,1)S(1)}, bf16[2,256,512]{2,1,0:T(8,128)(2,1)S(1)}, u32[]{:S(2)}, u32[]{:S(2)}) collective-permute-start(bf16[2,256,512]{2,1,0:T(8,128)(2,1)S(1)} %copy-done.10), channel_id=1, source_target_pairs={{0,3},{1,0},{2,1},{3,2},{4,7},{5,4},{6,5},{7,6},{8,11},{9,8},{10,9... | collective-permute-start | bytes 1572872 | tf_op jit(solution)/shard_map/ppermute | solution.py:843
  270.5 24.2 %collective-permute-start.52 = (bf16[2,256,512]{2,1,0:T(8,128)(2,1)}, bf16[2,256,512]{2,1,0:T(8,128)(2,1)S(1)}, u32[]{:S(2)}, u32[]{:S(2)}) collective-permute-start(bf16[2,256,512]{2,1,0:T(8,128)(2,1)} %blend.15.refs_0_), channel_id=1, source_target_pairs={{0,16},{4,20},{8,24},{12,28},{16,0},{20,4},{24,8},{28,12},{1,17},{... | collective-permute-start | bytes 1572872 | tf_op jit(solution)/shard_map/ppermute | solution.py:840
  (71 other events, 631.7 us)

commit v4 on v3

--- a/solution.py
+++ b/solution.py
@@ -354,9 +354,14 @@
     )(*arrays)
 
 
-def expert_kernel(place, slots, gates, small, tok, *refs, turn, sources, count_in):
+def expert_kernel(place, slots, gates, small, tok, *refs, turn, sources, count_in, count_side):
     arrays = refs[:count_in]
+    beside = refs[count_in : count_in + count_side]
+    count_in += count_side
     keep, send, pair_out, bias_out = refs[count_in : count_in + 4]
+    if count_side:
+        collected, passing, side_sems = refs[count_in + 4], refs[-2], refs[-1]
+        refs = refs[: count_in + 4] + refs[count_in + 5 : -2]
     tokens, onehot, buffer, grad_slots, rows, back, mine, inners, outers, staged, token_sem, in_sems, out_sems = (
         refs[count_in + 4 :]
     )
@@ -394,6 +399,10 @@
     outer_bias = jnp.concatenate([mine[28 + c : 29 + c, :] for c in range(model // 128)], axis=1)
     token_copy.wait()
     for copy in loads:
+        copy.start()
+    side_loads = [pltpu.make_async_copy(b, passing.at[k], side_sems.at[0, k]) for k, b in enumerate(beside)]
+    side_stores = [pltpu.make_async_copy(passing.at[k], collected.at[k], side_sems.at[1, k]) for k in range(count_side)]
+    for copy in side_loads:
         copy.start()
     buffer[...] = dot_nn(onehot[...], tokens[:, :model]).astype(BF16)
     grads = (dot_nn(onehot[...], tokens[:, model:]) * gate).astype(BF16)
@@ -423,6 +432,10 @@
     stores = []
     for i in range(steps):
         hidden, grad_active, lines = first_products(i)
+        if i == 1:
+            for load, store in zip(side_loads, side_stores):
+                load.wait()
+                store.start()
         here = slice(i * per, (i + 1) * per)
         active, slope = gelu_parts(hidden)
         active = active.astype(BF16)
@@ -446,11 +459,11 @@
         back[...] = new_back if i == 0 else new_back + back[...]
     pair_out[:, :model] = rows[...].astype(BF16)
     pair_out[:, model:] = back[...].astype(BF16)
-    for copy in stores:
+    for copy in stores + side_stores:
         copy.wait()
 
 
-def expert_call(turn, place, tok, slots, gates, small, weights):
+def expert_call(turn, place, tok, slots, gates, small, weights, beside=()):
     arrays, sources = weights
     model = tok.shape[1] // 2
     count = slots.shape[0]
@@ -461,15 +474,17 @@
     anywhere = pl.BlockSpec(memory_space=pl.ANY)
     half = jax.ShapeDtypeStruct((2, 2, 2, block, model), BF16)
     return pl.pallas_call(
-        functools.partial(expert_kernel, turn=turn, sources=sources, count_in=len(arrays)),
+        functools.partial(expert_kernel, turn=turn, sources=sources, count_in=len(arrays), count_side=len(beside)),
         out_shape=(
             half,
             half,
             jax.ShapeDtypeStruct((CAP, 2 * model), BF16),
             jax.ShapeDtypeStruct((32, 128), F32),
-        ),
-        in_specs=[pl.BlockSpec(memory_space=pltpu.SMEM), vmem, vmem, vmem, anywhere] + [anywhere] * len(arrays),
-        out_specs=[anywhere, anywhere, vmem, vmem],
+        )
+        + tuple(jax.ShapeDtypeStruct((len(beside),) + b.shape, BF16) for b in beside[:1]),
+        in_specs=[pl.BlockSpec(memory_space=pltpu.SMEM), vmem, vmem, vmem, anywhere]
+        + [anywhere] * (len(arrays) + len(beside)),
+        out_specs=[anywhere, anywhere, vmem, vmem] + [anywhere] * len(beside[:1]),
         scratch_shapes=[
             pltpu.VMEM(tok.shape, BF16),
             pltpu.VMEM((CAP, count * PAD), BF16),
@@ -484,11 +499,13 @@
             pltpu.SemaphoreType.DMA(()),
             pltpu.SemaphoreType.DMA((PIECES, 2)),
             pltpu.SemaphoreType.DMA((steps,)),
-        ],
+        ]
+        + [pltpu.VMEM((len(beside),) + b.shape, BF16) for b in beside[:1]]
+        + [pltpu.SemaphoreType.DMA((2, len(beside))) for _ in beside[:1]],
         compiler_params=params(),
         cost_estimate=cost(18, 14),
         name="expert",
-    )(place, slots, gates, small, tok, *arrays)
+    )(place, slots, gates, small, tok, *arrays, *beside)
 
 
 def norm_back(inner, xhat, rstd):
@@ -692,7 +709,7 @@
         depth = keep.shape[2]
         for pos in range(PIECES):
             for d in range(parts):
-                owner = lax.rem(place[0] + parts - d, parts) * PIECES
+                owner = jnp.bitwise_xor(place[0], d) * PIECES
                 row = pl.multiple_of((owner + jnp.bitwise_xor(place[1], offset_of(pos))) * depth, depth)
                 out = keep if pos < PIECES // 2 else send
                 spot = pos % (PIECES // 2)
@@ -842,6 +859,9 @@
     def along(value, shift):
         return lax.ppermute(value, "group", [(i, (i + shift) % n_group) for i in range(n_group)])
 
+    def between(value, bit):
+        return lax.ppermute(value, "group", [(i, i ^ bit) for i in range(n_group)])
+
     def plus(*values):
         return sum(v.astype(F32) for v in values).astype(BF16)
 
@@ -880,9 +900,6 @@
         seats.transpose(0, 2, 1), ((0, 0), (0, size - length), (0, 8 - n_group)), constant_values=-1
     )
 
-    def collected(pieces):
-        return ("collect", [(p, ()) for p in pieces])
-
     def sources(pos, side):
         return pos // (PIECES // 2), (pos % (PIECES // 2), side)
 
@@ -905,47 +922,45 @@
     spread_1 = spread(expert_z[1])
     piece, expert_z[1] = join(piece, expert_z[1])
     expert_z[2] = along(piece, 2)
+    images, slots_lane, slots_row = join(images, slots_lane, slots_row)
     qkv, att, res, lse, tok, gates, full, small = forward_call(place, images, cotangent, dense, own_table)
     tok, gates, small, piece, spread_1, expert_z = join(tok, gates, small, piece, spread_1, expert_z)
     tables = (slots_lane, gates, small)
 
-    half, = blend_call(collected(spread_1))
-    weights = (half, across(half, 1))
     spread_2 = spread(expert_z[2])
     expert_z[3] = along(piece, 3)
-    outs[0] = expert_call(0, place, tok, *tables, ((expert_inner, expert_outer), None))
-    outs, tok, weights, spread_2, expert_z = join(outs, tok, weights, spread_2, expert_z)
-
+    outs[0] = expert_call(0, place, tok, *tables, ((expert_inner, expert_outer), None), spread_1)
+    outs, tok, spread_2, expert_z = join(outs, tok, spread_2, expert_z)
+
+    weights = (outs[0][4], across(outs[0][4], 1))
     cores[0] = across(outs[0][1], 1)
-    half, = blend_call(collected(spread_2))
-    weights_2 = (half, across(half, 1))
     spread_3 = spread(expert_z[3])
-    outs[1] = expert_call(1, place, tok, *tables, (weights, sources))
-    outs, tok, cores, weights_2, spread_3 = join(outs, tok, cores, weights_2, spread_3)
-
+    outs[1] = expert_call(1, place, tok, *tables, (weights, sources), spread_2)
+    outs, tok, cores, spread_3 = join(outs, tok, cores, spread_3)
+
+    weights = (outs[1][4], across(outs[1][4], 1))
     cores[1] = across(outs[1][1], 1)
-    half, *parts = blend_call(collected(spread_3), *quarters(0))
-    weights_3 = (half, across(half, 1))
-    chips[0] = send_chips(parts)
-    outs[2] = expert_call(2, place, tok, *tables, (weights_2, sources))
-    outs, tok, cores, chips, weights_3 = join(outs, tok, cores, chips, weights_3)
-
+    chips[0] = send_chips(blend_call(*quarters(0)))
+    outs[2] = expert_call(2, place, tok, *tables, (weights, sources), spread_3)
+    outs, tok, cores, chips = join(outs, tok, cores, chips)
+
+    weights = (outs[2][4], across(outs[2][4], 1))
     cores[2] = across(outs[2][1], 1)
     chips[1] = send_chips(blend_call(*quarters(1)))
-    outs[3] = expert_call(3, place, tok, *tables, (weights_3, sources))
+    outs[3] = expert_call(3, place, tok, *tables, (weights, sources))
     outs, cores, chips, shards = join(outs, cores, chips, shards)
 
     cores[3] = across(outs[3][1], 1)
     chips[2] = send_chips(blend_call(*quarters(2)))
     pairs = [outs[k][2] for k in range(n_group)]
     biases = [outs[k][3] for k in range(n_group)]
-    block_out, gres, gatt, late, shards[0], shards[1] = combine_call(
-        (own_quarter(0), own_quarter(1)), place, cotangent, att, res, tok, slots_row, full, small, pairs, biases
-    )
-    gres, gatt, late, cores, chips, shards = join(gres, gatt, late, cores, chips, shards)
-
-    *parts, shards[2] = blend_call(*quarters(3), own_quarter(2))
+    block_out, gres, gatt, late, shards[0], shards[1], *parts = combine_call(
+        (own_quarter(0), own_quarter(1), *quarters(3)), place, cotangent, att, res, tok, slots_row, full, small, pairs, biases
+    )
+    gres, gatt, late, cores, chips, shards, parts = join(gres, gatt, late, cores, chips, shards, parts)
+
     chips[3] = send_chips(parts)
+    shards[2], = blend_call(own_quarter(2))
     passed = along(rest_of_replicas(shards.pop(2)), 1)
     for k in range(2):
         shards[k] = send_shard(k, shards[k])
@@ -963,8 +978,8 @@
     total, = blend_call(("sum", [(v, ()) for v in shards.values()]))
     value, total = join(value, total)
     own_half = spread(total)
-    value = plus(*([value[0]] + [along(value[d], -d) for d in range(1, n_group)]))
-    value, own_half = join(value, own_half)
+    value = plus(value[:2], between(value[2:], 2))
+    value = plus(value[0], between(value[1], 1))
     value = spread(value)
     other_half = [across(v, 1) for v in own_half]
     grads = finish_call(0, place, own_half)

time: 317 us -> 303 us (0.956)
  Pallas kernels: 175 us -> 169 us
  waiting for transfers between devices: 63.7 us -> 60.1 us
    pallas_call x8 -> x6, Pallas kernels: 24.9 us -> 16.3 us  [blend_call(): pl.pallas_call(functools.partial(blend_kernel, jobs=plan, count_in=len(ar...]
    ppermute x12 -> x9, starting transfers between devices: 20.9 us -> 15 us  [along(): lax.ppermute(value, 'group', [(i, (i + shift) % n_group) for i in range(n...]
    ppermute x50, waiting for transfers between devices: 52 us -> 46.3 us  [across(): lax.ppermute(value, 'replica', [(i, i ^ bit) for i in range(n_replica)])]
    ppermute x0 -> x2, waiting for transfers between devices: none -> 3.28 us  [between(): return lax.ppermute(value, 'group', [(i, i ^ bit) for i in range(n_group)])]
    ppermute x0 -> x2, starting transfers between devices: none -> 3.22 us  [between(): return lax.ppermute(value, 'group', [(i, i ^ bit) for i in range(n_group)])]
    ppermute x12 -> x9, waiting for transfers between devices: 11.7 us -> 10.6 us  [along(): lax.ppermute(value, 'group', [(i, (i + shift) % n_group) for i in range(n...]
  transfers between devices with their start and end apart: 62 -> 61, of which waited for: 24 -> 18; matrix products, arithmetic and copies ran while one was open for 1% -> 1% of each run, Pallas kernels for 53% -> 55%
where the time goes in v4:
time: 303 us; the launch traced here: 299 us
  Pallas kernels  169 us (56%)
  starting transfers between devices  60.1 us (20%)
  waiting for transfers between devices  60.1 us (20%)
  other arithmetic  3.96 us (1%)
  local copies, waits for them, and re-layouts  3.35 us (1%)
    pallas_call x4, Pallas kernels, expert_call(): pl.pallas_call(functools.partial(expert_kernel, turn=turn, sources=source...  78 us
    ppermute x50, waiting for transfers between devices, across(): lax.ppermute(value, 'replica', [(i, i ^ bit) for i in range(n_replica)])  46.3 us
    ppermute x50, starting transfers between devices, across(): lax.ppermute(value, 'replica', [(i, i ^ bit) for i in range(n_replica)])  41.8 us
    pallas_call x1, Pallas kernels, backward_call(): pl.pallas_call(backward_kernel, out_shape=outs, grid_spec=pltpu.PrefetchS...  22.5 us
    pallas_call x1, Pallas kernels, combine_call(): pl.pallas_call(functools.partial(combine_kernel, turns=turns, jobs=plan,...  20.8 us
    pallas_call x6, Pallas kernels, blend_call(): pl.pallas_call(functools.partial(blend_kernel, jobs=plan, count_in=len(ar...  16.3 us
    pallas_call x1, Pallas kernels, forward_call(): pl.pallas_call(forward_kernel, out_shape=outs, grid_spec=pltpu.PrefetchSc...  16.1 us
    ppermute x9, starting transfers between devices, along(): lax.ppermute(value, 'group', [(i, (i + shift) % n_group) for i in range(n...  15 us
  transfers between devices with their start and end apart: 61, of which 18 were waited for; matrix products, arithmetic and copies ran while one was open for 1% of the time, Pallas kernels for 55%

profile of v4, /device:TPU:0, one launch (start us, length us, event | category | flops | bytes accessed | tf_op | source)
XLA Modules:
  0.0 298.5 jit_solution(16992317475758674788)
XLA Ops:
  4.0 3.1 %collective-permute-start = (bf16[16,2176]{1,0:T(8,128)(2,1)}, bf16[16,2176]{1,0:T(8,128)(2,1)S(1)}, u32[]{:S(2)}, u32[]{:S(2)}) collective-permute-start(bf16[16,2176]{1,0:T(8,128)(2,1)} %get-tuple-element.191), channel_id=1, source_target_pairs={{0,1},{1,2},{2,3},{3,0},{4,5},{5,6},{6,7},{7,4},{8,9},{9,10},{10,1... | collective-permute-start | bytes 208904 | tf_op jit(solution)/shard_map/ppermute | solution.py:860
  11.0 2.6 cut_own.1
  20.1 4.6 %collective-permute-done.3.refs_1_ = bf16[3,16,2176]{2,1,0:T(8,128)(2,1)S(1)} collective-permute-done((bf16[3,16,2176]{2,1,0:T(8,128)(2,1)S(1)}, bf16[3,16,2176]{2,1,0:T(8,128)(2,1)S(1)}, u32[]{:S(2)}, u32[]{:S(2)}) %collective-permute-start.3) | collective-permute-done | bytes 208928 | tf_op jit(solution)/shard_map/ppermute | solution.py:857
  24.7 4.2 %collective-permute-done.4.refs_2_ = bf16[3,16,2176]{2,1,0:T(8,128)(2,1)S(1)} collective-permute-done((bf16[3,16,2176]{2,1,0:T(8,128)(2,1)S(1)}, bf16[3,16,2176]{2,1,0:T(8,128)(2,1)S(1)}, u32[]{:S(2)}, u32[]{:S(2)}) %collective-permute-start.4) | collective-permute-done | bytes 208928 | tf_op jit(solution)/shard_map/ppermute | solution.py:857
  35.6 16.1 %attention_forward.1 = (bf16[5,208,1536]{2,1,0:T(8,128)(2,1)}, bf16[5,208,512]{2,1,0:T(8,128)(2,1)}, f32[5,208,512]{2,1,0:T(8,128)}, f32[5,208,128]{2,1,0:T(8,12...) custom-call(s32[4]{0:T(128)} %pad_add_fusion.place, ...), custom_call_target="tpu_custom_call" | custom-call | flops 13200000000 | bytes 12582912 | tf_op jit(solution)/shard_map/attention_forward/pallas_call | solution.py:242
  51.8 6.0 %collective-permute-done.13.refs_5_ = bf16[2,256,512]{2,1,0:T(8,128)(2,1)} collective-permute-done((bf16[2,256,512]{2,1,0:T(8,128)(2,1)S(1)}, bf16[2,256,512]{2,1,0:T(8,128)(2,1)}, u32[]{:S(2)}, u32[]{:S(2)}) %collective-permute-start.13) | collective-permute-done | bytes 524320 | tf_op jit(solution)/shard_map/ppermute | solution.py:857
  63.5 19.5 %expert.4 = (bf16[2,2,2,256,512]{4,3,2,1,0:T(8,128)(2,1)}, bf16[2,2,2,256,512]{4,3,2,1,0:T(8,128)(2,1)}, bf16[640,1024]{1,0:T(8,128)(2,1)}, f32[32,128]{1,0:T(8,128)}, bf16[4,2,256,512]{3,2,1,0:T(8,128)(2,1)}) custom-call(s32[4]{0:T(128)} %pad_add_fusion.place, s32[5,8,256]{2,1,0:T(8,128)} %pad.8.slots, f32[5,8,256]{2,1,0:T(8,128)} %get-tuple-element.204.gates, ...), custom_call_target="tpu_custom_call" | custom-call | flops 19800000512 | bytes 14680064 | tf_op jit(solution)/shard_map/expert/pallas_call | solution.py:476
  87.8 19.8 %expert.5 = (bf16[2,2,2,256,512]{4,3,2,1,0:T(8,128)(2,1)}, bf16[2,2,2,256,512]{4,3,2,1,0:T(8,128)(2,1)}, bf16[640,1024]{1,0:T(8,128)(2,1)}, f32[32,128]{1,0:T(8,128)}, bf16[4,2,256,512]{3,2,1,0:T(8,128)(2,1)}) custom-call(s32[4]{0:T(128)} %pad_add_fusion.place, s32[5,8,256]{2,1,0:T(8,128)} %pad.8.slots, f32[5,8,256]{2,1,0:T(8,128)} %get-tuple-element.204.gates, ...), custom_call_target="tpu_custom_call" | custom-call | flops 19800000512 | bytes 14680064 | tf_op jit(solution)/shard_map/expert/pallas_call | solution.py:476
  110.2 2.8 blend.6
  116.6 19.6 %expert.6 = (bf16[2,2,2,256,512]{4,3,2,1,0:T(8,128)(2,1)}, bf16[2,2,2,256,512]{4,3,2,1,0:T(8,128)(2,1)}, bf16[640,1024]{1,0:T(8,128)(2,1)}, f32[32,128]{1,0:T(8,128)}, bf16[4,2,256,512]{3,2,1,0:T(8,128)(2,1)}) custom-call(s32[4]{0:T(128)} %pad_add_fusion.place, s32[5,8,256]{2,1,0:T(8,128)} %pad.8.slots, f32[5,8,256]{2,1,0:T(8,128)} %get-tuple-element.204.gates, ...), custom_call_target="tpu_custom_call" | custom-call | flops 19800000512 | bytes 14680064 | tf_op jit(solution)/shard_map/expert/pallas_call | solution.py:476
  139.8 2.8 blend.7
  146.2 19.2 %expert.7 = (bf16[2,2,2,256,512]{4,3,2,1,0:T(8,128)(2,1)}, bf16[2,2,2,256,512]{4,3,2,1,0:T(8,128)(2,1)}, bf16[640,1024]{1,0:T(8,128)(2,1)}, f32[32,128]{1,0:T(8,128)}) custom-call(s32[4]{0:T(128)} %pad_add_fusion.place, s32[5,8,256]{2,1,0:T(8,128)} %pad.8.slots, f32[5,8,256]{2,1,0:T(8,128)} %get-tuple-element.204.gates, ...), custom_call_target="tpu_custom_call" | custom-call | flops 19800000512 | bytes 14680064 | tf_op jit(solution)/shard_map/expert/pallas_call | solution.py:476
  165.4 3.4 %collective-permute-done.32.refs_23_ = bf16[2,256,512]{2,1,0:T(8,128)(2,1)S(1)} collective-permute-done((bf16[2,256,512]{2,1,0:T(8,128)(2,1)}, bf16[2,256,512]{2,1,0:T(8,128)(2,1)S(1)}, u32[]{:S(2)}, u32[]{:S(2)}) %collective-permute-start.32) | collective-permute-done | bytes 524320 | tf_op jit(solution)/shard_map/ppermute | solution.py:857
  168.8 3.1 %blend.8 = (bf16[2,256,512]{2,1,0:T(8,128)(2,1)}, bf16[2,256,512]{2,1,0:T(8,128)(2,1)}, bf16[2,256,512]{2,1,0:T(8,128)(2,1)}) custom-call(bf16[2,2,2,256,512]{4,3,2,1,0:T(8,128)(2,1)} %get-tuple-element.309.refs_0_, bf16[2,2,2,256,512]{4,3,2,1,0:T(8,128)(2,1)} %collective-permute-done.30.refs_1_), custom_call_target="tpu_custom_call" | custom-call | flops 3300000000 | bytes 3145728 | tf_op jit(solution)/shard_map/blend/pallas_call | solution.py:345
  175.5 20.8 %combine.1 = (bf16[5,197,512]{2,1,0:T(8,128)(2,1)}, f32[5,208,512]{2,1,0:T(8,128)}, bf16[5,208,512]{2,1,0:T(8,128)(2,1)}, bf16[512,640]{1,0:T(8,128)(2,1)}, bf16...) custom-call(s32[4]{0:T(128)} %pad_add_fusion.place, ...), custom_call_target="tpu_custom_call" | custom-call | flops 19800000512 | bytes 14680064 | tf_op jit(solution)/shard_map/combine/pallas_call | solution.py:620
  206.5 22.5 %attention_backward.1 = (f32[5,197,512]{2,1,0:T(8,128)}, bf16[4,4,16,2176]{3,2,1,0:T(8,128)(2,1)}, bf16[4,4,16,2176]{3,2,1,0:T(8,128)(2,1)}) custom-call(s32[4]{0:T(128)} %pad_add_fusion.place, bf16[5,197,512]{2,1,0:T(8,128)(2,1)} %images.1, bf16[5,208,1536]{2,1,0:T(8,128)(2,1)} %get-tuple-element.303.qkv, f32[5,208,128]{2,1,0:T(8,128)} %get-tuple-element.304.lse, ...), custom_call_target="tpu_custom_call" | custom-call | flops 24199999488 | bytes 14680064 | tf_op jit(solution)/shard_map/attention_backward/pallas_call | solution.py:726
  229.9 2.8 blend.10
  239.3 9.5 %collective-permute-done.47.refs_2_ = bf16[2,256,512]{2,1,0:T(8,128)(2,1)} collective-permute-done((bf16[2,256,512]{2,1,0:T(8,128)(2,1)}, bf16[2,256,512]{2,1,0:T(8,128)(2,1)}, u32[]{:S(2)}, u32[]{:S(2)}) %collective-permute-start.47) | collective-permute-done | bytes 524320 | tf_op jit(solution)/shard_map/ppermute | solution.py:860
  252.4 3.2 %collective-permute-start.48 = (bf16[2,16,2176]{2,1,0:T(8,128)(2,1)S(1)}, bf16[2,16,2176]{2,1,0:T(8,128)(2,1)S(1)}, u32[]{:S(2)}, u32[]{:S(2)}) collective-permute-start(bf16[2,16,2176]{2,1,0:T(8,128)(2,1)S(1)} %slice.29), channel_id=1, source_target_pairs={{0,2},{1,3},{2,0},{3,1},{4,6},{5,7},{6,4},{7,5},{8,10},{9,11},{10,... | collective-permute-start | bytes 417800 | tf_op jit(solution)/shard_map/ppermute | solution.py:863
  259.1 3.3 %collective-permute-done.48 = bf16[2,16,2176]{2,1,0:T(8,128)(2,1)S(1)} collective-permute-done((bf16[2,16,2176]{2,1,0:T(8,128)(2,1)S(1)}, bf16[2,16,2176]{2,1,0:T(8,128)(2,1)S(1)}, u32[]{:S(2)}, u32[]{:S(2)}) %collective-permute-start.48) | collective-permute-done | bytes 139296 | tf_op jit(solution)/shard_map/ppermute | solution.py:863
  262.6 8.0 %collective-permute-done.54.refs_1_ = bf16[2,256,512]{2,1,0:T(8,128)(2,1)S(1)} collective-permute-done((bf16[2,256,512]{2,1,0:T(8,128)(2,1)}, bf16[2,256,512]{2,1,0:T(8,128)(2,1)S(1)}, u32[]{:S(2)}, u32[]{:S(2)}) %collective-permute-start.54) | collective-permute-done | bytes 524320 | tf_op jit(solution)/shard_map/ppermute | solution.py:857
  270.6 10.7 %collective-permute-done.56.refs_2_ = bf16[2,256,512]{2,1,0:T(8,128)(2,1)S(1)} collective-permute-done((bf16[2,256,512]{2,1,0:T(8,128)(2,1)}, bf16[2,256,512]{2,1,0:T(8,128)(2,1)S(1)}, u32[]{:S(2)}, u32[]{:S(2)}) %collective-permute-start.56) | collective-permute-done | bytes 524320 | tf_op jit(solution)/shard_map/ppermute | solution.py:857
  282.4 3.9 %finish_experts.2 = (f32[1,512,2048]{2,1,0:T(8,128)}, f32[1,2048,512]{2,1,0:T(8,128)}) custom-call(s32[4]{0:T(128)} %pad_add_fusion.place, bf16[2,256,512]{2,1,0:T(8,128)(2,1)} %blend.11.refs_0_, bf16[2,256,512]{2,1,0:T(8,128)(2,1)} %copy-done.22, bf16[2,256,512]{2,1,0:T(8,128)(2,1)} %copy-done.18, bf16[2,256,512]{2,1,0:T(8,128)(2,1)} %copy-done.19), custom_call_target="tpu_custom_call" | custom-call | flops 4400000000 | bytes 6291456 | tf_op jit(solution)/shard_map/finish_experts/pallas_call | solution.py:774
  289.5 3.9 %finish_experts.3 = (f32[1,512,2048]{2,1,0:T(8,128)}, f32[1,2048,512]{2,1,0:T(8,128)}) custom-call(s32[4]{0:T(128)} %pad_add_fusion.place, bf16[2,256,512]{2,1,0:T(8,128)(2,1)} %collective-permute-done.53.refs_0_, bf16[2,256,512]{2,1,0:T(8,128)(2,1)} %collective-permute-done.55.refs_1_, ...), custom_call_target="tpu_custom_call", output_to_operand_aliasing={{0}: (5, {}), {1}: (6, {})} | custom-call | flops 4400000000 | bytes 6291456 | tf_op jit(solution)/shard_map/finish_experts/pallas_call | solution.py:774
  (191 shorter events, 80.7 us)
Async XLA Ops:
  31.3 26.5 %collective-permute-start.14 = (bf16[2,256,512]{2,1,0:T(8,128)(2,1)S(1)}, bf16[2,256,512]{2,1,0:T(8,128)(2,1)S(1)}, u32[]{:S(2)}, u32[]{:S(2)}) collective-permute-start(bf16[2,256,512]{2,1,0:T(8,128)(2,1)S(1)} %copy-done.4), channel_id=1, source_target_pairs={{0,2},{1,3},{2,0},{3,1},{4,6},{5,7},{6,4},{7,5},{8,10},{9,11},{10,... | collective-permute-start | bytes 1572872 | tf_op jit(solution)/shard_map/ppermute | solution.py:860
  33.9 23.9 %collective-permute-start.13 = (bf16[2,256,512]{2,1,0:T(8,128)(2,1)S(1)}, bf16[2,256,512]{2,1,0:T(8,128)(2,1)}, u32[]{:S(2)}, u32[]{:S(2)}) collective-permute-start(bf16[2,256,512]{2,1,0:T(8,128)(2,1)S(1)} %collective-permute-done.10.refs_2_), channel_id=1, source_target_pairs={{0,24},{4,28},{8,16},{12,20},{16,8},{20,12},{24,0},{28,4},{1,25},{... | collective-permute-start | bytes 1572872 | tf_op jit(solution)/shard_map/ppermute | solution.py:857
  57.7 25.3 %collective-permute-start.15 = (bf16[2,256,512]{2,1,0:T(8,128)(2,1)S(1)}, bf16[2,256,512]{2,1,0:T(8,128)(2,1)}, u32[]{:S(2)}, u32[]{:S(2)}) collective-permute-start(bf16[2,256,512]{2,1,0:T(8,128)(2,1)S(1)} %collective-permute-done.14.refs_2_), channel_id=1, source_target_pairs={{0,8},{4,12},{8,0},{12,4},{16,24},{20,28},{24,16},{28,20},{1,9},{5... | collective-permute-start | bytes 1572872 | tf_op jit(solution)/shard_map/ppermute | solution.py:857
  58.8 24.3 %collective-permute-start.16 = (bf16[2,256,512]{2,1,0:T(8,128)(2,1)S(1)}, bf16[2,256,512]{2,1,0:T(8,128)(2,1)}, u32[]{:S(2)}, u32[]{:S(2)}) collective-permute-start(bf16[2,256,512]{2,1,0:T(8,128)(2,1)S(1)} %collective-permute-done.14.refs_2_), channel_id=1, source_target_pairs={{0,16},{4,20},{8,24},{12,28},{16,0},{20,4},{24,8},{28,12},{1,17},{... | collective-permute-start | bytes 1572872 | tf_op jit(solution)/shard_map/ppermute | solution.py:857
  83.3 26.3 %collective-permute-start.20 = (bf16[2,2,2,256,512]{4,3,2,1,0:T(8,128)(2,1)}, bf16[2,2,2,256,512]{4,3,2,1,0:T(8,128)(2,1)}, u32[]{:S(2)}, u32[]{:S(2)}) collective-permute-start(bf16[2,2,2,256,512]{4,3,2,1,0:T(8,128)(2,1)} %get-tuple-element.219), channel_id=1, source_target_pairs={{0,4},{4,0},{8,12},{12,8},{16,20},{20,16},{24,28},{28,24},{1,5},{5... | collective-permute-start | bytes 6291464 | tf_op jit(solution)/shard_map/ppermute | solution.py:857
  83.8 23.8 %collective-permute-start.21 = (bf16[2,256,512]{2,1,0:T(8,128)(2,1)S(1)}, bf16[2,256,512]{2,1,0:T(8,128)(2,1)S(1)}, u32[]{:S(2)}, u32[]{:S(2)}) collective-permute-start(bf16[2,256,512]{2,1,0:T(8,128)(2,1)S(1)} %collective-permute-done.18.refs_2_), channel_id=1, source_target_pairs={{0,8},{4,12},{8,0},{12,4},{16,24},{20,28},{24,16},{28,20},{1,9},{5... | collective-permute-start | bytes 1572872 | tf_op jit(solution)/shard_map/ppermute | solution.py:857
  84.7 24.9 %collective-permute-start.22 = (bf16[2,256,512]{2,1,0:T(8,128)(2,1)S(1)}, bf16[2,256,512]{2,1,0:T(8,128)(2,1)S(1)}, u32[]{:S(2)}, u32[]{:S(2)}) collective-permute-start(bf16[2,256,512]{2,1,0:T(8,128)(2,1)S(1)} %collective-permute-done.18.refs_2_), channel_id=1, source_target_pairs={{0,16},{4,20},{8,24},{12,28},{16,0},{20,4},{24,8},{28,12},{1,17},{... | collective-permute-start | bytes 1572872 | tf_op jit(solution)/shard_map/ppermute | solution.py:857
  86.1 23.5 %collective-permute-start.23 = (bf16[2,256,512]{2,1,0:T(8,128)(2,1)S(1)}, bf16[2,256,512]{2,1,0:T(8,128)(2,1)}, u32[]{:S(2)}, u32[]{:S(2)}) collective-permute-start(bf16[2,256,512]{2,1,0:T(8,128)(2,1)S(1)} %collective-permute-done.18.refs_2_), channel_id=1, source_target_pairs={{0,24},{4,28},{8,16},{12,20},{16,8},{20,12},{24,0},{28,4},{1,25},{... | collective-permute-start | bytes 1572872 | tf_op jit(solution)/shard_map/ppermute | solution.py:857
  109.7 29.6 %collective-permute-start.25 = (bf16[2,2,2,256,512]{4,3,2,1,0:T(8,128)(2,1)}, bf16[2,2,2,256,512]{4,3,2,1,0:T(8,128)(2,1)}, u32[]{:S(2)}, u32[]{:S(2)}) collective-permute-start(bf16[2,2,2,256,512]{4,3,2,1,0:T(8,128)(2,1)} %get-tuple-element.238), channel_id=1, source_target_pairs={{0,4},{4,0},{8,12},{12,8},{16,20},{20,16},{24,28},{28,24},{1,5},{5... | collective-permute-start | bytes 6291464 | tf_op jit(solution)/shard_map/ppermute | solution.py:857
  114.3 23.6 %collective-permute-start.27 = (bf16[2,256,512]{2,1,0:T(8,128)(2,1)}, bf16[2,256,512]{2,1,0:T(8,128)(2,1)S(1)}, u32[]{:S(2)}, u32[]{:S(2)}) collective-permute-start(bf16[2,256,512]{2,1,0:T(8,128)(2,1)} %get-tuple-element.254), channel_id=1, source_target_pairs={{0,16},{4,20},{8,24},{12,28},{16,0},{20,4},{24,8},{28,12},{1,17},{... | collective-permute-start | bytes 1572872 | tf_op jit(solution)/shard_map/ppermute | solution.py:857
  115.1 24.1 %collective-permute-start.28 = (bf16[2,256,512]{2,1,0:T(8,128)(2,1)}, bf16[2,256,512]{2,1,0:T(8,128)(2,1)S(1)}, u32[]{:S(2)}, u32[]{:S(2)}) collective-permute-start(bf16[2,256,512]{2,1,0:T(8,128)(2,1)} %get-tuple-element.255), channel_id=1, source_target_pairs={{0,24},{4,28},{8,16},{12,20},{16,8},{20,12},{24,0},{28,4},{1,25},{... | collective-permute-start | bytes 1572872 | tf_op jit(solution)/shard_map/ppermute | solution.py:857
  139.3 29.4 %collective-permute-start.30 = (bf16[2,2,2,256,512]{4,3,2,1,0:T(8,128)(2,1)}, bf16[2,2,2,256,512]{4,3,2,1,0:T(8,128)(2,1)}, u32[]{:S(2)}, u32[]{:S(2)}) collective-permute-start(bf16[2,2,2,256,512]{4,3,2,1,0:T(8,128)(2,1)} %get-tuple-element.266), channel_id=1, source_target_pairs={{0,4},{4,0},{8,12},{12,8},{16,20},{20,16},{24,28},{28,24},{1,5},{5... | collective-permute-start | bytes 6291464 | tf_op jit(solution)/shard_map/ppermute | solution.py:857
  143.7 25.1 %collective-permute-start.32 = (bf16[2,256,512]{2,1,0:T(8,128)(2,1)}, bf16[2,256,512]{2,1,0:T(8,128)(2,1)S(1)}, u32[]{:S(2)}, u32[]{:S(2)}) collective-permute-start(bf16[2,256,512]{2,1,0:T(8,128)(2,1)} %get-tuple-element.280), channel_id=1, source_target_pairs={{0,16},{4,20},{8,24},{12,28},{16,0},{20,4},{24,8},{28,12},{1,17},{... | collective-permute-start | bytes 1572872 | tf_op jit(solution)/shard_map/ppermute | solution.py:857
  145.1 23.7 %collective-permute-start.33 = (bf16[2,256,512]{2,1,0:T(8,128)(2,1)}, bf16[2,256,512]{2,1,0:T(8,128)(2,1)S(1)}, u32[]{:S(2)}, u32[]{:S(2)}) collective-permute-start(bf16[2,256,512]{2,1,0:T(8,128)(2,1)} %get-tuple-element.281), channel_id=1, source_target_pairs={{0,24},{4,28},{8,16},{12,20},{16,8},{20,12},{24,0},{28,4},{1,25},{... | collective-permute-start | bytes 1572872 | tf_op jit(solution)/shard_map/ppermute | solution.py:857
  171.9 24.4 %collective-permute-start.35 = (bf16[2,256,512]{2,1,0:T(8,128)(2,1)}, bf16[2,256,512]{2,1,0:T(8,128)(2,1)S(1)}, u32[]{:S(2)}, u32[]{:S(2)}) collective-permute-start(bf16[2,256,512]{2,1,0:T(8,128)(2,1)} %get-tuple-element.310), channel_id=1, source_target_pairs={{0,8},{4,12},{8,0},{12,4},{16,24},{20,28},{24,16},{28,20},{1,9},{5... | collective-permute-start | bytes 1572872 | tf_op jit(solution)/shard_map/ppermute | solution.py:857
  173.0 24.0 %collective-permute-start.36 = (bf16[2,256,512]{2,1,0:T(8,128)(2,1)}, bf16[2,256,512]{2,1,0:T(8,128)(2,1)S(1)}, u32[]{:S(2)}, u32[]{:S(2)}) collective-permute-start(bf16[2,256,512]{2,1,0:T(8,128)(2,1)} %get-tuple-element.311), channel_id=1, source_target_pairs={{0,16},{4,20},{8,24},{12,28},{16,0},{20,4},{24,8},{28,12},{1,17},{... | collective-permute-start | bytes 1572872 | tf_op jit(solution)/shard_map/ppermute | solution.py:857
  174.1 24.3 %collective-permute-start.37 = (bf16[2,256,512]{2,1,0:T(8,128)(2,1)}, bf16[2,256,512]{2,1,0:T(8,128)(2,1)S(1)}, u32[]{:S(2)}, u32[]{:S(2)}) collective-permute-start(bf16[2,256,512]{2,1,0:T(8,128)(2,1)} %get-tuple-element.312), channel_id=1, source_target_pairs={{0,24},{4,28},{8,16},{12,20},{16,8},{20,12},{24,0},{28,4},{1,25},{... | collective-permute-start | bytes 1572872 | tf_op jit(solution)/shard_map/ppermute | solution.py:857
  198.3 30.7 %collective-permute-start.38 = (bf16[2,256,512]{2,1,0:T(8,128)(2,1)}, bf16[2,256,512]{2,1,0:T(8,128)(2,1)}, u32[]{:S(2)}, u32[]{:S(2)}) collective-permute-start(bf16[2,256,512]{2,1,0:T(8,128)(2,1)} %get-tuple-element.327), channel_id=1, source_target_pairs={{0,8},{4,12},{8,0},{12,4},{16,24},{20,28},{24,16},{28,20},{1,9},{5... | collective-permute-start | bytes 1572872 | tf_op jit(solution)/shard_map/ppermute | solution.py:857
  199.3 29.8 %collective-permute-start.39 = (bf16[2,256,512]{2,1,0:T(8,128)(2,1)}, bf16[2,256,512]{2,1,0:T(8,128)(2,1)}, u32[]{:S(2)}, u32[]{:S(2)}) collective-permute-start(bf16[2,256,512]{2,1,0:T(8,128)(2,1)} %get-tuple-element.328), channel_id=1, source_target_pairs={{0,16},{4,20},{8,24},{12,28},{16,0},{20,4},{24,8},{28,12},{1,17},{... | collective-permute-start | bytes 1572872 | tf_op jit(solution)/shard_map/ppermute | solution.py:857
  200.7 28.3 %collective-permute-start.40 = (bf16[2,256,512]{2,1,0:T(8,128)(2,1)}, bf16[2,256,512]{2,1,0:T(8,128)(2,1)}, u32[]{:S(2)}, u32[]{:S(2)}) collective-permute-start(bf16[2,256,512]{2,1,0:T(8,128)(2,1)} %get-tuple-element.329), channel_id=1, source_target_pairs={{0,24},{4,28},{8,16},{12,20},{16,8},{20,12},{24,0},{28,4},{1,25},{... | collective-permute-start | bytes 1572872 | tf_op jit(solution)/shard_map/ppermute | solution.py:857
  201.8 27.2 %collective-permute-start.41 = (bf16[2,256,512]{2,1,0:T(8,128)(2,1)}, bf16[2,256,512]{2,1,0:T(8,128)(2,1)S(1)}, u32[]{:S(2)}, u32[]{:S(2)}) collective-permute-start(bf16[2,256,512]{2,1,0:T(8,128)(2,1)} %get-tuple-element.331), channel_id=1, source_target_pairs={{0,3},{1,0},{2,1},{3,2},{4,7},{5,4},{6,5},{7,6},{8,11},{9,8},{10,9... | collective-permute-start | bytes 1572872 | tf_op jit(solution)/shard_map/ppermute | solution.py:860
  256.6 24.7 %collective-permute-start.56 = (bf16[2,256,512]{2,1,0:T(8,128)(2,1)}, bf16[2,256,512]{2,1,0:T(8,128)(2,1)S(1)}, u32[]{:S(2)}, u32[]{:S(2)}) collective-permute-start(bf16[2,256,512]{2,1,0:T(8,128)(2,1)} %blend.11.refs_0_), channel_id=1, source_target_pairs={{0,16},{4,20},{8,24},{12,28},{16,0},{20,4},{24,8},{28,12},{1,17},{... | collective-permute-start | bytes 1572872 | tf_op jit(solution)/shard_map/ppermute | solution.py:857
  257.9 23.5 %collective-permute-start.58 = (bf16[2,256,512]{2,1,0:T(8,128)(2,1)}, bf16[2,256,512]{2,1,0:T(8,128)(2,1)S(1)}, u32[]{:S(2)}, u32[]{:S(2)}) collective-permute-start(bf16[2,256,512]{2,1,0:T(8,128)(2,1)} %blend.11.refs_0_), channel_id=1, source_target_pairs={{0,24},{4,28},{8,16},{12,20},{16,8},{20,12},{24,0},{28,4},{1,25},{... | collective-permute-start | bytes 1572872 | tf_op jit(solution)/shard_map/ppermute | solution.py:857
  262.5 23.9 %collective-permute-start.53 = (bf16[2,256,512]{2,1,0:T(8,128)(2,1)}, bf16[2,256,512]{2,1,0:T(8,128)(2,1)}, u32[]{:S(2)}, u32[]{:S(2)}) collective-permute-start(bf16[2,256,512]{2,1,0:T(8,128)(2,1)} %blend.11.refs_0_), channel_id=1, source_target_pairs={{0,4},{4,0},{8,12},{12,8},{16,20},{20,16},{24,28},{28,24},{1,5},{5... | collective-permute-start | bytes 1572872 | tf_op jit(solution)/shard_map/ppermute | solution.py:857
  (67 other events, 700.7 us)

commit v5 on v4

--- a/solution.py
+++ b/solution.py
@@ -978,8 +978,9 @@
     total, = blend_call(("sum", [(v, ()) for v in shards.values()]))
     value, total = join(value, total)
     own_half = spread(total)
-    value = plus(value[:2], between(value[2:], 2))
-    value = plus(value[0], between(value[1], 1))
+    value = value.reshape((2, 2) + value.shape[1:])
+    value = plus(value[:, 0], between(value[:, 1], 1))
+    value = plus(value[0], between(value[1], 2))
     value = spread(value)
     other_half = [across(v, 1) for v in own_half]
     grads = finish_call(0, place, own_half)

time: 303 us -> 301 us (level)
  no operation moved by 1% of the time
where the time goes in v5:
time: 301 us; the launch traced here: 297 us
  Pallas kernels  169 us (56%)
  starting transfers between devices  61.3 us (20%)
  waiting for transfers between devices  57.2 us (19%)
  other arithmetic  3.96 us (1%)
  local copies, waits for them, and re-layouts  3.35 us (1%)
    pallas_call x4, Pallas kernels, expert_call(): pl.pallas_call(functools.partial(expert_kernel, turn=turn, sources=source...  78 us
    ppermute x50, waiting for transfers between devices, across(): lax.ppermute(value, 'replica', [(i, i ^ bit) for i in range(n_replica)])  45.8 us
    ppermute x50, starting transfers between devices, across(): lax.ppermute(value, 'replica', [(i, i ^ bit) for i in range(n_replica)])  41.7 us
    pallas_call x1, Pallas kernels, backward_call(): pl.pallas_call(backward_kernel, out_shape=outs, grid_spec=pltpu.PrefetchS...  22.5 us
    pallas_call x1, Pallas kernels, combine_call(): pl.pallas_call(functools.partial(combine_kernel, turns=turns, jobs=plan,...  20.8 us
    pallas_call x6, Pallas kernels, blend_call(): pl.pallas_call(functools.partial(blend_kernel, jobs=plan, count_in=len(ar...  16.3 us
    pallas_call x1, Pallas kernels, forward_call(): pl.pallas_call(forward_kernel, out_shape=outs, grid_spec=pltpu.PrefetchSc...  16.1 us
    ppermute x9, starting transfers between devices, along(): lax.ppermute(value, 'group', [(i, (i + shift) % n_group) for i in range(n...  15 us
  transfers between devices with their start and end apart: 61, of which 18 were waited for; matrix products, arithmetic and copies ran while one was open for 1% of the time, Pallas kernels for 55%

profile of v5, /device:TPU:0, one launch (start us, length us, event | category | flops | bytes accessed | tf_op | source)
XLA Modules:
  0.0 296.8 jit_solution(13376579668814273361)
XLA Ops:
  4.0 3.1 %collective-permute-start = (bf16[16,2176]{1,0:T(8,128)(2,1)}, bf16[16,2176]{1,0:T(8,128)(2,1)S(1)}, u32[]{:S(2)}, u32[]{:S(2)}) collective-permute-start(bf16[16,2176]{1,0:T(8,128)(2,1)} %get-tuple-element.191), channel_id=1, source_target_pairs={{0,1},{1,2},{2,3},{3,0},{4,5},{5,6},{6,7},{7,4},{8,9},{9,10},{10,1... | collective-permute-start | bytes 208904 | tf_op jit(solution)/shard_map/ppermute | solution.py:860
  11.0 2.6 cut_own.1
  20.1 4.6 %collective-permute-done.3.refs_1_ = bf16[3,16,2176]{2,1,0:T(8,128)(2,1)S(1)} collective-permute-done((bf16[3,16,2176]{2,1,0:T(8,128)(2,1)S(1)}, bf16[3,16,2176]{2,1,0:T(8,128)(2,1)S(1)}, u32[]{:S(2)}, u32[]{:S(2)}) %collective-permute-start.3) | collective-permute-done | bytes 208928 | tf_op jit(solution)/shard_map/ppermute | solution.py:857
  24.7 4.2 %collective-permute-done.4.refs_2_ = bf16[3,16,2176]{2,1,0:T(8,128)(2,1)S(1)} collective-permute-done((bf16[3,16,2176]{2,1,0:T(8,128)(2,1)S(1)}, bf16[3,16,2176]{2,1,0:T(8,128)(2,1)S(1)}, u32[]{:S(2)}, u32[]{:S(2)}) %collective-permute-start.4) | collective-permute-done | bytes 208928 | tf_op jit(solution)/shard_map/ppermute | solution.py:857
  35.6 16.1 %attention_forward.1 = (bf16[5,208,1536]{2,1,0:T(8,128)(2,1)}, bf16[5,208,512]{2,1,0:T(8,128)(2,1)}, f32[5,208,512]{2,1,0:T(8,128)}, f32[5,208,128]{2,1,0:T(8,12...) custom-call(s32[4]{0:T(128)} %pad_add_fusion.place, ...), custom_call_target="tpu_custom_call" | custom-call | flops 13200000000 | bytes 12582912 | tf_op jit(solution)/shard_map/attention_forward/pallas_call | solution.py:242
  51.8 6.0 %collective-permute-done.13.refs_5_ = bf16[2,256,512]{2,1,0:T(8,128)(2,1)} collective-permute-done((bf16[2,256,512]{2,1,0:T(8,128)(2,1)S(1)}, bf16[2,256,512]{2,1,0:T(8,128)(2,1)}, u32[]{:S(2)}, u32[]{:S(2)}) %collective-permute-start.13) | collective-permute-done | bytes 524320 | tf_op jit(solution)/shard_map/ppermute | solution.py:857
  63.5 19.5 %expert.4 = (bf16[2,2,2,256,512]{4,3,2,1,0:T(8,128)(2,1)}, bf16[2,2,2,256,512]{4,3,2,1,0:T(8,128)(2,1)}, bf16[640,1024]{1,0:T(8,128)(2,1)}, f32[32,128]{1,0:T(8,128)}, bf16[4,2,256,512]{3,2,1,0:T(8,128)(2,1)}) custom-call(s32[4]{0:T(128)} %pad_add_fusion.place, s32[5,8,256]{2,1,0:T(8,128)} %pad.8.slots, f32[5,8,256]{2,1,0:T(8,128)} %get-tuple-element.204.gates, ...), custom_call_target="tpu_custom_call" | custom-call | flops 19800000512 | bytes 14680064 | tf_op jit(solution)/shard_map/expert/pallas_call | solution.py:476
  87.8 19.8 %expert.5 = (bf16[2,2,2,256,512]{4,3,2,1,0:T(8,128)(2,1)}, bf16[2,2,2,256,512]{4,3,2,1,0:T(8,128)(2,1)}, bf16[640,1024]{1,0:T(8,128)(2,1)}, f32[32,128]{1,0:T(8,128)}, bf16[4,2,256,512]{3,2,1,0:T(8,128)(2,1)}) custom-call(s32[4]{0:T(128)} %pad_add_fusion.place, s32[5,8,256]{2,1,0:T(8,128)} %pad.8.slots, f32[5,8,256]{2,1,0:T(8,128)} %get-tuple-element.204.gates, ...), custom_call_target="tpu_custom_call" | custom-call | flops 19800000512 | bytes 14680064 | tf_op jit(solution)/shard_map/expert/pallas_call | solution.py:476
  110.2 2.8 blend.6
  116.6 19.6 %expert.6 = (bf16[2,2,2,256,512]{4,3,2,1,0:T(8,128)(2,1)}, bf16[2,2,2,256,512]{4,3,2,1,0:T(8,128)(2,1)}, bf16[640,1024]{1,0:T(8,128)(2,1)}, f32[32,128]{1,0:T(8,128)}, bf16[4,2,256,512]{3,2,1,0:T(8,128)(2,1)}) custom-call(s32[4]{0:T(128)} %pad_add_fusion.place, s32[5,8,256]{2,1,0:T(8,128)} %pad.8.slots, f32[5,8,256]{2,1,0:T(8,128)} %get-tuple-element.204.gates, ...), custom_call_target="tpu_custom_call" | custom-call | flops 19800000512 | bytes 14680064 | tf_op jit(solution)/shard_map/expert/pallas_call | solution.py:476
  139.8 2.8 blend.7
  146.2 19.2 %expert.7 = (bf16[2,2,2,256,512]{4,3,2,1,0:T(8,128)(2,1)}, bf16[2,2,2,256,512]{4,3,2,1,0:T(8,128)(2,1)}, bf16[640,1024]{1,0:T(8,128)(2,1)}, f32[32,128]{1,0:T(8,128)}) custom-call(s32[4]{0:T(128)} %pad_add_fusion.place, s32[5,8,256]{2,1,0:T(8,128)} %pad.8.slots, f32[5,8,256]{2,1,0:T(8,128)} %get-tuple-element.204.gates, ...), custom_call_target="tpu_custom_call" | custom-call | flops 19800000512 | bytes 14680064 | tf_op jit(solution)/shard_map/expert/pallas_call | solution.py:476
  165.4 3.4 %collective-permute-done.32.refs_23_ = bf16[2,256,512]{2,1,0:T(8,128)(2,1)S(1)} collective-permute-done((bf16[2,256,512]{2,1,0:T(8,128)(2,1)}, bf16[2,256,512]{2,1,0:T(8,128)(2,1)S(1)}, u32[]{:S(2)}, u32[]{:S(2)}) %collective-permute-start.32) | collective-permute-done | bytes 524320 | tf_op jit(solution)/shard_map/ppermute | solution.py:857
  168.8 3.1 %blend.8 = (bf16[2,256,512]{2,1,0:T(8,128)(2,1)}, bf16[2,256,512]{2,1,0:T(8,128)(2,1)}, bf16[2,256,512]{2,1,0:T(8,128)(2,1)}) custom-call(bf16[2,2,2,256,512]{4,3,2,1,0:T(8,128)(2,1)} %get-tuple-element.309.refs_0_, bf16[2,2,2,256,512]{4,3,2,1,0:T(8,128)(2,1)} %collective-permute-done.30.refs_1_), custom_call_target="tpu_custom_call" | custom-call | flops 3300000000 | bytes 3145728 | tf_op jit(solution)/shard_map/blend/pallas_call | solution.py:345
  175.5 20.8 %combine.1 = (bf16[5,197,512]{2,1,0:T(8,128)(2,1)}, f32[5,208,512]{2,1,0:T(8,128)}, bf16[5,208,512]{2,1,0:T(8,128)(2,1)}, bf16[512,640]{1,0:T(8,128)(2,1)}, bf16...) custom-call(s32[4]{0:T(128)} %pad_add_fusion.place, ...), custom_call_target="tpu_custom_call" | custom-call | flops 19800000512 | bytes 14680064 | tf_op jit(solution)/shard_map/combine/pallas_call | solution.py:620
  203.6 2.6 blend.9
  206.5 22.5 %attention_backward.1 = (f32[5,197,512]{2,1,0:T(8,128)}, bf16[4,4,16,2176]{3,2,1,0:T(8,128)(2,1)}, bf16[4,4,16,2176]{3,2,1,0:T(8,128)(2,1)}) custom-call(s32[4]{0:T(128)} %pad_add_fusion.place, bf16[5,197,512]{2,1,0:T(8,128)(2,1)} %images.1, bf16[5,208,1536]{2,1,0:T(8,128)(2,1)} %get-tuple-element.303.qkv, f32[5,208,128]{2,1,0:T(8,128)} %get-tuple-element.304.lse, ...), custom_call_target="tpu_custom_call" | custom-call | flops 24199999488 | bytes 14680064 | tf_op jit(solution)/shard_map/attention_backward/pallas_call | solution.py:726
  229.9 2.8 blend.10
  239.3 9.5 %collective-permute-done.47.refs_2_ = bf16[2,256,512]{2,1,0:T(8,128)(2,1)} collective-permute-done((bf16[2,256,512]{2,1,0:T(8,128)(2,1)}, bf16[2,256,512]{2,1,0:T(8,128)(2,1)}, u32[]{:S(2)}, u32[]{:S(2)}) %collective-permute-start.47) | collective-permute-done | bytes 524320 | tf_op jit(solution)/shard_map/ppermute | solution.py:860
  257.9 3.4 %collective-permute-start.49 = (bf16[16,2176]{1,0:T(8,128)(2,1)S(1)}, bf16[16,2176]{1,0:T(8,128)(2,1)S(1)}, u32[]{:S(2)}, u32[]{:S(2)}) collective-permute-start(bf16[16,2176]{1,0:T(8,128)(2,1)S(1)} %slice_bitcast_fusion.6), channel_id=1, source_target_pairs={{0,2},{1,3},{2,0},{3,1},{4,6},{5,7},{6,4},{7,5},{8,10},{9,11},{10,... | collective-permute-start | bytes 208904 | tf_op jit(solution)/shard_map/ppermute | solution.py:863
  261.3 7.3 %collective-permute-done.54.refs_1_ = bf16[2,256,512]{2,1,0:T(8,128)(2,1)S(1)} collective-permute-done((bf16[2,256,512]{2,1,0:T(8,128)(2,1)}, bf16[2,256,512]{2,1,0:T(8,128)(2,1)S(1)}, u32[]{:S(2)}, u32[]{:S(2)}) %collective-permute-start.54) | collective-permute-done | bytes 524320 | tf_op jit(solution)/shard_map/ppermute | solution.py:857
  268.6 11.0 %collective-permute-done.56.refs_2_ = bf16[2,256,512]{2,1,0:T(8,128)(2,1)S(1)} collective-permute-done((bf16[2,256,512]{2,1,0:T(8,128)(2,1)}, bf16[2,256,512]{2,1,0:T(8,128)(2,1)S(1)}, u32[]{:S(2)}, u32[]{:S(2)}) %collective-permute-start.56) | collective-permute-done | bytes 524320 | tf_op jit(solution)/shard_map/ppermute | solution.py:857
  280.8 3.9 %finish_experts.2 = (f32[1,512,2048]{2,1,0:T(8,128)}, f32[1,2048,512]{2,1,0:T(8,128)}) custom-call(s32[4]{0:T(128)} %pad_add_fusion.place, bf16[2,256,512]{2,1,0:T(8,128)(2,1)} %blend.11.refs_0_, bf16[2,256,512]{2,1,0:T(8,128)(2,1)} %copy-done.22, bf16[2,256,512]{2,1,0:T(8,128)(2,1)} %copy-done.18, bf16[2,256,512]{2,1,0:T(8,128)(2,1)} %copy-done.19), custom_call_target="tpu_custom_call" | custom-call | flops 4400000000 | bytes 6291456 | tf_op jit(solution)/shard_map/finish_experts/pallas_call | solution.py:774
  287.7 3.9 %finish_experts.3 = (f32[1,512,2048]{2,1,0:T(8,128)}, f32[1,2048,512]{2,1,0:T(8,128)}) custom-call(s32[4]{0:T(128)} %pad_add_fusion.place, bf16[2,256,512]{2,1,0:T(8,128)(2,1)} %collective-permute-done.53.refs_0_, bf16[2,256,512]{2,1,0:T(8,128)(2,1)} %collective-permute-done.55.refs_1_, ...), custom_call_target="tpu_custom_call", output_to_operand_aliasing={{0}: (5, {}), {1}: (6, {})} | custom-call | flops 4400000000 | bytes 6291456 | tf_op jit(solution)/shard_map/finish_experts/pallas_call | solution.py:774
  (191 shorter events, 79.9 us)
Async XLA Ops:
  31.3 26.5 %collective-permute-start.14 = (bf16[2,256,512]{2,1,0:T(8,128)(2,1)S(1)}, bf16[2,256,512]{2,1,0:T(8,128)(2,1)S(1)}, u32[]{:S(2)}, u32[]{:S(2)}) collective-permute-start(bf16[2,256,512]{2,1,0:T(8,128)(2,1)S(1)} %copy-done.4), channel_id=1, source_target_pairs={{0,2},{1,3},{2,0},{3,1},{4,6},{5,7},{6,4},{7,5},{8,10},{9,11},{10,... | collective-permute-start | bytes 1572872 | tf_op jit(solution)/shard_map/ppermute | solution.py:860
  33.9 23.9 %collective-permute-start.13 = (bf16[2,256,512]{2,1,0:T(8,128)(2,1)S(1)}, bf16[2,256,512]{2,1,0:T(8,128)(2,1)}, u32[]{:S(2)}, u32[]{:S(2)}) collective-permute-start(bf16[2,256,512]{2,1,0:T(8,128)(2,1)S(1)} %collective-permute-done.10.refs_2_), channel_id=1, source_target_pairs={{0,24},{4,28},{8,16},{12,20},{16,8},{20,12},{24,0},{28,4},{1,25},{... | collective-permute-start | bytes 1572872 | tf_op jit(solution)/shard_map/ppermute | solution.py:857
  57.7 25.3 %collective-permute-start.15 = (bf16[2,256,512]{2,1,0:T(8,128)(2,1)S(1)}, bf16[2,256,512]{2,1,0:T(8,128)(2,1)}, u32[]{:S(2)}, u32[]{:S(2)}) collective-permute-start(bf16[2,256,512]{2,1,0:T(8,128)(2,1)S(1)} %collective-permute-done.14.refs_2_), channel_id=1, source_target_pairs={{0,8},{4,12},{8,0},{12,4},{16,24},{20,28},{24,16},{28,20},{1,9},{5... | collective-permute-start | bytes 1572872 | tf_op jit(solution)/shard_map/ppermute | solution.py:857
  58.8 24.3 %collective-permute-start.16 = (bf16[2,256,512]{2,1,0:T(8,128)(2,1)S(1)}, bf16[2,256,512]{2,1,0:T(8,128)(2,1)}, u32[]{:S(2)}, u32[]{:S(2)}) collective-permute-start(bf16[2,256,512]{2,1,0:T(8,128)(2,1)S(1)} %collective-permute-done.14.refs_2_), channel_id=1, source_target_pairs={{0,16},{4,20},{8,24},{12,28},{16,0},{20,4},{24,8},{28,12},{1,17},{... | collective-permute-start | bytes 1572872 | tf_op jit(solution)/shard_map/ppermute | solution.py:857
  83.3 26.3 %collective-permute-start.20 = (bf16[2,2,2,256,512]{4,3,2,1,0:T(8,128)(2,1)}, bf16[2,2,2,256,512]{4,3,2,1,0:T(8,128)(2,1)}, u32[]{:S(2)}, u32[]{:S(2)}) collective-permute-start(bf16[2,2,2,256,512]{4,3,2,1,0:T(8,128)(2,1)} %get-tuple-element.219), channel_id=1, source_target_pairs={{0,4},{4,0},{8,12},{12,8},{16,20},{20,16},{24,28},{28,24},{1,5},{5... | collective-permute-start | bytes 6291464 | tf_op jit(solution)/shard_map/ppermute | solution.py:857
  83.8 23.8 %collective-permute-start.21 = (bf16[2,256,512]{2,1,0:T(8,128)(2,1)S(1)}, bf16[2,256,512]{2,1,0:T(8,128)(2,1)S(1)}, u32[]{:S(2)}, u32[]{:S(2)}) collective-permute-start(bf16[2,256,512]{2,1,0:T(8,128)(2,1)S(1)} %collective-permute-done.18.refs_2_), channel_id=1, source_target_pairs={{0,8},{4,12},{8,0},{12,4},{16,24},{20,28},{24,16},{28,20},{1,9},{5... | collective-permute-start | bytes 1572872 | tf_op jit(solution)/shard_map/ppermute | solution.py:857
  84.7 24.9 %collective-permute-start.22 = (bf16[2,256,512]{2,1,0:T(8,128)(2,1)S(1)}, bf16[2,256,512]{2,1,0:T(8,128)(2,1)S(1)}, u32[]{:S(2)}, u32[]{:S(2)}) collective-permute-start(bf16[2,256,512]{2,1,0:T(8,128)(2,1)S(1)} %collective-permute-done.18.refs_2_), channel_id=1, source_target_pairs={{0,16},{4,20},{8,24},{12,28},{16,0},{20,4},{24,8},{28,12},{1,17},{... | collective-permute-start | bytes 1572872 | tf_op jit(solution)/shard_map/ppermute | solution.py:857
  86.1 23.5 %collective-permute-start.23 = (bf16[2,256,512]{2,1,0:T(8,128)(2,1)S(1)}, bf16[2,256,512]{2,1,0:T(8,128)(2,1)}, u32[]{:S(2)}, u32[]{:S(2)}) collective-permute-start(bf16[2,256,512]{2,1,0:T(8,128)(2,1)S(1)} %collective-permute-done.18.refs_2_), channel_id=1, source_target_pairs={{0,24},{4,28},{8,16},{12,20},{16,8},{20,12},{24,0},{28,4},{1,25},{... | collective-permute-start | bytes 1572872 | tf_op jit(solution)/shard_map/ppermute | solution.py:857
  109.7 29.6 %collective-permute-start.25 = (bf16[2,2,2,256,512]{4,3,2,1,0:T(8,128)(2,1)}, bf16[2,2,2,256,512]{4,3,2,1,0:T(8,128)(2,1)}, u32[]{:S(2)}, u32[]{:S(2)}) collective-permute-start(bf16[2,2,2,256,512]{4,3,2,1,0:T(8,128)(2,1)} %get-tuple-element.238), channel_id=1, source_target_pairs={{0,4},{4,0},{8,12},{12,8},{16,20},{20,16},{24,28},{28,24},{1,5},{5... | collective-permute-start | bytes 6291464 | tf_op jit(solution)/shard_map/ppermute | solution.py:857
  114.3 23.6 %collective-permute-start.27 = (bf16[2,256,512]{2,1,0:T(8,128)(2,1)}, bf16[2,256,512]{2,1,0:T(8,128)(2,1)S(1)}, u32[]{:S(2)}, u32[]{:S(2)}) collective-permute-start(bf16[2,256,512]{2,1,0:T(8,128)(2,1)} %get-tuple-element.254), channel_id=1, source_target_pairs={{0,16},{4,20},{8,24},{12,28},{16,0},{20,4},{24,8},{28,12},{1,17},{... | collective-permute-start | bytes 1572872 | tf_op jit(solution)/shard_map/ppermute | solution.py:857
  115.1 24.1 %collective-permute-start.28 = (bf16[2,256,512]{2,1,0:T(8,128)(2,1)}, bf16[2,256,512]{2,1,0:T(8,128)(2,1)S(1)}, u32[]{:S(2)}, u32[]{:S(2)}) collective-permute-start(bf16[2,256,512]{2,1,0:T(8,128)(2,1)} %get-tuple-element.255), channel_id=1, source_target_pairs={{0,24},{4,28},{8,16},{12,20},{16,8},{20,12},{24,0},{28,4},{1,25},{... | collective-permute-start | bytes 1572872 | tf_op jit(solution)/shard_map/ppermute | solution.py:857
  139.3 29.4 %collective-permute-start.30 = (bf16[2,2,2,256,512]{4,3,2,1,0:T(8,128)(2,1)}, bf16[2,2,2,256,512]{4,3,2,1,0:T(8,128)(2,1)}, u32[]{:S(2)}, u32[]{:S(2)}) collective-permute-start(bf16[2,2,2,256,512]{4,3,2,1,0:T(8,128)(2,1)} %get-tuple-element.266), channel_id=1, source_target_pairs={{0,4},{4,0},{8,12},{12,8},{16,20},{20,16},{24,28},{28,24},{1,5},{5... | collective-permute-start | bytes 6291464 | tf_op jit(solution)/shard_map/ppermute | solution.py:857
  143.7 25.1 %collective-permute-start.32 = (bf16[2,256,512]{2,1,0:T(8,128)(2,1)}, bf16[2,256,512]{2,1,0:T(8,128)(2,1)S(1)}, u32[]{:S(2)}, u32[]{:S(2)}) collective-permute-start(bf16[2,256,512]{2,1,0:T(8,128)(2,1)} %get-tuple-element.280), channel_id=1, source_target_pairs={{0,16},{4,20},{8,24},{12,28},{16,0},{20,4},{24,8},{28,12},{1,17},{... | collective-permute-start | bytes 1572872 | tf_op jit(solution)/shard_map/ppermute | solution.py:857
  145.1 23.7 %collective-permute-start.33 = (bf16[2,256,512]{2,1,0:T(8,128)(2,1)}, bf16[2,256,512]{2,1,0:T(8,128)(2,1)S(1)}, u32[]{:S(2)}, u32[]{:S(2)}) collective-permute-start(bf16[2,256,512]{2,1,0:T(8,128)(2,1)} %get-tuple-element.281), channel_id=1, source_target_pairs={{0,24},{4,28},{8,16},{12,20},{16,8},{20,12},{24,0},{28,4},{1,25},{... | collective-permute-start | bytes 1572872 | tf_op jit(solution)/shard_map/ppermute | solution.py:857
  171.9 24.4 %collective-permute-start.35 = (bf16[2,256,512]{2,1,0:T(8,128)(2,1)}, bf16[2,256,512]{2,1,0:T(8,128)(2,1)S(1)}, u32[]{:S(2)}, u32[]{:S(2)}) collective-permute-start(bf16[2,256,512]{2,1,0:T(8,128)(2,1)} %get-tuple-element.310), channel_id=1, source_target_pairs={{0,8},{4,12},{8,0},{12,4},{16,24},{20,28},{24,16},{28,20},{1,9},{5... | collective-permute-start | bytes 1572872 | tf_op jit(solution)/shard_map/ppermute | solution.py:857
  173.0 24.0 %collective-permute-start.36 = (bf16[2,256,512]{2,1,0:T(8,128)(2,1)}, bf16[2,256,512]{2,1,0:T(8,128)(2,1)S(1)}, u32[]{:S(2)}, u32[]{:S(2)}) collective-permute-start(bf16[2,256,512]{2,1,0:T(8,128)(2,1)} %get-tuple-element.311), channel_id=1, source_target_pairs={{0,16},{4,20},{8,24},{12,28},{16,0},{20,4},{24,8},{28,12},{1,17},{... | collective-permute-start | bytes 1572872 | tf_op jit(solution)/shard_map/ppermute | solution.py:857
  174.1 24.3 %collective-permute-start.37 = (bf16[2,256,512]{2,1,0:T(8,128)(2,1)}, bf16[2,256,512]{2,1,0:T(8,128)(2,1)S(1)}, u32[]{:S(2)}, u32[]{:S(2)}) collective-permute-start(bf16[2,256,512]{2,1,0:T(8,128)(2,1)} %get-tuple-element.312), channel_id=1, source_target_pairs={{0,24},{4,28},{8,16},{12,20},{16,8},{20,12},{24,0},{28,4},{1,25},{... | collective-permute-start | bytes 1572872 | tf_op jit(solution)/shard_map/ppermute | solution.py:857
  198.3 30.7 %collective-permute-start.38 = (bf16[2,256,512]{2,1,0:T(8,128)(2,1)}, bf16[2,256,512]{2,1,0:T(8,128)(2,1)}, u32[]{:S(2)}, u32[]{:S(2)}) collective-permute-start(bf16[2,256,512]{2,1,0:T(8,128)(2,1)} %get-tuple-element.327), channel_id=1, source_target_pairs={{0,8},{4,12},{8,0},{12,4},{16,24},{20,28},{24,16},{28,20},{1,9},{5... | collective-permute-start | bytes 1572872 | tf_op jit(solution)/shard_map/ppermute | solution.py:857
  199.3 29.8 %collective-permute-start.39 = (bf16[2,256,512]{2,1,0:T(8,128)(2,1)}, bf16[2,256,512]{2,1,0:T(8,128)(2,1)}, u32[]{:S(2)}, u32[]{:S(2)}) collective-permute-start(bf16[2,256,512]{2,1,0:T(8,128)(2,1)} %get-tuple-element.328), channel_id=1, source_target_pairs={{0,16},{4,20},{8,24},{12,28},{16,0},{20,4},{24,8},{28,12},{1,17},{... | collective-permute-start | bytes 1572872 | tf_op jit(solution)/shard_map/ppermute | solution.py:857
  200.7 28.3 %collective-permute-start.40 = (bf16[2,256,512]{2,1,0:T(8,128)(2,1)}, bf16[2,256,512]{2,1,0:T(8,128)(2,1)}, u32[]{:S(2)}, u32[]{:S(2)}) collective-permute-start(bf16[2,256,512]{2,1,0:T(8,128)(2,1)} %get-tuple-element.329), channel_id=1, source_target_pairs={{0,24},{4,28},{8,16},{12,20},{16,8},{20,12},{24,0},{28,4},{1,25},{... | collective-permute-start | bytes 1572872 | tf_op jit(solution)/shard_map/ppermute | solution.py:857
  201.8 27.2 %collective-permute-start.41 = (bf16[2,256,512]{2,1,0:T(8,128)(2,1)}, bf16[2,256,512]{2,1,0:T(8,128)(2,1)S(1)}, u32[]{:S(2)}, u32[]{:S(2)}) collective-permute-start(bf16[2,256,512]{2,1,0:T(8,128)(2,1)} %get-tuple-element.331), channel_id=1, source_target_pairs={{0,3},{1,0},{2,1},{3,2},{4,7},{5,4},{6,5},{7,6},{8,11},{9,8},{10,9... | collective-permute-start | bytes 1572872 | tf_op jit(solution)/shard_map/ppermute | solution.py:860
  254.9 24.7 %collective-permute-start.56 = (bf16[2,256,512]{2,1,0:T(8,128)(2,1)}, bf16[2,256,512]{2,1,0:T(8,128)(2,1)S(1)}, u32[]{:S(2)}, u32[]{:S(2)}) collective-permute-start(bf16[2,256,512]{2,1,0:T(8,128)(2,1)} %blend.11.refs_0_), channel_id=1, source_target_pairs={{0,16},{4,20},{8,24},{12,28},{16,0},{20,4},{24,8},{28,12},{1,17},{... | collective-permute-start | bytes 1572872 | tf_op jit(solution)/shard_map/ppermute | solution.py:857
  255.5 24.1 %collective-permute-start.58 = (bf16[2,256,512]{2,1,0:T(8,128)(2,1)}, bf16[2,256,512]{2,1,0:T(8,128)(2,1)S(1)}, u32[]{:S(2)}, u32[]{:S(2)}) collective-permute-start(bf16[2,256,512]{2,1,0:T(8,128)(2,1)} %blend.11.refs_0_), channel_id=1, source_target_pairs={{0,24},{4,28},{8,16},{12,20},{16,8},{20,12},{24,0},{28,4},{1,25},{... | collective-permute-start | bytes 1572872 | tf_op jit(solution)/shard_map/ppermute | solution.py:857
  261.3 23.5 %collective-permute-start.53 = (bf16[2,256,512]{2,1,0:T(8,128)(2,1)}, bf16[2,256,512]{2,1,0:T(8,128)(2,1)}, u32[]{:S(2)}, u32[]{:S(2)}) collective-permute-start(bf16[2,256,512]{2,1,0:T(8,128)(2,1)} %blend.11.refs_0_), channel_id=1, source_target_pairs={{0,4},{4,0},{8,12},{12,8},{16,20},{20,16},{24,28},{28,24},{1,5},{5... | collective-permute-start | bytes 1572872 | tf_op jit(solution)/shard_map/ppermute | solution.py:857
  (67 other events, 699.7 us)

commit v6 on v5

--- a/solution.py
+++ b/solution.py
@@ -955,21 +955,23 @@
     pairs = [outs[k][2] for k in range(n_group)]
     biases = [outs[k][3] for k in range(n_group)]
     block_out, gres, gatt, late, shards[0], shards[1], *parts = combine_call(
-        (own_quarter(0), own_quarter(1), *quarters(3)), place, cotangent, att, res, tok, slots_row, full, small, pairs, biases
+        (own_quarter(0), own_quarter(1), *quarters(3), ("sum", [(outs[3][0], (0, 0)), (cores[3], (0, 0))])), place, cotangent, att, res, tok, slots_row, full, small, pairs, biases
     )
     gres, gatt, late, cores, chips, shards, parts = join(gres, gatt, late, cores, chips, shards, parts)
 
+    *parts, local_3 = parts
     chips[3] = send_chips(parts)
     shards[2], = blend_call(own_quarter(2))
     passed = along(rest_of_replicas(shards.pop(2)), 1)
     for k in range(2):
         shards[k] = send_shard(k, shards[k])
     input_grad, keep, send = backward_call(place, images, qkv, lse, gres, gatt, full, small, late, n_group)
-    keep, send, chips, shards, passed = join(keep, send, chips, shards, passed)
+    keep, send, chips, shards, passed, local_3 = join(keep, send, chips, shards, passed, local_3)
+    local_3 = [(local_3, ())] + [(v, ()) for v in chips[3]]
     if n_replica == PIECES:
-        value, = blend_call(("sum", own_quarter(3)[1] + [(passed, ())]))
+        value, = blend_call(("sum", local_3 + [(passed, ())]))
     else:
-        value = plus(rest_of_replicas(*blend_call(own_quarter(3))), passed)
+        value = plus(rest_of_replicas(*blend_call(("sum", local_3))), passed)
     shards[3] = along(value, 1)
 
     value = plus(keep, across(send, 1))

time: 301 us -> 301 us (level)
  no operation moved by 1% of the time
where the time goes in v6:
time: 301 us; the launch traced here: 297 us
  Pallas kernels  169 us (56%)
  starting transfers between devices  61.3 us (20%)
  waiting for transfers between devices  56.9 us (19%)
  other arithmetic  3.94 us (1%)
  local copies, waits for them, and re-layouts  3.34 us (1%)
    pallas_call x4, Pallas kernels, expert_call(): pl.pallas_call(functools.partial(expert_kernel, turn=turn, sources=source...  78.1 us
    ppermute x50, waiting for transfers between devices, across(): lax.ppermute(value, 'replica', [(i, i ^ bit) for i in range(n_replica)])  45.5 us
    ppermute x50, starting transfers between devices, across(): lax.ppermute(value, 'replica', [(i, i ^ bit) for i in range(n_replica)])  41.7 us
    pallas_call x1, Pallas kernels, backward_call(): pl.pallas_call(backward_kernel, out_shape=outs, grid_spec=pltpu.PrefetchS...  22.5 us
    pallas_call x1, Pallas kernels, combine_call(): pl.pallas_call(functools.partial(combine_kernel, turns=turns, jobs=plan,...  21 us
    pallas_call x6, Pallas kernels, blend_call(): pl.pallas_call(functools.partial(blend_kernel, jobs=plan, count_in=len(ar...  16.2 us
    pallas_call x1, Pallas kernels, forward_call(): pl.pallas_call(forward_kernel, out_shape=outs, grid_spec=pltpu.PrefetchSc...  16.1 us
    ppermute x9, starting transfers between devices, along(): lax.ppermute(value, 'group', [(i, (i + shift) % n_group) for i in range(n...  15.1 us
  transfers between devices with their start and end apart: 61, of which 18 were waited for; matrix products, arithmetic and copies ran while one was open for 1% of the time, Pallas kernels for 55%

profile of v6, /device:TPU:0, one launch (start us, length us, event | category | flops | bytes accessed | tf_op | source)
XLA Modules:
  0.0 296.6 jit_solution(5131815067584749484)
XLA Ops:
  4.0 3.1 %collective-permute-start = (bf16[16,2176]{1,0:T(8,128)(2,1)}, bf16[16,2176]{1,0:T(8,128)(2,1)S(1)}, u32[]{:S(2)}, u32[]{:S(2)}) collective-permute-start(bf16[16,2176]{1,0:T(8,128)(2,1)} %get-tuple-element.193), channel_id=1, source_target_pairs={{0,1},{1,2},{2,3},{3,0},{4,5},{5,6},{6,7},{7,4},{8,9},{9,10},{10,1... | collective-permute-start | bytes 208904 | tf_op jit(solution)/shard_map/ppermute | solution.py:860
  11.0 2.6 cut_own.1
  20.1 4.6 %collective-permute-done.3.refs_1_ = bf16[3,16,2176]{2,1,0:T(8,128)(2,1)S(1)} collective-permute-done((bf16[3,16,2176]{2,1,0:T(8,128)(2,1)S(1)}, bf16[3,16,2176]{2,1,0:T(8,128)(2,1)S(1)}, u32[]{:S(2)}, u32[]{:S(2)}) %collective-permute-start.3) | collective-permute-done | bytes 208928 | tf_op jit(solution)/shard_map/ppermute | solution.py:857
  24.7 4.2 %collective-permute-done.4.refs_2_ = bf16[3,16,2176]{2,1,0:T(8,128)(2,1)S(1)} collective-permute-done((bf16[3,16,2176]{2,1,0:T(8,128)(2,1)S(1)}, bf16[3,16,2176]{2,1,0:T(8,128)(2,1)S(1)}, u32[]{:S(2)}, u32[]{:S(2)}) %collective-permute-start.4) | collective-permute-done | bytes 208928 | tf_op jit(solution)/shard_map/ppermute | solution.py:857
  35.6 16.1 %attention_forward.1 = (bf16[5,208,1536]{2,1,0:T(8,128)(2,1)}, bf16[5,208,512]{2,1,0:T(8,128)(2,1)}, f32[5,208,512]{2,1,0:T(8,128)}, f32[5,208,128]{2,1,0:T(8,12...) custom-call(s32[4]{0:T(128)} %pad_add_fusion.place, ...), custom_call_target="tpu_custom_call" | custom-call | flops 13200000000 | bytes 12582912 | tf_op jit(solution)/shard_map/attention_forward/pallas_call | solution.py:242
  51.7 6.0 %collective-permute-done.13.refs_5_ = bf16[2,256,512]{2,1,0:T(8,128)(2,1)} collective-permute-done((bf16[2,256,512]{2,1,0:T(8,128)(2,1)S(1)}, bf16[2,256,512]{2,1,0:T(8,128)(2,1)}, u32[]{:S(2)}, u32[]{:S(2)}) %collective-permute-start.13) | collective-permute-done | bytes 524320 | tf_op jit(solution)/shard_map/ppermute | solution.py:857
  63.5 19.4 %expert.4 = (bf16[2,2,2,256,512]{4,3,2,1,0:T(8,128)(2,1)}, bf16[2,2,2,256,512]{4,3,2,1,0:T(8,128)(2,1)}, bf16[640,1024]{1,0:T(8,128)(2,1)}, f32[32,128]{1,0:T(8,128)}, bf16[4,2,256,512]{3,2,1,0:T(8,128)(2,1)}) custom-call(s32[4]{0:T(128)} %pad_add_fusion.place, s32[5,8,256]{2,1,0:T(8,128)} %pad.8.slots, f32[5,8,256]{2,1,0:T(8,128)} %get-tuple-element.206.gates, ...), custom_call_target="tpu_custom_call" | custom-call | flops 19800000512 | bytes 14680064 | tf_op jit(solution)/shard_map/expert/pallas_call | solution.py:476
  87.8 19.9 %expert.5 = (bf16[2,2,2,256,512]{4,3,2,1,0:T(8,128)(2,1)}, bf16[2,2,2,256,512]{4,3,2,1,0:T(8,128)(2,1)}, bf16[640,1024]{1,0:T(8,128)(2,1)}, f32[32,128]{1,0:T(8,128)}, bf16[4,2,256,512]{3,2,1,0:T(8,128)(2,1)}) custom-call(s32[4]{0:T(128)} %pad_add_fusion.place, s32[5,8,256]{2,1,0:T(8,128)} %pad.8.slots, f32[5,8,256]{2,1,0:T(8,128)} %get-tuple-element.206.gates, ...), custom_call_target="tpu_custom_call" | custom-call | flops 19800000512 | bytes 14680064 | tf_op jit(solution)/shard_map/expert/pallas_call | solution.py:476
  110.2 2.8 blend.6
  116.5 19.5 %expert.6 = (bf16[2,2,2,256,512]{4,3,2,1,0:T(8,128)(2,1)}, bf16[2,2,2,256,512]{4,3,2,1,0:T(8,128)(2,1)}, bf16[640,1024]{1,0:T(8,128)(2,1)}, f32[32,128]{1,0:T(8,128)}, bf16[4,2,256,512]{3,2,1,0:T(8,128)(2,1)}) custom-call(s32[4]{0:T(128)} %pad_add_fusion.place, s32[5,8,256]{2,1,0:T(8,128)} %pad.8.slots, f32[5,8,256]{2,1,0:T(8,128)} %get-tuple-element.206.gates, ...), custom_call_target="tpu_custom_call" | custom-call | flops 19800000512 | bytes 14680064 | tf_op jit(solution)/shard_map/expert/pallas_call | solution.py:476
  139.8 2.8 blend.7
  146.2 19.2 %expert.7 = (bf16[2,2,2,256,512]{4,3,2,1,0:T(8,128)(2,1)}, bf16[2,2,2,256,512]{4,3,2,1,0:T(8,128)(2,1)}, bf16[640,1024]{1,0:T(8,128)(2,1)}, f32[32,128]{1,0:T(8,128)}) custom-call(s32[4]{0:T(128)} %pad_add_fusion.place, s32[5,8,256]{2,1,0:T(8,128)} %pad.8.slots, f32[5,8,256]{2,1,0:T(8,128)} %get-tuple-element.206.gates, ...), custom_call_target="tpu_custom_call" | custom-call | flops 19800000512 | bytes 14680064 | tf_op jit(solution)/shard_map/expert/pallas_call | solution.py:476
  165.4 3.3 %collective-permute-done.32.refs_23_ = bf16[2,256,512]{2,1,0:T(8,128)(2,1)S(1)} collective-permute-done((bf16[2,256,512]{2,1,0:T(8,128)(2,1)}, bf16[2,256,512]{2,1,0:T(8,128)(2,1)S(1)}, u32[]{:S(2)}, u32[]{:S(2)}) %collective-permute-start.32) | collective-permute-done | bytes 524320 | tf_op jit(solution)/shard_map/ppermute | solution.py:857
  168.8 3.1 %blend.8 = (bf16[2,256,512]{2,1,0:T(8,128)(2,1)}, bf16[2,256,512]{2,1,0:T(8,128)(2,1)}, bf16[2,256,512]{2,1,0:T(8,128)(2,1)}) custom-call(bf16[2,2,2,256,512]{4,3,2,1,0:T(8,128)(2,1)} %get-tuple-element.311.refs_0_, bf16[2,2,2,256,512]{4,3,2,1,0:T(8,128)(2,1)} %collective-permute-done.30.refs_1_), custom_call_target="tpu_custom_call" | custom-call | flops 3300000000 | bytes 3145728 | tf_op jit(solution)/shard_map/blend/pallas_call | solution.py:345
  175.5 21.0 %combine.1 = (bf16[5,197,512]{2,1,0:T(8,128)(2,1)}, f32[5,208,512]{2,1,0:T(8,128)}, bf16[5,208,512]{2,1,0:T(8,128)(2,1)}, bf16[512,640]{1,0:T(8,128)(2,1)}, bf16...) custom-call(s32[4]{0:T(128)} %pad_add_fusion.place, ...), custom_call_target="tpu_custom_call" | custom-call | flops 19800000512 | bytes 14680064 | tf_op jit(solution)/shard_map/combine/pallas_call | solution.py:620
  203.6 2.6 blend.9
  206.6 22.5 %attention_backward.1 = (f32[5,197,512]{2,1,0:T(8,128)}, bf16[4,4,16,2176]{3,2,1,0:T(8,128)(2,1)}, bf16[4,4,16,2176]{3,2,1,0:T(8,128)(2,1)}) custom-call(s32[4]{0:T(128)} %pad_add_fusion.place, bf16[5,197,512]{2,1,0:T(8,128)(2,1)} %images.1, bf16[5,208,1536]{2,1,0:T(8,128)(2,1)} %get-tuple-element.305.qkv, f32[5,208,128]{2,1,0:T(8,128)} %get-tuple-element.306.lse, ...), custom_call_target="tpu_custom_call" | custom-call | flops 24199999488 | bytes 14680064 | tf_op jit(solution)/shard_map/attention_backward/pallas_call | solution.py:726
  229.9 2.6 blend.10
  239.2 9.5 %collective-permute-done.47.refs_2_ = bf16[2,256,512]{2,1,0:T(8,128)(2,1)} collective-permute-done((bf16[2,256,512]{2,1,0:T(8,128)(2,1)}, bf16[2,256,512]{2,1,0:T(8,128)(2,1)}, u32[]{:S(2)}, u32[]{:S(2)}) %collective-permute-start.47) | collective-permute-done | bytes 524320 | tf_op jit(solution)/shard_map/ppermute | solution.py:860
  257.7 3.4 %collective-permute-start.49 = (bf16[16,2176]{1,0:T(8,128)(2,1)S(1)}, bf16[16,2176]{1,0:T(8,128)(2,1)S(1)}, u32[]{:S(2)}, u32[]{:S(2)}) collective-permute-start(bf16[16,2176]{1,0:T(8,128)(2,1)S(1)} %slice_bitcast_fusion.6), channel_id=1, source_target_pairs={{0,2},{1,3},{2,0},{3,1},{4,6},{5,7},{6,4},{7,5},{8,10},{9,11},{10,... | collective-permute-start | bytes 208904 | tf_op jit(solution)/shard_map/ppermute | solution.py:863
  261.1 7.3 %collective-permute-done.54.refs_1_ = bf16[2,256,512]{2,1,0:T(8,128)(2,1)S(1)} collective-permute-done((bf16[2,256,512]{2,1,0:T(8,128)(2,1)}, bf16[2,256,512]{2,1,0:T(8,128)(2,1)S(1)}, u32[]{:S(2)}, u32[]{:S(2)}) %collective-permute-start.54) | collective-permute-done | bytes 524320 | tf_op jit(solution)/shard_map/ppermute | solution.py:857
  268.4 11.0 %collective-permute-done.56.refs_2_ = bf16[2,256,512]{2,1,0:T(8,128)(2,1)S(1)} collective-permute-done((bf16[2,256,512]{2,1,0:T(8,128)(2,1)}, bf16[2,256,512]{2,1,0:T(8,128)(2,1)S(1)}, u32[]{:S(2)}, u32[]{:S(2)}) %collective-permute-start.56) | collective-permute-done | bytes 524320 | tf_op jit(solution)/shard_map/ppermute | solution.py:857
  280.6 3.9 %finish_experts.2 = (f32[1,512,2048]{2,1,0:T(8,128)}, f32[1,2048,512]{2,1,0:T(8,128)}) custom-call(s32[4]{0:T(128)} %pad_add_fusion.place, bf16[2,256,512]{2,1,0:T(8,128)(2,1)} %blend.11.refs_0_, bf16[2,256,512]{2,1,0:T(8,128)(2,1)} %copy-done.22, bf16[2,256,512]{2,1,0:T(8,128)(2,1)} %copy-done.19, bf16[2,256,512]{2,1,0:T(8,128)(2,1)} %copy-done.20), custom_call_target="tpu_custom_call" | custom-call | flops 4400000000 | bytes 6291456 | tf_op jit(solution)/shard_map/finish_experts/pallas_call | solution.py:774
  287.6 3.9 %finish_experts.3 = (f32[1,512,2048]{2,1,0:T(8,128)}, f32[1,2048,512]{2,1,0:T(8,128)}) custom-call(s32[4]{0:T(128)} %pad_add_fusion.place, bf16[2,256,512]{2,1,0:T(8,128)(2,1)} %collective-permute-done.53.refs_0_, bf16[2,256,512]{2,1,0:T(8,128)(2,1)} %collective-permute-done.55.refs_1_, ...), custom_call_target="tpu_custom_call", output_to_operand_aliasing={{0}: (5, {}), {1}: (6, {})} | custom-call | flops 4400000000 | bytes 6291456 | tf_op jit(solution)/shard_map/finish_experts/pallas_call | solution.py:774
  (191 shorter events, 79.7 us)
Async XLA Ops:
  31.2 26.5 %collective-permute-start.14 = (bf16[2,256,512]{2,1,0:T(8,128)(2,1)S(1)}, bf16[2,256,512]{2,1,0:T(8,128)(2,1)S(1)}, u32[]{:S(2)}, u32[]{:S(2)}) collective-permute-start(bf16[2,256,512]{2,1,0:T(8,128)(2,1)S(1)} %copy-done.4), channel_id=1, source_target_pairs={{0,2},{1,3},{2,0},{3,1},{4,6},{5,7},{6,4},{7,5},{8,10},{9,11},{10,... | collective-permute-start | bytes 1572872 | tf_op jit(solution)/shard_map/ppermute | solution.py:860
  33.8 23.9 %collective-permute-start.13 = (bf16[2,256,512]{2,1,0:T(8,128)(2,1)S(1)}, bf16[2,256,512]{2,1,0:T(8,128)(2,1)}, u32[]{:S(2)}, u32[]{:S(2)}) collective-permute-start(bf16[2,256,512]{2,1,0:T(8,128)(2,1)S(1)} %collective-permute-done.10.refs_2_), channel_id=1, source_target_pairs={{0,24},{4,28},{8,16},{12,20},{16,8},{20,12},{24,0},{28,4},{1,25},{... | collective-permute-start | bytes 1572872 | tf_op jit(solution)/shard_map/ppermute | solution.py:857
  57.7 25.3 %collective-permute-start.15 = (bf16[2,256,512]{2,1,0:T(8,128)(2,1)S(1)}, bf16[2,256,512]{2,1,0:T(8,128)(2,1)}, u32[]{:S(2)}, u32[]{:S(2)}) collective-permute-start(bf16[2,256,512]{2,1,0:T(8,128)(2,1)S(1)} %collective-permute-done.14.refs_2_), channel_id=1, source_target_pairs={{0,8},{4,12},{8,0},{12,4},{16,24},{20,28},{24,16},{28,20},{1,9},{5... | collective-permute-start | bytes 1572872 | tf_op jit(solution)/shard_map/ppermute | solution.py:857
  58.8 24.2 %collective-permute-start.16 = (bf16[2,256,512]{2,1,0:T(8,128)(2,1)S(1)}, bf16[2,256,512]{2,1,0:T(8,128)(2,1)}, u32[]{:S(2)}, u32[]{:S(2)}) collective-permute-start(bf16[2,256,512]{2,1,0:T(8,128)(2,1)S(1)} %collective-permute-done.14.refs_2_), channel_id=1, source_target_pairs={{0,16},{4,20},{8,24},{12,28},{16,0},{20,4},{24,8},{28,12},{1,17},{... | collective-permute-start | bytes 1572872 | tf_op jit(solution)/shard_map/ppermute | solution.py:857
  83.3 26.3 %collective-permute-start.20 = (bf16[2,2,2,256,512]{4,3,2,1,0:T(8,128)(2,1)}, bf16[2,2,2,256,512]{4,3,2,1,0:T(8,128)(2,1)}, u32[]{:S(2)}, u32[]{:S(2)}) collective-permute-start(bf16[2,2,2,256,512]{4,3,2,1,0:T(8,128)(2,1)} %get-tuple-element.221), channel_id=1, source_target_pairs={{0,4},{4,0},{8,12},{12,8},{16,20},{20,16},{24,28},{28,24},{1,5},{5... | collective-permute-start | bytes 6291464 | tf_op jit(solution)/shard_map/ppermute | solution.py:857
  83.8 23.9 %collective-permute-start.21 = (bf16[2,256,512]{2,1,0:T(8,128)(2,1)S(1)}, bf16[2,256,512]{2,1,0:T(8,128)(2,1)S(1)}, u32[]{:S(2)}, u32[]{:S(2)}) collective-permute-start(bf16[2,256,512]{2,1,0:T(8,128)(2,1)S(1)} %collective-permute-done.18.refs_2_), channel_id=1, source_target_pairs={{0,8},{4,12},{8,0},{12,4},{16,24},{20,28},{24,16},{28,20},{1,9},{5... | collective-permute-start | bytes 1572872 | tf_op jit(solution)/shard_map/ppermute | solution.py:857
  84.7 24.9 %collective-permute-start.22 = (bf16[2,256,512]{2,1,0:T(8,128)(2,1)S(1)}, bf16[2,256,512]{2,1,0:T(8,128)(2,1)S(1)}, u32[]{:S(2)}, u32[]{:S(2)}) collective-permute-start(bf16[2,256,512]{2,1,0:T(8,128)(2,1)S(1)} %collective-permute-done.18.refs_2_), channel_id=1, source_target_pairs={{0,16},{4,20},{8,24},{12,28},{16,0},{20,4},{24,8},{28,12},{1,17},{... | collective-permute-start | bytes 1572872 | tf_op jit(solution)/shard_map/ppermute | solution.py:857
  86.1 23.5 %collective-permute-start.23 = (bf16[2,256,512]{2,1,0:T(8,128)(2,1)S(1)}, bf16[2,256,512]{2,1,0:T(8,128)(2,1)}, u32[]{:S(2)}, u32[]{:S(2)}) collective-permute-start(bf16[2,256,512]{2,1,0:T(8,128)(2,1)S(1)} %collective-permute-done.18.refs_2_), channel_id=1, source_target_pairs={{0,24},{4,28},{8,16},{12,20},{16,8},{20,12},{24,0},{28,4},{1,25},{... | collective-permute-start | bytes 1572872 | tf_op jit(solution)/shard_map/ppermute | solution.py:857
  109.7 29.6 %collective-permute-start.25 = (bf16[2,2,2,256,512]{4,3,2,1,0:T(8,128)(2,1)}, bf16[2,2,2,256,512]{4,3,2,1,0:T(8,128)(2,1)}, u32[]{:S(2)}, u32[]{:S(2)}) collective-permute-start(bf16[2,2,2,256,512]{4,3,2,1,0:T(8,128)(2,1)} %get-tuple-element.240), channel_id=1, source_target_pairs={{0,4},{4,0},{8,12},{12,8},{16,20},{20,16},{24,28},{28,24},{1,5},{5... | collective-permute-start | bytes 6291464 | tf_op jit(solution)/shard_map/ppermute | solution.py:857
  114.2 23.6 %collective-permute-start.27 = (bf16[2,256,512]{2,1,0:T(8,128)(2,1)}, bf16[2,256,512]{2,1,0:T(8,128)(2,1)S(1)}, u32[]{:S(2)}, u32[]{:S(2)}) collective-permute-start(bf16[2,256,512]{2,1,0:T(8,128)(2,1)} %get-tuple-element.256), channel_id=1, source_target_pairs={{0,16},{4,20},{8,24},{12,28},{16,0},{20,4},{24,8},{28,12},{1,17},{... | collective-permute-start | bytes 1572872 | tf_op jit(solution)/shard_map/ppermute | solution.py:857
  115.1 24.1 %collective-permute-start.28 = (bf16[2,256,512]{2,1,0:T(8,128)(2,1)}, bf16[2,256,512]{2,1,0:T(8,128)(2,1)S(1)}, u32[]{:S(2)}, u32[]{:S(2)}) collective-permute-start(bf16[2,256,512]{2,1,0:T(8,128)(2,1)} %get-tuple-element.257), channel_id=1, source_target_pairs={{0,24},{4,28},{8,16},{12,20},{16,8},{20,12},{24,0},{28,4},{1,25},{... | collective-permute-start | bytes 1572872 | tf_op jit(solution)/shard_map/ppermute | solution.py:857
  139.3 29.5 %collective-permute-start.30 = (bf16[2,2,2,256,512]{4,3,2,1,0:T(8,128)(2,1)}, bf16[2,2,2,256,512]{4,3,2,1,0:T(8,128)(2,1)}, u32[]{:S(2)}, u32[]{:S(2)}) collective-permute-start(bf16[2,2,2,256,512]{4,3,2,1,0:T(8,128)(2,1)} %get-tuple-element.268), channel_id=1, source_target_pairs={{0,4},{4,0},{8,12},{12,8},{16,20},{20,16},{24,28},{28,24},{1,5},{5... | collective-permute-start | bytes 6291464 | tf_op jit(solution)/shard_map/ppermute | solution.py:857
  143.6 25.1 %collective-permute-start.32 = (bf16[2,256,512]{2,1,0:T(8,128)(2,1)}, bf16[2,256,512]{2,1,0:T(8,128)(2,1)S(1)}, u32[]{:S(2)}, u32[]{:S(2)}) collective-permute-start(bf16[2,256,512]{2,1,0:T(8,128)(2,1)} %get-tuple-element.282), channel_id=1, source_target_pairs={{0,16},{4,20},{8,24},{12,28},{16,0},{20,4},{24,8},{28,12},{1,17},{... | collective-permute-start | bytes 1572872 | tf_op jit(solution)/shard_map/ppermute | solution.py:857
  145.1 23.7 %collective-permute-start.33 = (bf16[2,256,512]{2,1,0:T(8,128)(2,1)}, bf16[2,256,512]{2,1,0:T(8,128)(2,1)S(1)}, u32[]{:S(2)}, u32[]{:S(2)}) collective-permute-start(bf16[2,256,512]{2,1,0:T(8,128)(2,1)} %get-tuple-element.283), channel_id=1, source_target_pairs={{0,24},{4,28},{8,16},{12,20},{16,8},{20,12},{24,0},{28,4},{1,25},{... | collective-permute-start | bytes 1572872 | tf_op jit(solution)/shard_map/ppermute | solution.py:857
  172.0 24.6 %collective-permute-start.35 = (bf16[2,256,512]{2,1,0:T(8,128)(2,1)}, bf16[2,256,512]{2,1,0:T(8,128)(2,1)S(1)}, u32[]{:S(2)}, u32[]{:S(2)}) collective-permute-start(bf16[2,256,512]{2,1,0:T(8,128)(2,1)} %get-tuple-element.312), channel_id=1, source_target_pairs={{0,8},{4,12},{8,0},{12,4},{16,24},{20,28},{24,16},{28,20},{1,9},{5... | collective-permute-start | bytes 1572872 | tf_op jit(solution)/shard_map/ppermute | solution.py:857
  173.0 24.0 %collective-permute-start.36 = (bf16[2,256,512]{2,1,0:T(8,128)(2,1)}, bf16[2,256,512]{2,1,0:T(8,128)(2,1)S(1)}, u32[]{:S(2)}, u32[]{:S(2)}) collective-permute-start(bf16[2,256,512]{2,1,0:T(8,128)(2,1)} %get-tuple-element.313), channel_id=1, source_target_pairs={{0,16},{4,20},{8,24},{12,28},{16,0},{20,4},{24,8},{28,12},{1,17},{... | collective-permute-start | bytes 1572872 | tf_op jit(solution)/shard_map/ppermute | solution.py:857
  174.1 24.3 %collective-permute-start.37 = (bf16[2,256,512]{2,1,0:T(8,128)(2,1)}, bf16[2,256,512]{2,1,0:T(8,128)(2,1)S(1)}, u32[]{:S(2)}, u32[]{:S(2)}) collective-permute-start(bf16[2,256,512]{2,1,0:T(8,128)(2,1)} %get-tuple-element.314), channel_id=1, source_target_pairs={{0,24},{4,28},{8,16},{12,20},{16,8},{20,12},{24,0},{28,4},{1,25},{... | collective-permute-start | bytes 1572872 | tf_op jit(solution)/shard_map/ppermute | solution.py:857
  198.3 30.7 %collective-permute-start.38 = (bf16[2,256,512]{2,1,0:T(8,128)(2,1)}, bf16[2,256,512]{2,1,0:T(8,128)(2,1)}, u32[]{:S(2)}, u32[]{:S(2)}) collective-permute-start(bf16[2,256,512]{2,1,0:T(8,128)(2,1)} %get-tuple-element.330), channel_id=1, source_target_pairs={{0,8},{4,12},{8,0},{12,4},{16,24},{20,28},{24,16},{28,20},{1,9},{5... | collective-permute-start | bytes 1572872 | tf_op jit(solution)/shard_map/ppermute | solution.py:857
  199.3 29.7 %collective-permute-start.39 = (bf16[2,256,512]{2,1,0:T(8,128)(2,1)}, bf16[2,256,512]{2,1,0:T(8,128)(2,1)}, u32[]{:S(2)}, u32[]{:S(2)}) collective-permute-start(bf16[2,256,512]{2,1,0:T(8,128)(2,1)} %get-tuple-element.331), channel_id=1, source_target_pairs={{0,16},{4,20},{8,24},{12,28},{16,0},{20,4},{24,8},{28,12},{1,17},{... | collective-permute-start | bytes 1572872 | tf_op jit(solution)/shard_map/ppermute | solution.py:857
  200.7 28.3 %collective-permute-start.40 = (bf16[2,256,512]{2,1,0:T(8,128)(2,1)}, bf16[2,256,512]{2,1,0:T(8,128)(2,1)}, u32[]{:S(2)}, u32[]{:S(2)}) collective-permute-start(bf16[2,256,512]{2,1,0:T(8,128)(2,1)} %get-tuple-element.332), channel_id=1, source_target_pairs={{0,24},{4,28},{8,16},{12,20},{16,8},{20,12},{24,0},{28,4},{1,25},{... | collective-permute-start | bytes 1572872 | tf_op jit(solution)/shard_map/ppermute | solution.py:857
  201.8 27.2 %collective-permute-start.41 = (bf16[2,256,512]{2,1,0:T(8,128)(2,1)}, bf16[2,256,512]{2,1,0:T(8,128)(2,1)S(1)}, u32[]{:S(2)}, u32[]{:S(2)}) collective-permute-start(bf16[2,256,512]{2,1,0:T(8,128)(2,1)} %get-tuple-element.334), channel_id=1, source_target_pairs={{0,3},{1,0},{2,1},{3,2},{4,7},{5,4},{6,5},{7,6},{8,11},{9,8},{10,9... | collective-permute-start | bytes 1572872 | tf_op jit(solution)/shard_map/ppermute | solution.py:860
  254.7 24.7 %collective-permute-start.56 = (bf16[2,256,512]{2,1,0:T(8,128)(2,1)}, bf16[2,256,512]{2,1,0:T(8,128)(2,1)S(1)}, u32[]{:S(2)}, u32[]{:S(2)}) collective-permute-start(bf16[2,256,512]{2,1,0:T(8,128)(2,1)} %blend.11.refs_0_), channel_id=1, source_target_pairs={{0,16},{4,20},{8,24},{12,28},{16,0},{20,4},{24,8},{28,12},{1,17},{... | collective-permute-start | bytes 1572872 | tf_op jit(solution)/shard_map/ppermute | solution.py:857
  255.3 24.1 %collective-permute-start.58 = (bf16[2,256,512]{2,1,0:T(8,128)(2,1)}, bf16[2,256,512]{2,1,0:T(8,128)(2,1)S(1)}, u32[]{:S(2)}, u32[]{:S(2)}) collective-permute-start(bf16[2,256,512]{2,1,0:T(8,128)(2,1)} %blend.11.refs_0_), channel_id=1, source_target_pairs={{0,24},{4,28},{8,16},{12,20},{16,8},{20,12},{24,0},{28,4},{1,25},{... | collective-permute-start | bytes 1572872 | tf_op jit(solution)/shard_map/ppermute | solution.py:857
  261.1 23.5 %collective-permute-start.53 = (bf16[2,256,512]{2,1,0:T(8,128)(2,1)}, bf16[2,256,512]{2,1,0:T(8,128)(2,1)}, u32[]{:S(2)}, u32[]{:S(2)}) collective-permute-start(bf16[2,256,512]{2,1,0:T(8,128)(2,1)} %blend.11.refs_0_), channel_id=1, source_target_pairs={{0,4},{4,0},{8,12},{12,8},{16,20},{20,16},{24,28},{28,24},{1,5},{5... | collective-permute-start | bytes 1572872 | tf_op jit(solution)/shard_map/ppermute | solution.py:857
  (67 other events, 699.3 us)
